TPU v7x, 32 devices: a whole 2x2x4 slice. The times are simulated.
32 devices in a mesh: major: 4 (over y, x), minor: 8 (over z, core).
Axes of the slice: x: 2, y: 2, z: 4, core: 2. Of those that a mesh axis runs over, the one named last changes fastest.
Arguments:
- block_in: bfloat16 [4096, 1024], P(('major', 'minor')), may hold values from -6 to 6
- out_cot: bfloat16 [4096, 1024], P(('major', 'minor')), may hold values from -6 to 6
- w_in: bfloat16 [1024, 3072], replicated, may hold values from -0.1875 to 0.1875
- w_out: bfloat16 [1024, 1024], replicated, may hold values from -0.1875 to 0.1875
- conv_one: bfloat16 [4096, 1024], P(('major', 'minor')), may hold values from -6 to 6
- conv_two: bfloat16 [4096, 1024], P(('major', 'minor')), may hold values from -6 to 6
- filter_one: bfloat16 [4096, 1024], P(('major', 'minor')), may hold values from -6 to 6
- filter_two: bfloat16 [4096, 1024], P(('major', 'minor')), may hold values from -6 to 6
Outputs:
- in_grad: bfloat16 [4096, 1024], P(('major', 'minor'))
- w_in_grad: float32 [1024, 3072], P(('major', 'minor'))
- w_out_grad: float32 [1024, 1024], P(('major', 'minor'))
- filter_one_grad: bfloat16 [4096, 1024], P(('major', 'minor'))
- filter_two_grad: bfloat16 [4096, 1024], P(('major', 'minor'))
All inputs are finite; a program needn't handle non-finite values.
Results may differ from a plain program's by a relative error of at most 0.014.
Values may be sent and summed in bfloat16 or wider, within the bound.
No kernel may reach another device: no remote copies, remote signals or barrier semaphores. Data moves between devices by JAX's collectives and lax.ppermute only.
A program may use at most 128 MiB of HBM per device.

v0:
```python
import math

import jax
import jax.numpy as jnp
from jax import lax
from jax.sharding import PartitionSpec as P

EXACT = lax.Precision.HIGHEST


def apply_table(matrix, data, form):
    return jnp.einsum(form, matrix, data, precision=EXACT)


def product(left, right):
    return (left.astype(jnp.float32) * right.astype(jnp.float32)).astype(jnp.bfloat16)


def conj_times(left_re, left_im, right_re, right_im):
    return (left_re * right_re + left_im * right_im, left_re * right_im - left_im * right_re)


def spectral_move(moving):
    moved = lax.all_to_all(moving, ("major", "minor"), split_axis=2, concat_axis=2, tiled=True)
    return moved


def build_tables(rows_dev):
    devices = lax.axis_size(("major", "minor"))
    index = lax.axis_index(("major", "minor"))
    per_group = rows_dev // devices
    seq_len = rows_dev * devices
    grid = jnp.arange(devices, dtype=jnp.int32)
    line = jnp.arange(rows_dev, dtype=jnp.int32)
    local_pos = index * per_group + jnp.arange(per_group, dtype=jnp.int32)
    grid_angle = (
        -2.0 * math.pi * (grid[:, None] * grid[None, :] % devices).astype(jnp.float32) / devices
    )
    line_angle = (
        -2.0 * math.pi * (line[:, None] * line[None, :] % rows_dev).astype(jnp.float32) / rows_dev
    )
    steps_held = rows_dev * grid[:, None] + local_pos[None, :]
    seq_angle = -math.pi * steps_held.astype(jnp.float32) / seq_len
    turn_angle = (
        -2.0
        * math.pi
        * (grid[:, None] * local_pos[None, :] % seq_len).astype(jnp.float32)
        / seq_len
    )
    back_angle = 2.0 * math.pi * (line * index % seq_len).astype(jnp.float32) / seq_len
    return {
        "grid_cos": jnp.cos(grid_angle),
        "grid_sin": jnp.sin(grid_angle),
        "line_cos": jnp.cos(line_angle),
        "line_sin": jnp.sin(line_angle),
        "seq_cos": jnp.cos(seq_angle),
        "seq_sin": jnp.sin(seq_angle),
        "turn_cos": jnp.cos(turn_angle),
        "turn_sin": jnp.sin(turn_angle),
        "back_cos": jnp.cos(back_angle),
        "back_sin": jnp.sin(back_angle),
    }


def forward_spectrum(fields, tables):
    count, rows_dev, width = fields.shape
    devices = tables["grid_cos"].shape[0]
    per_group = rows_dev // devices
    pieces = fields.reshape(count, devices, per_group, width)
    landed = lax.all_to_all(
        pieces, ("major", "minor"), split_axis=1, concat_axis=1, tiled=True
    ).astype(jnp.float32)
    twist_re = landed * tables["seq_cos"][None, :, :, None]
    twist_im = landed * tables["seq_sin"][None, :, :, None]
    form = "ka,fard->fkrd"
    grid_cos = tables["grid_cos"]
    grid_sin = tables["grid_sin"]
    even_re = apply_table(grid_cos, landed, form)
    even_im = apply_table(grid_sin, landed, form)
    odd_re = apply_table(grid_cos, twist_re, form) - apply_table(grid_sin, twist_im, form)
    odd_im = apply_table(grid_cos, twist_im, form) + apply_table(grid_sin, twist_re, form)
    part_re = jnp.stack([even_re, odd_re], axis=1)
    part_im = jnp.stack([even_im, odd_im], axis=1)
    turn_cos = tables["turn_cos"][None, None, :, :, None]
    turn_sin = tables["turn_sin"][None, None, :, :, None]
    moving = jnp.concatenate(
        [part_re * turn_cos - part_im * turn_sin, part_re * turn_sin + part_im * turn_cos], axis=1
    )
    arrived = spectral_move(moving).reshape(count, 4, rows_dev, width)
    line_re = arrived[:, :2]
    line_im = arrived[:, 2:]
    form_line = "kb,fcbd->fckd"
    line_cos = tables["line_cos"]
    line_sin = tables["line_sin"]
    out_re = apply_table(line_cos, line_re, form_line) - apply_table(line_sin, line_im, form_line)
    out_im = apply_table(line_cos, line_im, form_line) + apply_table(line_sin, line_re, form_line)
    return (out_re, out_im)


def inverse_field(spec_re, spec_im, factor, tables):
    count, _, rows_dev, width = spec_re.shape
    devices = tables["grid_cos"].shape[0]
    per_group = rows_dev // devices
    form_line = "bk,fckd->fcbd"
    line_cos = tables["line_cos"]
    line_sin = tables["line_sin"]
    back_re = apply_table(line_cos, spec_re, form_line) + apply_table(line_sin, spec_im, form_line)
    back_im = apply_table(line_cos, spec_im, form_line) - apply_table(line_sin, spec_re, form_line)
    turn_cos = tables["back_cos"][None, None, :, None]
    turn_sin = tables["back_sin"][None, None, :, None]
    moving = jnp.concatenate(
        [back_re * turn_cos - back_im * turn_sin, back_re * turn_sin + back_im * turn_cos], axis=1
    )
    moving = moving.reshape(count, 4, devices, per_group, width)
    moved = spectral_move(moving)
    head_re = moved[:, :2]
    head_im = moved[:, 2:]
    grid_cos = tables["grid_cos"]
    grid_sin = tables["grid_sin"]
    form_grid = "ak,fckrd->fcard"
    grid_re = apply_table(grid_cos, head_re, form_grid) + apply_table(grid_sin, head_im, form_grid)
    form_odd = "ak,fkrd->fard"
    odd_im = apply_table(grid_cos, head_im[:, 1], form_odd) - apply_table(
        grid_sin, head_re[:, 1], form_odd
    )
    seq_cos = tables["seq_cos"][None, :, :, None]
    seq_sin = tables["seq_sin"][None, :, :, None]
    total = ((grid_re[:, 0] + grid_re[:, 1] * seq_cos + odd_im * seq_sin) * factor).astype(
        jnp.bfloat16
    )
    returned = lax.all_to_all(total, ("major", "minor"), split_axis=1, concat_axis=2, tiled=True)
    return returned.reshape(count, rows_dev, width)


def shards(block_in, out_cot, w_in, w_out, conv_one, conv_two, filter_one, filter_two):
    rows_dev, width = block_in.shape
    devices = lax.axis_size(("major", "minor"))
    seq_len = rows_dev * devices
    scale = seq_len ** (-0.5)
    factor = scale / (2.0 * seq_len)
    tables = build_tables(rows_dev)
    contract_last = (((1,), (1,)), ((), ()))
    contract_first = (((0,), (0,)), ((), ()))
    proj = jnp.dot(block_in, w_in, preferred_element_type=jnp.float32).astype(jnp.bfloat16)
    value = proj[:, :width]
    gate_one = proj[:, width : 2 * width]
    gate_two = proj[:, 2 * width :]
    first_out = product(gate_one, conv_one)
    second_out = product(gate_two, conv_two)
    grad_second = lax.dot_general(
        out_cot, w_out, contract_last, preferred_element_type=jnp.float32
    ).astype(jnp.bfloat16)
    grad_conv_two = product(grad_second, gate_two)
    grad_gate_two = product(grad_second, conv_two)
    spec_re, spec_im = forward_spectrum(
        jnp.stack([value, first_out, filter_one, filter_two, grad_conv_two]), tables
    )
    pair_re, pair_im = conj_times(
        jnp.stack([spec_re[3], spec_re[1]]),
        jnp.stack([spec_im[3], spec_im[1]]),
        spec_re[4][None],
        spec_im[4][None],
    )
    first_back = inverse_field(pair_re, pair_im, factor, tables)
    grad_first = first_back[0]
    filter_two_grad = first_back[1]
    grad_conv_one = product(grad_first, gate_one)
    grad_gate_one = product(grad_first, conv_one)
    single_re, single_im = forward_spectrum(grad_conv_one[None], tables)
    pair_re, pair_im = conj_times(
        jnp.stack([spec_re[2], spec_re[0]]),
        jnp.stack([spec_im[2], spec_im[0]]),
        single_re,
        single_im,
    )
    second_back = inverse_field(pair_re, pair_im, factor, tables)
    grad_value = second_back[0]
    filter_one_grad = second_back[1]
    grad_proj = jnp.concatenate([grad_value, grad_gate_one, grad_gate_two], axis=1)
    in_grad = lax.dot_general(
        grad_proj, w_in, contract_last, preferred_element_type=jnp.float32
    ).astype(jnp.bfloat16)
    in_part = lax.dot_general(
        block_in, grad_proj, contract_first, preferred_element_type=jnp.float32
    )
    out_part = lax.dot_general(
        second_out, out_cot, contract_first, preferred_element_type=jnp.float32
    )
    summed = (
        lax.psum_scatter(
            jnp.concatenate([in_part, out_part], axis=1),
            ("major", "minor"),
            scatter_dimension=0,
            tiled=True,
        )
        * scale
    )
    return (
        in_grad,
        summed[:, : 3 * width],
        summed[:, 3 * width :],
        filter_one_grad,
        filter_two_grad,
    )


def solution(mesh):
    return jax.shard_map(
        shards,
        mesh=mesh,
        in_specs=(
            P(("major", "minor"), None),
            P(("major", "minor"), None),
            P(),
            P(),
            P(("major", "minor"), None),
            P(("major", "minor"), None),
            P(("major", "minor"), None),
            P(("major", "minor"), None),
        ),
        out_specs=(
            P(("major", "minor"), None),
            P(("major", "minor"), None),
            P(("major", "minor"), None),
            P(("major", "minor"), None),
            P(("major", "minor"), None),
        ),
        check_vma=False,
    )
```

profile of v0, /device:TPU:0, one launch (start us, length us, event | category | flops | bytes accessed | tf_op | source)
XLA Modules:
  0.0 1041.3 jit_solution(13866321607982394423)
XLA Ops:
  9.4 3.9 convolution_convert_fusion
  23.9 7.5 all-to-all-start
  31.5 32.9 %all-to-all-done = bf16[5,32,4,1024]{3,2,0,1:T(4,128)(2,1)S(1)} async-done(((bf16[5,32,4,1024]{3,2,0,1:T(4,128)(2,1)}), bf16[5,32,4,1024]{3,2,0,1:T(4,128)(2,1)S(1)}, u32[]{:S(2)}, u32[]{:S(2)}) %all-to-all-start) | async-done | bytes 1310752 | tf_op jit(solution)/shard_map/all_to_all | solution.py:70
  77.8 3.6 add_bitcast_fusion.1
  81.4 4.8 multiply_subtract_fusion
  86.2 10.3 pad_maximum_fusion.1
  96.5 14.7 %copy.119 = f32[5,4,32,4,1024]{4,3,0,1,2:T(4,128)} copy(f32[5,4,32,4,1024]{4,2,3,0,1:T(8,128)} %pad_maximum_fusion.1) | data formatting | bytes 20971520 | tf_op jit(solution)/shard_map/concatenate | solution.py:86
  111.1 4.2 all-to-all-start.1
  115.4 229.8 %all-to-all-done.1 = f32[5,4,32,4,1024]{4,3,0,1,2:T(4,128)} async-done(((f32[5,4,32,4,1024]{4,3,0,1,2:T(4,128)}), f32[5,4,32,4,1024]{4,3,0,1,2:T(4,128)}, u32[]{:S(2)}, u32[]{:S(2)}) %all-to-all-start.1) | async-done | bytes 10485792 | tf_op jit(solution)/shard_map/all_to_all | solution.py:24
  345.2 18.4 %copy.120 = f32[5,4,32,4,1024]{4,1,3,2,0:T(4,128)} copy(f32[5,4,32,4,1024]{4,3,0,1,2:T(4,128)} %all-to-all-done.1) | data formatting | bytes 20971520 | tf_op jit(solution)/shard_map/all_to_all | solution.py:24
  363.6 15.5 %fusion.326 = (f32[5,2,128,1024]{3,1,2,0:T(2,128)}, f32[5,2,128,1024]{3,1,2,0:T(2,128)}) fusion(f32[5,4,128,1024]{3,1,2,0:T(4,128)} %bitcast.284), kind=kLoop, calls=%fused_computation.377 | loop fusion | bytes 20971520 | tf_op jit(solution)/shard_map/slice | solution.py:90
  379.1 8.7 copy.182
  387.8 8.9 copy.183
  396.7 6.8 fusion.95
  403.6 4.5 fusion.97
  408.1 6.5 add_bitcast_fusion
  414.5 6.8 subtract_bitcast_fusion
  421.3 4.7 fusion.327
  439.0 5.2 reshape.336
  447.4 96.9 %all_to_all.48 = f32[2,4,32,4,1024]{4,3,1,0,2:T(4,128)S(1)} all-to-all(f32[2,4,32,4,1024]{4,3,1,0,2:T(4,128)S(1)} %copy.127), channel_id=1, replica_groups=mesh['major'=4,'minor'=8] {'major','minor'}, dimensions={2} | all-to-all | bytes 8388608 | tf_op jit(solution)/shard_map/all_to_all | solution.py:24
  551.5 3.5 add_bitcast_fusion.4
  557.7 18.4 %all_to_all.49 = bf16[2,32,4,1024]{3,2,0,1:T(4,128)(2,1)S(1)} all-to-all(bf16[2,32,4,1024]{3,2,0,1:T(4,128)(2,1)S(1)} %copy.133), channel_id=1, replica_groups=mesh['major'=4,'minor'=8] {'major','minor'}, dimensions={1} | all-to-all | bytes 1048576 | tf_op jit(solution)/shard_map/all_to_all | solution.py:131
  581.8 10.2 all-to-all-done.4
  598.8 52.3 %all_to_all.50 = f32[1,4,32,4,1024]{4,3,1,0,2:T(4,128)S(1)} all-to-all(f32[1,4,32,4,1024]{4,3,1,0,2:T(4,128)S(1)} %copy.142), channel_id=1, replica_groups=mesh['major'=4,'minor'=8] {'major','minor'}, dimensions={2} | all-to-all | bytes 4194304 | tf_op jit(solution)/shard_map/all_to_all | solution.py:24
  677.6 5.2 reshape.343
  686.0 97.0 %all_to_all.51 = f32[2,4,32,4,1024]{4,3,1,0,2:T(4,128)S(1)} all-to-all(f32[2,4,32,4,1024]{4,3,1,0,2:T(4,128)S(1)} %copy.150), channel_id=1, replica_groups=mesh['major'=4,'minor'=8] {'major','minor'}, dimensions={2} | all-to-all | bytes 8388608 | tf_op jit(solution)/shard_map/all_to_all | solution.py:24
  800.0 3.7 fusion.67
  803.7 12.6 %all-to-all-done.7 = bf16[2,32,4,1024]{3,2,0,1:T(4,128)(2,1)S(1)} async-done(((bf16[2,32,4,1024]{3,2,0,1:T(4,128)(2,1)}), bf16[2,32,4,1024]{3,2,0,1:T(4,128)(2,1)S(1)}, u32[]{:S(2)}, u32[]{:S(2)}) %all-to-all-start.7) | async-done | bytes 524320 | tf_op jit(solution)/shard_map/all_to_all | solution.py:131
  818.7 7.2 pad_maximum_fusion
  825.8 17.5 %copy.180 = f32[1024,4096]{1,0:T(8,128)} copy(f32[1024,4096]{0,1:T(8,128)} %pad_maximum_fusion) | data formatting | bytes 33554432
  845.8 6.1 convolution_convert_fusion.1
  851.9 175.8 %reduce-scatter.4.cloned.1.call-done = f32[32,4096]{1,0:T(8,128)} async-done(((f32[1024,4096]{1,0:T(8,128)}), f32[32,4096]{1,0:T(8,128)}) %reduce-scatter.4.cloned.1.call-update) | async-done | bytes 524304
  (128 shorter events, 122.4 us)
Async XLA Ops:
  7.2 8.7 copy-start
  13.3 5.4 copy-start.9
  23.9 40.5 %all-to-all-start = ((bf16[5,32,4,1024]{3,2,0,1:T(4,128)(2,1)}), bf16[5,32,4,1024]{3,2,0,1:T(4,128)(2,1)S(1)}, u32[]{:S(2)}, u32[]{:S(2)}) async-start(bf16[5,32,4,1024]{3,2,0,1:T(4,128)(2,1)} %copy.115), calls=%async_computation | async-start | bytes 2621440 | tf_op jit(solution)/shard_map/all_to_all | solution.py:70
  111.1 234.0 %all-to-all-start.1 = ((f32[5,4,32,4,1024]{4,3,0,1,2:T(4,128)}), f32[5,4,32,4,1024]{4,3,0,1,2:T(4,128)}, u32[]{:S(2)}, u32[]{:S(2)}) async-start(f32[5,4,32,4,1024]{4,3,0,1,2:T(4,128)} %copy.119), calls=%async_computation.1 | async-start | bytes 20971520 | tf_op jit(solution)/shard_map/all_to_all | solution.py:24
  387.8 15.7 %slice-start = ((s8[5242880]{0:T(1024)(128)(4,1)}), s8[1048576]{0:T(1024)(128)(4,1)S(1)}, s32[]{:S(2)}) async-start(s8[5242880]{0:T(1024)(128)(4,1)} %bitcast.280), calls=%async_computation.10 | async-start | bytes 2097152
  396.7 6.8 slice-start.1
  403.6 11.0 %slice-start.2 = ((s8[5242880]{0:T(1024)(128)(4,1)}), s8[4194304]{0:T(1024)(128)(4,1)S(1)}, s32[]{:S(2)}) async-start(s8[5242880]{0:T(1024)(128)(4,1)} %bitcast.282), calls=%async_computation.12 | async-start | bytes 8388608
  408.0 6.5 slice-start.3
  414.5 6.8 copy-start.5
  557.1 20.1 %copy-start.15 = (bf16[128,1024]{1,0:T(8,128)(2,1)S(1)}, bf16[128,1024]{1,0:T(8,128)(2,1)}, u32[]{:S(2)}) copy-start(bf16[128,1024]{1,0:T(8,128)(2,1)} %param.12) | copy-start | bytes 786436
  579.0 13.0 %all-to-all-start.4 = ((bf16[1,32,4,1024]{3,2,0,1:T(4,128)(2,1)}), bf16[1,32,4,1024]{3,2,0,1:T(4,128)(2,1)S(1)}, u32[]{:S(2)}, u32[]{:S(2)}) async-start(bf16[1,32,4,1024]{3,2,0,1:T(4,128)(2,1)} %bitcast.37), calls=%async_computation.4 | async-start | bytes 524288 | tf_op jit(solution)/shard_map/all_to_all | solution.py:70
  658.5 1.2 copy-start.7
  661.0 1.2 copy-start.8
  662.2 1.3 copy-start.2
  662.2 1.5 copy-start.3
  662.2 1.8 copy-start.4
  793.7 6.2 copy-start.13
  793.7 6.2 copy-start.14
  797.2 19.0 %all-to-all-start.7 = ((bf16[2,32,4,1024]{3,2,0,1:T(4,128)(2,1)}), bf16[2,32,4,1024]{3,2,0,1:T(4,128)(2,1)S(1)}, u32[]{:S(2)}, u32[]{:S(2)}) async-start(bf16[2,32,4,1024]{3,2,0,1:T(4,128)(2,1)} %copy.157), calls=%async_computation.7 | async-start | bytes 1048576 | tf_op jit(solution)/shard_map/all_to_all | solution.py:131
  799.9 16.6 %copy-start.10 = (bf16[128,1024]{1,0:T(8,128)(2,1)S(1)}, bf16[128,1024]{1,0:T(8,128)(2,1)}, u32[]{:S(2)}) copy-start(bf16[128,1024]{1,0:T(8,128)(2,1)} %param.8) | copy-start | bytes 786436
  799.9 16.6 %copy-start.11 = (bf16[128,1024]{1,0:T(8,128)(2,1)S(1)}, bf16[128,1024]{1,0:T(8,128)(2,1)}, u32[]{:S(2)}) copy-start(bf16[128,1024]{1,0:T(8,128)(2,1)} %get-tuple-element.63) | copy-start | bytes 786436
  799.9 227.8 %reduce-scatter.4.cloned.1.call-start = ((), (), s32[]{:S(2)}) async-start(), calls=%async_computation.9 | async-start | bytes 17301504
  816.5 2.2 copy-start.6
  843.3 0.9 copy-start.12
  1029.5 4.7 copy-start.1
Sparse Core Ops, SparseCore 0:
  843.4 184.1 reduce-scatter.3
where the time goes:
time: 1050 us; the launch traced here: 1040 us
  waiting for transfers between devices  461 us (44%)
  blocking collectives  265 us (25%)
  local copies, waits for them, and re-layouts  141 us (13%)
  matrix products  112 us (11%)
  other arithmetic  29.8 us (3%)
  starting transfers between devices  16.9 us (2%)
  between operations  15 us (1%)
    all_to_all x3, blocking collectives, spectral_move(): lax.all_to_all(moving, ('major', 'minor'), split_axis=2, concat_axis=2, t...  246 us
    all_to_all x1, waiting for transfers between devices, spectral_move(): lax.all_to_all(moving, ('major', 'minor'), split_axis=2, concat_axis=2, t...  230 us
    unnamed x2, waiting for transfers between devices  176 us
    dot_general x36, matrix products, apply_table(): return jnp.einsum(form, matrix, data, precision=EXACT)  94.1 us
    unnamed x52, local copies, waits for them, and re-layouts  46.9 us
    all_to_all x2, waiting for transfers between devices, forward_spectrum(): lax.all_to_all(pieces, ('major', 'minor'), split_axis=1, concat_axis=1, t...  43.1 us
  transfers between devices with their start and end apart: 5, of which 5 were waited for; matrix products, arithmetic and copies ran while one was open for 1% of the time, Pallas kernels for 0%

commit v1 on v0

v1 whole, which is shorter than its diff:
```python
import functools
import math

import jax
import jax.numpy as jnp
import numpy as np
from jax import lax
from jax.experimental import pallas as pl
from jax.experimental.pallas import tpu as pltpu
from jax.sharding import PartitionSpec as P

AXES = ("major", "minor")
LAST = (((1,), (1,)), ((), ()))


def product(left, right):
    return (left.astype(jnp.float32) * right.astype(jnp.float32)).astype(jnp.bfloat16)


def tables(devices, rows_dev):
    seq_len = devices * rows_dev
    line = np.arange(rows_dev)
    angle = -2.0 * math.pi * (line[:, None] * line[None, :] % rows_dev) / rows_dev
    cos, sin = np.cos(angle), np.sin(angle)
    forward = np.block([[cos, sin], [-sin, cos]])
    backward = np.block([[cos, -sin], [sin, cos]])
    turn = -2.0 * math.pi * (np.arange(devices)[:, None] + 0.25) * line[None, :] / seq_len
    turn_cos = np.repeat(np.cos(turn), 8, axis=0)
    turn_sin = np.repeat(np.sin(turn), 8, axis=0)
    return (
        jnp.asarray(forward, jnp.bfloat16),
        jnp.asarray(backward, jnp.bfloat16),
        jnp.asarray(turn_cos, jnp.float32),
        jnp.asarray(turn_sin, jnp.float32),
    )


def fft_real(xs):
    size = len(xs)
    if size == 1:
        return [(xs[0], None)]
    if size == 2:
        turned = xs[1] * math.cos(math.pi / 4)
        return [(xs[0] + turned, -turned), (xs[0] - turned, turned)]
    even, odd = fft_real(xs[0::2]), fft_real(xs[1::2])
    low, high = [], []
    for k in range(size // 2):
        angle = -2.0 * math.pi * (k + 0.25) / size
        cos, sin = math.cos(angle), math.sin(angle)
        (er, ei), (orr, oi) = even[k], odd[k]
        tr = orr * cos - oi * sin
        ti = orr * sin + oi * cos
        low.append((er + tr, ei + ti))
        high.append((er - tr, ei - ti))
    return low + high


def fft_back(pairs):
    size = len(pairs)
    if size == 2:
        (ar, ai), (br, bi) = pairs
        return [ar + br, ((ar - br) - (ai - bi)) * math.cos(math.pi / 4)]
    half = size // 2
    even, odd = [], []
    for k in range(half):
        angle = 2.0 * math.pi * (k + 0.25) / size
        cos, sin = math.cos(angle), math.sin(angle)
        (ar, ai), (br, bi) = pairs[k], pairs[k + half]
        even.append((ar + br, ai + bi))
        dr, di = ar - br, ai - bi
        odd.append((dr * cos - di * sin, dr * sin + di * cos))
    even, odd = fft_back(even), fft_back(odd)
    return [term for pair in zip(even, odd) for term in pair]


def long_kernel(
    devices, group, scale,
    grad_two, filter_two, gate_one, conv_one, filter_one, value, forward, backward, turn_cos, turn_sin,
    gate_grad, filter_two_grad, value_grad, filter_one_grad,
    held, grad_one, spec_a, spec_b, spec_c,
):
    rows = devices * group
    cols = held.shape[1]
    halves = group // 8

    def into(source, spec):
        if source is not held:
            held[...] = source[...].astype(jnp.float32)

        def step(j, carry):
            xs = [held[pl.ds(n * group + j * 8, 8), :] for n in range(devices)]
            for k, (re, im) in enumerate(fft_real(xs)):
                cos, sin = turn_cos[8 * k : 8 * k + 8, :], turn_sin[8 * k : 8 * k + 8, :]
                at = pl.ds(k * group + j * 8, 8)
                spec[at, :cols] = re * cos - im * sin
                spec[at, cols:] = re * sin + im * cos
            return carry

        lax.fori_loop(0, halves, step, 0)

    def outof(spec):
        def step(j, carry):
            pairs = []
            for k in range(devices):
                cos, sin = turn_cos[8 * k : 8 * k + 8, :], turn_sin[8 * k : 8 * k + 8, :]
                at = pl.ds(k * group + j * 8, 8)
                re, im = spec[at, :cols], spec[at, cols:]
                pairs.append((re * cos + im * sin, im * cos - re * sin))
            for n, term in enumerate(fft_back(pairs)):
                held[pl.ds(n * group + j * 8, 8), :] = term * scale
            return carry

        lax.fori_loop(0, halves, step, 0)

    def correlate():
        block = min(rows, 256)

        def step(i, carry):
            at = pl.ds(pl.multiple_of(i * block, block), block)

            def line(spec):
                moved = jnp.dot(spec[at, :].astype(jnp.bfloat16), forward[...], preferred_element_type=jnp.float32)
                return moved[:, :cols], moved[:, cols:]

            ar, ai = line(spec_a)
            for spec in (spec_b, spec_c):
                br, bi = line(spec)
                mixed = jnp.concatenate([ar * br + ai * bi, ai * br - ar * bi], axis=1).astype(jnp.bfloat16)
                spec[at, :] = jnp.dot(mixed, backward[...], preferred_element_type=jnp.float32)
            return carry

        lax.fori_loop(0, rows // block, step, 0)

    into(grad_two, spec_a)
    into(filter_two, spec_b)
    held[...] = product(gate_one[...], conv_one[...]).astype(jnp.float32)
    into(held, spec_c)
    correlate()
    outof(spec_c)
    filter_two_grad[...] = held[...].astype(jnp.bfloat16)
    outof(spec_b)
    grad_first = held[...].astype(jnp.bfloat16)
    gate_grad[...] = product(grad_first, conv_one[...])
    held[...] = product(grad_first, gate_one[...]).astype(jnp.float32)
    into(held, spec_a)
    into(filter_one, spec_b)
    into(value, spec_c)
    correlate()
    outof(spec_b)
    value_grad[...] = held[...].astype(jnp.bfloat16)
    outof(spec_c)
    filter_one_grad[...] = held[...].astype(jnp.bfloat16)


def long_convs(fields, devices, group, rows_dev):
    rows = devices * group
    seq_len = devices * rows_dev
    scale = seq_len ** (-0.5) / seq_len
    field = jax.ShapeDtypeStruct((rows, rows_dev), jnp.bfloat16)
    spec = pltpu.VMEM((rows, 2 * rows_dev), jnp.float32)
    return pl.pallas_call(
        functools.partial(long_kernel, devices, group, scale),
        out_shape=[field] * 4,
        in_specs=[pl.BlockSpec(memory_space=pltpu.VMEM)] * 10,
        out_specs=[pl.BlockSpec(memory_space=pltpu.VMEM)] * 4,
        scratch_shapes=[pltpu.VMEM((rows, rows_dev), jnp.float32), pltpu.VMEM((8, rows_dev), jnp.float32), spec, spec, spec],
        compiler_params=pltpu.CompilerParams(vmem_limit_bytes=40 * 2**20),
    )(*fields, *tables(devices, rows_dev))


def pair_gather(block, axis):
    count = lax.axis_size(axis)
    held, step = block[None], 1
    while step < count:
        other = lax.ppermute(held, axis, [(i, i ^ step) for i in range(count)])
        high = (lax.axis_index(axis) & step) != 0
        held = jnp.concatenate([jnp.where(high, other, held), jnp.where(high, held, other)])
        step *= 2
    return held


def shards(block_in, out_cot, w_in, w_out, conv_one, conv_two, filter_one, filter_two):
    rows_dev, width = block_in.shape
    devices, majors, minors = lax.axis_size(AXES), lax.axis_size("major"), lax.axis_size("minor")
    group = width // devices
    scale = (rows_dev * devices) ** (-0.5)
    all_in = lax.all_gather(block_in, AXES, axis=0, tiled=False)
    major_cot = pair_gather(out_cot, "major")
    first = (((0,), (1,)), ((), ()))
    proj = lax.dot_general(w_in, block_in, first, preferred_element_type=jnp.float32).astype(jnp.bfloat16)
    value, gate_one, gate_two = proj[:width], proj[width : 2 * width], proj[2 * width :]
    grad_second = lax.dot_general(w_out, out_cot, LAST, preferred_element_type=jnp.float32).astype(jnp.bfloat16)
    conv_two = conv_two.T
    second_out = product(gate_two, conv_two)
    grad_conv_two = product(grad_second, gate_two)
    grad_gate_two = product(grad_second, conv_two)
    moving = jnp.concatenate(
        [grad_conv_two, filter_two.T, gate_one, conv_one.T, filter_one.T, value, grad_gate_two]
    )
    moving = lax.optimization_barrier(moving).reshape(7, devices, group, rows_dev)
    here = lax.all_to_all(moving, AXES, split_axis=1, concat_axis=1, tiled=True)
    fields = [here[i].reshape(devices * group, rows_dev) for i in range(6)]
    major_out = lax.all_to_all(
        second_out.reshape(majors, width // majors, rows_dev), "major", split_axis=0, concat_axis=0, tiled=True
    )
    out_part = jnp.einsum("mct,mtw->cw", major_out, major_cot, preferred_element_type=jnp.float32)
    out_part = out_part.astype(jnp.bfloat16).reshape(minors, group, width)
    out_part = lax.all_to_all(out_part, "minor", split_axis=0, concat_axis=0, tiled=True)
    w_out_grad = out_part.astype(jnp.float32).sum(axis=0) * scale
    gate_grad, filter_two_grad, value_grad, filter_one_grad = long_convs(fields, devices, group, rows_dev)
    by_device = lambda x: x.reshape(devices, group, rows_dev)
    grads = jnp.stack([by_device(value_grad), by_device(gate_grad), here[6]])
    in_part = jnp.einsum("dtw,fdct->wfc", all_in, grads, preferred_element_type=jnp.float32) * scale
    in_part = in_part.astype(jnp.bfloat16).reshape(devices, group, 3 * group)
    in_part = lax.all_to_all(in_part, AXES, split_axis=0, concat_axis=0, tiled=True)
    w_in_grad = in_part.reshape(devices, group, 3, group).transpose(1, 2, 0, 3).reshape(group, 3 * width)
    back = jnp.concatenate([value_grad, gate_grad, filter_one_grad, filter_two_grad])
    back = lax.optimization_barrier(back).reshape(4, devices, group, rows_dev)
    back = lax.all_to_all(back, AXES, split_axis=1, concat_axis=1, tiled=True).reshape(4, width, rows_dev)
    grad_proj = jnp.concatenate([back[0], back[1], grad_gate_two], axis=0)
    in_grad = lax.dot_general(grad_proj, w_in, (((0,), (1,)), ((), ())), preferred_element_type=jnp.float32)
    return in_grad.astype(jnp.bfloat16), w_in_grad.astype(jnp.float32), w_out_grad, back[2].T, back[3].T


def solution(mesh):
    tokens = P(AXES, None)
    return jax.shard_map(
        shards,
        mesh=mesh,
        in_specs=(tokens, tokens, P(), P(), tokens, tokens, tokens, tokens),
        out_specs=(tokens,) * 5,
        check_vma=False,
    )
```

time: 1050 us -> 194 us (0.18)
  waiting for transfers between devices: 461 us -> 96.8 us
  blocking collectives: 265 us -> 0 us
  local copies, waits for them, and re-layouts: 141 us -> 23.8 us
  matrix products: 112 us -> 19.4 us
  other arithmetic: 29.8 us -> 3.38 us
    all_to_all x4 -> x0, blocking collectives: 265 us -> none  [the longest x3 246 us: spectral_move(): lax.all_to_all(moving, ('major', 'minor'), split_axis=2, concat_axis=2, t...]
    all_to_all x4 -> x5, waiting for transfers between devices: 285 us -> 55.4 us  [the longest x1 26.8 us: shards(): lax.all_to_all(back, AXES, split_axis=1, concat_axis=1, tiled=True)]
    unnamed x2 -> x1, waiting for transfers between devices: 176 us -> 0.68 us
    dot_general x41 -> x5, matrix products: 112 us -> 19.4 us  [the longest x1 5.9 us: shards(): lax.dot_general(grad_proj, w_in, (((0,), (1,)), ((), ())), preferred_elem...]
    ppermute x0 -> x2, waiting for transfers between devices: none -> 40.7 us  [pair_gather(): other = lax.ppermute(held, axis, [(i, i ^ step) for i in range(count)])]
    unnamed x52 -> x32, local copies, waits for them, and re-layouts: 46.9 us -> 8.73 us
    slice x11 -> x1, local copies, waits for them, and re-layouts: 28.8 us -> 2.07 us  [shards(): back[3]]
    concatenate x5 -> x3, other arithmetic: 22.2 us -> 1.76 us  [the longest x1 0.88 us: pair_gather(): jnp.concatenate([jnp.where(high, other, held), jnp.where(high, held, othe...]
  transfers between devices with their start and end apart: 5 -> 8, of which waited for: 5 -> 6; matrix products, arithmetic and copies ran while one was open for 1% -> 16% of each run, Pallas kernels for 0% -> 5%
where the time goes in v1:
time: 194 us; the launch traced here: 193 us
  waiting for transfers between devices  96.8 us (50%)
  starting transfers between devices  25.1 us (13%)
  local copies, waits for them, and re-layouts  23.8 us (12%)
  matrix products  19.4 us (10%)
  between operations  14.3 us (7%)
  Pallas kernels  10 us (5%)
  other arithmetic  3.38 us (2%)
    ppermute x2, waiting for transfers between devices, pair_gather(): other = lax.ppermute(held, axis, [(i, i ^ step) for i in range(count)])  40.7 us
    all_to_all x1, waiting for transfers between devices, shards(): lax.all_to_all(back, AXES, split_axis=1, concat_axis=1, tiled=True)  26.8 us
    all_to_all x1, waiting for transfers between devices, shards(): here = lax.all_to_all(moving, AXES, split_axis=1, concat_axis=1, tiled=True)  19.8 us
    pallas_call x1, Pallas kernels, long_convs(): pl.pallas_call(functools.partial(long_kernel, devices, group, scale), out...  10 us
    unnamed x32, local copies, waits for them, and re-layouts  8.73 us
    convert_element_type x3, local copies, waits for them, and re-layouts, shards(): w_in_grad.astype(jnp.float32)  8.28 us
    all_to_all x1, starting transfers between devices, shards(): here = lax.all_to_all(moving, AXES, split_axis=1, concat_axis=1, tiled=True)  6.71 us
    dot_general x1, matrix products, shards(): lax.dot_general(grad_proj, w_in, (((0,), (1,)), ((), ())), preferred_elem...  5.9 us
  transfers between devices with their start and end apart: 8, of which 6 were waited for; matrix products, arithmetic and copies ran while one was open for 16% of the time, Pallas kernels for 5%

profile of v1, /device:TPU:0, one launch (start us, length us, event | category | flops | bytes accessed | tf_op | source)
XLA Modules:
  0.0 192.8 jit_solution(12283643459327238173)
XLA Ops:
  7.9 1.1 copy.59
  9.1 4.7 %convolution_convert_fusion = bf16[3072,128]{1,0:T(8,128)(2,1)S(1)} fusion(bf16[1024,3072]{1,0:T(8,128)(2,1)} %param.14, bf16[128,1024]{1,0:T(8,128)(2,1)} %param.12), kind=kOutput, calls=%fused_computation | convolution fusion | flops 805699584 | bytes 7340032 | tf_op jit(solution)/shard_map/dot_general | solution.py:190
  14.5 5.2 %all-to-all-start.3 = ((bf16[4,256,128]{2,1,0:T(8,128)(2,1)}), bf16[4,256,128]{2,1,0:T(8,128)(2,1)}, u32[]{:S(2)}, u32[]{:S(2)}) async-start(bf16[4,256,128]{2,1,0:T(8,128)(2,1)} %bitcast.22), calls=%async_computation.3 | async-start | bytes 524288 | tf_op jit(solution)/shard_map/all_to_all | solution.py:203
  20.5 1.8 copy.57
  22.4 1.1 copy.58
  23.5 1.7 fusion.21
  26.3 1.5 copy.60
  27.8 6.7 %all-to-all-start = ((bf16[7,32,32,128]{3,2,0,1:T(8,128)(2,1)}), bf16[7,32,32,128]{3,2,0,1:T(8,128)(2,1)}, u32[]{:S(2)}, u32[]{:S(2)}) async-start(bf16[7,32,32,128]{3,2,0,1:T(8,128)(2,1)} %copy.60), calls=%async_computation | async-start | bytes 3670016 | tf_op jit(solution)/shard_map/all_to_all | solution.py:201
  34.6 1.8 collective-permute-start
  36.3 27.0 %collective-permute-done = bf16[1,128,1024]{2,1,0:T(8,128)(2,1)S(1)} collective-permute-done((bf16[1,128,1024]{2,1,0:T(8,128)(2,1)S(1)}, bf16[1,128,1024]{2,1,0:T(8,128)(2,1)S(1)}, u32[]{:S(2)}, u32[]{:S(2)}) %collective-permute-start) | collective-permute-done | bytes 262176 | tf_op jit(solution)/shard_map/ppermute | solution.py:175
  63.4 0.9 pad_maximum_fusion.1
  64.3 1.5 collective-permute-start.1
  65.8 13.7 %collective-permute-done.1 = bf16[2,128,1024]{2,1,0:T(8,128)(2,1)S(1)} collective-permute-done((bf16[2,128,1024]{2,1,0:T(8,128)(2,1)}, bf16[2,128,1024]{2,1,0:T(8,128)(2,1)S(1)}, u32[]{:S(2)}, u32[]{:S(2)}) %collective-permute-start.1) | collective-permute-done | bytes 524320 | tf_op jit(solution)/shard_map/ppermute | solution.py:175
  79.5 2.2 %fusion = bf16[256,1024]{1,0:T(8,128)(2,1)} fusion(bf16[4,256,128]{2,1,0:T(8,128)(2,1)} %all-to-all-done.3, bf16[2,128,1024]{2,1,0:T(8,128)(2,1)S(1)} %get-tuple-element.47, bf16[2,128,1024]{2,1,0:T(8,128)(2,1)S(1)} %get-tuple-element.46), kind=kOutput, calls=%fused_computation.2 | convolution fusion | flops 269221888 | bytes 1835008 | tf_op jit(solution)/shard_map/mct,mtw->cw/dot_general | solution.py:206
  81.7 19.8 %all-to-all-done = bf16[7,32,32,128]{3,2,0,1:T(8,128)(2,1)} async-done(((bf16[7,32,32,128]{3,2,0,1:T(8,128)(2,1)}), bf16[7,32,32,128]{3,2,0,1:T(8,128)(2,1)}, u32[]{:S(2)}, u32[]{:S(2)}) %all-to-all-start) | async-done | bytes 1835040 | tf_op jit(solution)/shard_map/all_to_all | solution.py:201
  101.5 3.5 %all-to-all-start.4 = ((bf16[8,32,1024]{2,1,0:T(8,128)(2,1)}), bf16[8,32,1024]{2,1,0:T(8,128)(2,1)S(1)}, u32[]{:S(2)}, u32[]{:S(2)}) async-start(bf16[8,32,1024]{2,1,0:T(8,128)(2,1)} %bitcast.25), calls=%async_computation.4 | async-start | bytes 1048576 | tf_op jit(solution)/shard_map/all_to_all | solution.py:208
  105.1 1.9 slice_bitcast_fusion
  107.0 10.0 %shard_map.155 = (bf16[1024,128]{1,0:T(8,128)(2,1)S(1)}, bf16[1024,128]{1,0:T(8,128)(2,1)S(1)}, bf16[1024,128]{1,0:T(8,128)(2,1)S(1)}, bf16[1024,128]{1,0:T(8,128)(2,1)S(1)}) custom-call(bf16[1024,128]{1,0:T(8,128)(2,1)S(1)} %bitcast.76, bf16[1024,128]{1,0:T(8,128)(2,1)S(1)} %bitcast.75, bf16[1024,128]{1,0:T(8,128)(2,1)S(1)} %bitcast.74, ...), custom_call_target="tpu_custom_call" | custom-call | tf_op jit(solution)/shard_map/pallas_call | solution.py:161
  117.2 1.1 copy.61
  118.3 4.4 %all-to-all-done.4 = bf16[8,32,1024]{2,1,0:T(8,128)(2,1)S(1)} async-done(((bf16[8,32,1024]{2,1,0:T(8,128)(2,1)}), bf16[8,32,1024]{2,1,0:T(8,128)(2,1)S(1)}, u32[]{:S(2)}, u32[]{:S(2)}) %all-to-all-start.4) | async-done | bytes 524320 | tf_op jit(solution)/shard_map/all_to_all | solution.py:208
  122.7 3.7 %all-to-all-start.1 = ((bf16[4,32,32,128]{3,2,0,1:T(8,128)(2,1)}), bf16[4,32,32,128]{3,2,0,1:T(8,128)(2,1)}, u32[]{:S(2)}, u32[]{:S(2)}) async-start(bf16[4,32,32,128]{3,2,0,1:T(8,128)(2,1)} %copy.61), calls=%async_computation.1 | async-start | bytes 2097152 | tf_op jit(solution)/shard_map/all_to_all | solution.py:219
  127.1 26.8 %all-to-all-done.1 = bf16[4,32,32,128]{3,2,0,1:T(8,128)(2,1)} async-done(((bf16[4,32,32,128]{3,2,0,1:T(8,128)(2,1)}), bf16[4,32,32,128]{3,2,0,1:T(8,128)(2,1)}, u32[]{:S(2)}, u32[]{:S(2)}) %all-to-all-start.1) | async-done | bytes 1048608 | tf_op jit(solution)/shard_map/all_to_all | solution.py:219
  154.0 2.1 %fusion.26 = (bf16[1,32,32,128]{3,2,0,1:T(8,128)(2,1)S(1)}, bf16[1,32,32,128]{3,2,0,1:T(8,128)(2,1)S(1)}, bf16[1,32,32,128]{3,2,0,1:T(8,128)(2,1)}, bf16[1,32,32,128]{3,2,0,1:T(8,128)(2,1)}) fusion(bf16[4,32,32,128]{3,2,0,1:T(8,128)(2,1)} %all-to-all-done.1), kind=kLoop, calls=%fused_computation.48 | loop fusion | bytes 2097152 | tf_op jit(solution)/shard_map/slice | solution.py:222
  156.9 0.8 copy.68
  157.7 4.8 %fusion.4 = bf16[1024,3,32]{0,2,1:T(8,128)(2,1)S(1)} fusion(bf16[32,128,1024,1]{2,1,0,3:T(8,128)(2,1)} %bitcast.79, bf16[1,32,32,128]{3,2,1,0:T(8,128)(2,1)S(1)} %get-tuple-element.35, bf16[1,32,32,128]{3,2,1,0:T(8,128)(2,1)S(1)} %bitcast.77, bf16[1,32,32,128]{3,2,1,0:T(8,128)(2,1)S(1)} %bitcast.78), kind=kOutput, calls=%fused_computation.9 | convolution fusion | flops 806289408 | bytes 9371648 | tf_op jit(solution)/shard_map/dtw,fdct->wfc/dot_general | solution.py:213
  163.1 1.5 copy.63
  164.7 2.8 %all-to-all-start.2 = ((bf16[32,32,96]{2,1,0:T(8,128)(2,1)}), bf16[32,32,96]{2,1,0:T(8,128)(2,1)S(1)}, u32[]{:S(2)}, u32[]{:S(2)}) async-start(bf16[32,32,96]{2,1,0:T(8,128)(2,1)} %copy.63), calls=%async_computation.2 | async-start | bytes 524288 | tf_op jit(solution)/shard_map/all_to_all | solution.py:215
  167.4 5.9 %convolution_convert_fusion.1 = bf16[128,1024]{1,0:T(8,128)(2,1)} fusion(bf16[1024,3072]{1,0:T(8,128)(2,1)} %param.14, bf16[1024,128]{1,0:T(8,128)(2,1)S(1)} %copy-done.8, bf16[1024,128]{1,0:T(8,128)(2,1)} %bitcast.86, bf16[1024,128]{1,0:T(8,128)(2,1)} %bitcast.87), kind=kOutput, calls=%fused_computation.5 | convolution fusion | flops 807796736 | bytes 7340032 | tf_op jit(solution)/shard_map/dot_general | solution.py:221
  173.3 4.3 %all-to-all-done.2 = bf16[32,32,96]{2,1,0:T(8,128)(2,1)S(1)} async-done(((bf16[32,32,96]{2,1,0:T(8,128)(2,1)}), bf16[32,32,96]{2,1,0:T(8,128)(2,1)S(1)}, u32[]{:S(2)}, u32[]{:S(2)}) %all-to-all-start.2) | async-done | bytes 196640 | tf_op jit(solution)/shard_map/all_to_all | solution.py:215
  177.6 1.8 reshape.46
  179.4 3.6 %copy.64 = f32[32,3,32,32]{3,2,1,0:T(8,128)} copy(f32[32,3,32,32]{3,1,0,2:T(4,128)} %bitcast.80) | data formatting | bytes 786432 | tf_op jit(solution)/shard_map/convert_element_type | solution.py:222
  183.1 2.9 %reshape.45 = f32[32,3072]{1,0:T(8,128)} reshape(f32[32,3,32,32]{3,2,1,0:T(8,128)} %copy.64) | data formatting | bytes 786432 | tf_op jit(solution)/shard_map/convert_element_type | solution.py:222
  (39 shorter events, 5.7 us)
Async XLA Ops:
  7.2 16.3 %copy-start = (bf16[1024,1024]{1,0:T(8,128)(2,1)S(1)}, bf16[1024,1024]{1,0:T(8,128)(2,1)}, u32[]{:S(2)}) copy-start(bf16[1024,1024]{1,0:T(8,128)(2,1)} %param.15) | copy-start | bytes 6291460
  7.2 150.6 %all-gather.3.cloned.1.call-start = ((), (), s32[]{:S(2)}) async-start(), calls=%async_computation.5 | async-start | bytes 8650752 | tf_op jit(solution)/shard_map/all_gather | solution.py:187
  9.0 10.7 %copy-start.9 = (bf16[128,1024]{1,0:T(8,128)(2,1)S(1)}, bf16[128,1024]{1,0:T(8,128)(2,1)}, u32[]{:S(2)}) copy-start(bf16[128,1024]{1,0:T(8,128)(2,1)} %param.19) | copy-start | bytes 786436
  14.5 13.3 %all-to-all-start.3 = ((bf16[4,256,128]{2,1,0:T(8,128)(2,1)}), bf16[4,256,128]{2,1,0:T(8,128)(2,1)}, u32[]{:S(2)}, u32[]{:S(2)}) async-start(bf16[4,256,128]{2,1,0:T(8,128)(2,1)} %bitcast.22), calls=%async_computation.3 | async-start | bytes 524288 | tf_op jit(solution)/shard_map/all_to_all | solution.py:203
  23.5 1.7 copy-start.6
  23.5 1.8 copy-start.5
  27.8 6.7 %copy-start.7 = (bf16[128,1024]{1,0:T(8,128)(2,1)S(1)}, bf16[128,1024]{1,0:T(8,128)(2,1)}, u32[]{:S(2)}) copy-start(bf16[128,1024]{1,0:T(8,128)(2,1)} %param.13) | copy-start | bytes 786436
  27.8 73.7 %all-to-all-start = ((bf16[7,32,32,128]{3,2,0,1:T(8,128)(2,1)}), bf16[7,32,32,128]{3,2,0,1:T(8,128)(2,1)}, u32[]{:S(2)}, u32[]{:S(2)}) async-start(bf16[7,32,32,128]{3,2,0,1:T(8,128)(2,1)} %copy.60), calls=%async_computation | async-start | bytes 3670016 | tf_op jit(solution)/shard_map/all_to_all | solution.py:201
  34.6 28.8 %collective-permute-start = (bf16[1,128,1024]{2,1,0:T(8,128)(2,1)S(1)}, bf16[1,128,1024]{2,1,0:T(8,128)(2,1)S(1)}, u32[]{:S(2)}, u32[]{:S(2)}) collective-permute-start(bf16[1,128,1024]{2,1,0:T(8,128)(2,1)S(1)} %bitcast.85), channel_id=1, source_target_pairs={{0,8},{8,0},{16,24},{24,16},{1,9},{9,1},{17,25},{25,17},{2,10},{10... | collective-permute-start | bytes 786440 | tf_op jit(solution)/shard_map/ppermute | solution.py:175
  64.3 15.1 %collective-permute-start.1 = (bf16[2,128,1024]{2,1,0:T(8,128)(2,1)}, bf16[2,128,1024]{2,1,0:T(8,128)(2,1)S(1)}, u32[]{:S(2)}, u32[]{:S(2)}) collective-permute-start(bf16[2,128,1024]{2,1,0:T(8,128)(2,1)} %pad_maximum_fusion.1), channel_id=1, source_target_pairs={{0,16},{8,24},{16,0},{24,8},{1,17},{9,25},{17,1},{25,9},{2,18},{10... | collective-permute-start | bytes 1572872 | tf_op jit(solution)/shard_map/ppermute | solution.py:175
  101.5 21.2 %all-to-all-start.4 = ((bf16[8,32,1024]{2,1,0:T(8,128)(2,1)}), bf16[8,32,1024]{2,1,0:T(8,128)(2,1)S(1)}, u32[]{:S(2)}, u32[]{:S(2)}) async-start(bf16[8,32,1024]{2,1,0:T(8,128)(2,1)} %bitcast.25), calls=%async_computation.4 | async-start | bytes 1048576 | tf_op jit(solution)/shard_map/all_to_all | solution.py:208
  105.0 2.0 %copy-start.1 = (bf16[256,256]{1,0:T(8,128)(2,1)S(1)}, bf16[256,256]{1,0:T(8,128)(2,1)}, u32[]{:S(2)}) copy-start(bf16[256,256]{1,0:T(8,128)(2,1)} %constant.24.clone.forward) | copy-start | bytes 393220
  105.1 2.0 %copy-start.2 = (bf16[256,256]{1,0:T(8,128)(2,1)S(1)}, bf16[256,256]{1,0:T(8,128)(2,1)}, u32[]{:S(2)}) copy-start(bf16[256,256]{1,0:T(8,128)(2,1)} %constant.25.clone.backward) | copy-start | bytes 393220
  105.1 2.0 %copy-start.3 = (f32[256,128]{1,0:T(8,128)S(1)}, f32[256,128]{1,0:T(8,128)}, u32[]{:S(2)}) copy-start(f32[256,128]{1,0:T(8,128)} %constant.26.clone.turn_cos) | copy-start | bytes 393220
  105.1 2.0 %copy-start.4 = (f32[256,128]{1,0:T(8,128)S(1)}, f32[256,128]{1,0:T(8,128)}, u32[]{:S(2)}) copy-start(f32[256,128]{1,0:T(8,128)} %constant.27.clone.turn_sin) | copy-start | bytes 393220
  122.7 31.2 %all-to-all-start.1 = ((bf16[4,32,32,128]{3,2,0,1:T(8,128)(2,1)}), bf16[4,32,32,128]{3,2,0,1:T(8,128)(2,1)}, u32[]{:S(2)}, u32[]{:S(2)}) async-start(bf16[4,32,32,128]{3,2,0,1:T(8,128)(2,1)} %copy.61), calls=%async_computation.1 | async-start | bytes 2097152 | tf_op jit(solution)/shard_map/all_to_all | solution.py:219
  162.6 4.9 %copy-start.8 = (bf16[1024,128]{1,0:T(8,128)(2,1)S(1)}, bf16[1024,128]{1,0:T(8,128)(2,1)}, u32[]{:S(2)}) copy-start(bf16[1024,128]{1,0:T(8,128)(2,1)} %get-tuple-element.34) | copy-start | bytes 786436
  164.7 13.0 %all-to-all-start.2 = ((bf16[32,32,96]{2,1,0:T(8,128)(2,1)}), bf16[32,32,96]{2,1,0:T(8,128)(2,1)S(1)}, u32[]{:S(2)}, u32[]{:S(2)}) async-start(bf16[32,32,96]{2,1,0:T(8,128)(2,1)} %copy.63), calls=%async_computation.2 | async-start | bytes 524288 | tf_op jit(solution)/shard_map/all_to_all | solution.py:215
Sparse Core Ops, SparseCore 0:
  11.0 105.0 all-gather.2

commit v2 on v1

v2 whole, which is shorter than its diff:
```python
import functools
import math

import jax
import jax.numpy as jnp
import numpy as np
from jax import lax
from jax.experimental import pallas as pl
from jax.experimental.pallas import tpu as pltpu
from jax.sharding import PartitionSpec as P

AXES = ("major", "minor")
LAST = (((1,), (1,)), ((), ()))


def product(left, right):
    return (left.astype(jnp.float32) * right.astype(jnp.float32)).astype(jnp.bfloat16)


def tables(devices, rows_dev):
    seq_len = devices * rows_dev
    line = np.arange(rows_dev)
    angle = -2.0 * math.pi * (line[:, None] * line[None, :] % rows_dev) / rows_dev
    cos, sin = np.cos(angle), np.sin(angle)
    forward = np.block([[cos, sin], [-sin, cos]])
    backward = np.block([[cos, -sin], [sin, cos]])
    turn = -2.0 * math.pi * (np.arange(devices)[:, None] + 0.25) * line[None, :] / seq_len
    turn_cos = np.repeat(np.cos(turn), 8, axis=0)
    turn_sin = np.repeat(np.sin(turn), 8, axis=0)
    return (
        jnp.asarray(forward, jnp.bfloat16),
        jnp.asarray(backward, jnp.bfloat16),
        jnp.asarray(turn_cos, jnp.float32),
        jnp.asarray(turn_sin, jnp.float32),
    )


def fft_real(xs):
    size = len(xs)
    if size == 1:
        return [(xs[0], None)]
    if size == 2:
        turned = xs[1] * math.cos(math.pi / 4)
        return [(xs[0] + turned, -turned), (xs[0] - turned, turned)]
    even, odd = fft_real(xs[0::2]), fft_real(xs[1::2])
    low, high = [], []
    for k in range(size // 2):
        angle = -2.0 * math.pi * (k + 0.25) / size
        cos, sin = math.cos(angle), math.sin(angle)
        (er, ei), (orr, oi) = even[k], odd[k]
        tr = orr * cos - oi * sin
        ti = orr * sin + oi * cos
        low.append((er + tr, ei + ti))
        high.append((er - tr, ei - ti))
    return low + high


def fft_back(pairs):
    size = len(pairs)
    if size == 2:
        (ar, ai), (br, bi) = pairs
        return [ar + br, ((ar - br) - (ai - bi)) * math.cos(math.pi / 4)]
    half = size // 2
    even, odd = [], []
    for k in range(half):
        angle = 2.0 * math.pi * (k + 0.25) / size
        cos, sin = math.cos(angle), math.sin(angle)
        (ar, ai), (br, bi) = pairs[k], pairs[k + half]
        even.append((ar + br, ai + bi))
        dr, di = ar - br, ai - bi
        odd.append((dr * cos - di * sin, dr * sin + di * cos))
    even, odd = fft_back(even), fft_back(odd)
    return [term for pair in zip(even, odd) for term in pair]


def transforms(devices, group, held, turn_cos, turn_sin):
    cols = held.shape[1]

    def into(spec):
        def step(j, carry):
            xs = [held[pl.ds(n * group + j * 8, 8), :] for n in range(devices)]
            for k, (re, im) in enumerate(fft_real(xs)):
                cos, sin = turn_cos[8 * k : 8 * k + 8, :], turn_sin[8 * k : 8 * k + 8, :]
                at = pl.ds(k * group + j * 8, 8)
                spec[at, :cols] = re * cos - im * sin
                spec[at, cols:] = re * sin + im * cos
            return carry

        lax.fori_loop(0, group // 8, step, 0)

    def outof(spec, scale):
        def step(j, carry):
            pairs = []
            for k in range(devices):
                cos, sin = turn_cos[8 * k : 8 * k + 8, :], turn_sin[8 * k : 8 * k + 8, :]
                at = pl.ds(k * group + j * 8, 8)
                re, im = spec[at, :cols], spec[at, cols:]
                pairs.append((re * cos + im * sin, im * cos - re * sin))
            for n, term in enumerate(fft_back(pairs)):
                held[pl.ds(n * group + j * 8, 8), :] = term * scale
            return carry

        lax.fori_loop(0, group // 8, step, 0)

    return into, outof


def correlate(spec_a, spec_b, spec_c, forward, backward):
    rows, cols = spec_a.shape[0], spec_a.shape[1] // 2
    block = min(rows, 256)

    def step(i, carry):
        at = pl.ds(pl.multiple_of(i * block, block), block)

        def line(spec):
            moved = jnp.dot(spec[at, :].astype(jnp.bfloat16), forward[...], preferred_element_type=jnp.float32)
            return moved[:, :cols], moved[:, cols:]

        ar, ai = line(spec_a)
        for spec in (spec_b, spec_c):
            br, bi = line(spec)
            mixed = jnp.concatenate([ar * br + ai * bi, ai * br - ar * bi], axis=1).astype(jnp.bfloat16)
            spec[at, :] = jnp.dot(mixed, backward[...], preferred_element_type=jnp.float32)
        return carry

    lax.fori_loop(0, rows // block, step, 0)


def fetch(sources, slots, done):
    copies = [pltpu.make_async_copy(source, slot, done.at[i]) for i, (source, slot) in enumerate(zip(sources, slots))]
    for copy in copies:
        copy.start()
    return copies


def begin_kernel(
    square, conv_one, filter_two, filter_one, out_cot, conv_two, block_in, w_out, w_in,
    sent, second_out, late, rows_here, w_out_here, w_in_here, done,
):
    devices, _, group, lanes = sent.shape
    width = out_cot.shape[1]
    copies = fetch(
        [conv_one, filter_two, filter_one, out_cot, w_out, conv_two, block_in] + [w_in.at[:, i * width : (i + 1) * width] for i in (2, 1, 0)],
        [rows_here.at[i] for i in range(4)] + [w_out_here, rows_here.at[4], rows_here.at[5]] + [w_in_here.at[i] for i in (2, 1, 0)],
        done,
    )

    def turned(x):
        parts = [
            lax.dot_general(square[...], x[:, at : at + lanes], LAST, preferred_element_type=jnp.float32)
            for at in range(0, width, lanes)
        ]
        return jnp.concatenate(parts, axis=0).astype(jnp.bfloat16)

    def send(i, x):
        sent[:, i] = turned(x).reshape(devices, group, lanes)

    def project(i):
        return jnp.dot(rows_here[5], w_in_here[i], preferred_element_type=jnp.float32).astype(jnp.bfloat16)

    for i in range(3):
        copies[i].wait()
        send(i, rows_here[i])
    copies[3].wait()
    copies[4].wait()
    grad_second = lax.dot_general(rows_here[3], w_out_here[...], LAST, preferred_element_type=jnp.float32).astype(jnp.bfloat16)
    copies[5].wait()
    grad_gate_two = product(grad_second, rows_here[4])
    late[...] = grad_gate_two
    send(6, grad_gate_two)
    copies[6].wait()
    copies[7].wait()
    gate_two = project(2)
    send(3, product(grad_second, gate_two))
    second_out[...] = turned(product(gate_two, rows_here[4]))
    copies[8].wait()
    send(4, project(1))
    copies[9].wait()
    send(5, project(0))


def middle_kernel(scale, me, here, forward, backward, turn_cos, turn_sin, back, slab, held, spec_a, spec_b, spec_c):
    devices, _, group, cols = here.shape
    rows = devices * group
    into, outof = transforms(devices, group, held, turn_cos, turn_sin)
    flat = lambda i: here[:, i].astype(jnp.float32).reshape(rows, cols)
    blocks = lambda x: x.astype(jnp.bfloat16).reshape(devices, group, cols)

    def lay(kind, x):
        for n in range(devices):
            place = n ^ me[0]
            at = pl.ds(pl.multiple_of(((place & 1) * (devices // 2) + (place >> 1)) * cols, cols), cols)
            slab[kind * group : (kind + 1) * group, at] = x[n * group : (n + 1) * group].astype(slab.dtype)

    held[...] = flat(3)
    into(spec_a)
    held[...] = flat(1)
    into(spec_b)
    held[...] = (flat(4) * flat(0)).astype(jnp.bfloat16).astype(jnp.float32)
    into(spec_c)
    correlate(spec_a, spec_b, spec_c, forward, backward)
    outof(spec_c, scale)
    back[:, 3] = blocks(held[...])
    outof(spec_b, scale)
    grad_first = held[...].astype(jnp.bfloat16).astype(jnp.float32)
    gate_grad = grad_first * flat(0)
    back[:, 1] = blocks(gate_grad)
    lay(1, gate_grad)
    held[...] = (grad_first * flat(4)).astype(jnp.bfloat16).astype(jnp.float32)
    into(spec_a)
    held[...] = flat(2)
    into(spec_b)
    held[...] = flat(5)
    into(spec_c)
    lay(2, flat(6))
    slab[3 * group :, :] = jnp.zeros((cols - 3 * group, devices * cols), slab.dtype)
    correlate(spec_a, spec_b, spec_c, forward, backward)
    outof(spec_c, scale)
    back[:, 2] = blocks(held[...])
    outof(spec_b, scale)
    back[:, 0] = blocks(held[...])
    lay(0, held[...])


def slab_kernel(scale, slab, *refs):
    *pieces, part, slots, done = refs
    count, (depth, steps, width) = len(pieces), slots.shape
    devices, group, cols = part.shape
    copies = [pltpu.make_async_copy(piece, slots.at[i % depth], done.at[i]) for i, piece in enumerate(pieces)]
    for copy in copies[:depth]:
        copy.start()
    total = jnp.zeros((cols, width), jnp.float32)
    for i, copy in enumerate(copies):
        copy.wait()
        total += jnp.dot(slab[:, i * steps : (i + 1) * steps], slots[i % depth], preferred_element_type=jnp.float32)
        if i + depth < count:
            copies[i + depth].start()
    part[...] = (total * scale).T.astype(jnp.bfloat16).reshape(devices, group, cols)


def on_chip(kernel, out_shape, args, scratch=(), far=(), vmem_mib=48):
    vmem = pl.BlockSpec(memory_space=pltpu.VMEM)
    spaces = [pltpu.SMEM if x.dtype == jnp.int32 else pltpu.HBM if i in far else pltpu.VMEM for i, x in enumerate(args)]
    return pl.pallas_call(
        kernel,
        out_shape=out_shape,
        in_specs=[pl.BlockSpec(memory_space=space) for space in spaces],
        out_specs=jax.tree.map(lambda _: vmem, out_shape),
        scratch_shapes=list(scratch),
        compiler_params=pltpu.CompilerParams(vmem_limit_bytes=vmem_mib * 2**20),
    )(*args)


def long_convs(rows, rows_dev):
    spec = pltpu.VMEM((rows, 2 * rows_dev), jnp.float32)
    return [pltpu.VMEM((rows, rows_dev), jnp.float32), spec, spec, spec]


def home_kernel(square, home, part, w_in, in_grad, filter_one_grad, filter_two_grad, home_here, part_here, w_in_here, done):
    devices, _, group, lanes = home.shape
    width = devices * group
    copies = fetch(
        [home, part] + [w_in.at[:, i * width : (i + 1) * width] for i in range(2)],
        [home_here, part_here] + [w_in_here.at[i] for i in range(2)],
        done,
    )

    def whole(i):
        field = home_here[:, i].astype(jnp.float32).reshape(width, lanes).astype(jnp.bfloat16)
        return lax.dot_general(square[...], field, LAST, preferred_element_type=jnp.float32).astype(jnp.bfloat16)

    copies[0].wait()
    filter_one_grad[...] = whole(2)
    filter_two_grad[...] = whole(3)
    copies[1].wait()
    total = part_here[...]
    for i in (0, 1):
        copies[2 + i].wait()
        total += lax.dot_general(whole(i), w_in_here[i], LAST, preferred_element_type=jnp.float32)
    in_grad[...] = total.astype(jnp.bfloat16)


def place_kernel(taken, moves, w_in_grad):
    devices, group, lanes = taken.shape
    per, kinds = moves.shape[0], moves.shape[2] // lanes
    for g in range(devices // per):
        total = jnp.zeros((group, kinds * lanes), jnp.float32)
        for s in range(per):
            total += jnp.dot(taken[g * per + s], moves[s], preferred_element_type=jnp.float32)
        for f in range(kinds):
            at = f * devices * group + g * lanes
            w_in_grad[:, at : at + lanes] = total[:, f * lanes : (f + 1) * lanes]


def moves_of(group, lanes, kinds):
    per = lanes // group
    table = np.zeros((per, lanes, kinds * lanes), np.float32)
    for s in range(per):
        for f in range(kinds):
            for c in range(group):
                table[s, f * group + c, f * lanes + s * group + c] = 1.0
    return jnp.asarray(table, jnp.bfloat16)


def bits_of(count):
    return [1 << i for i in range(count.bit_length() - 1)]


def swap(block, axis, bit):
    return lax.ppermute(block, axis, [(i, i ^ bit) for i in range(lax.axis_size(axis))])


def after(x, *others):
    return lax.optimization_barrier((x, *others))[0]


def near_chips(block):
    bits = bits_of(lax.axis_size("minor"))[1:]
    blocks = [block] + [None] * (2 ** len(bits) - 1)
    for bit in bits:
        blocks[bit // 2] = swap(block, "minor", bit)
    return blocks


def far_chips(blocks, later):
    blocks = [block if block is None else after(block, later) for block in blocks]
    for j in range(1, len(blocks)):
        low = j & -j
        if j != low:
            blocks[j] = swap(blocks[j ^ low], "minor", 2 * low)
    return blocks


def major_near(blocks):
    half = max(len(blocks) // 2, 1)
    lines = []
    for part in (blocks[:half], blocks[half:]):
        held = [jnp.concatenate(part)] + [None] * (lax.axis_size("major") - 1)
        for bit in bits_of(lax.axis_size("major")):
            held[bit] = swap(held[0], "major", bit)
        lines.append(held)
    return lines


def gather_chips(lines, later):
    pieces = []
    for turn, line in enumerate(lines):
        held = [piece if piece is None else after(piece, later) for piece in line]
        for j in range(1, len(held)):
            bit = j & -j if turn else 1 << (j.bit_length() - 1)
            if j != bit:
                held[j] = swap(held[j ^ bit], "major", bit)
        pieces.append(held)
    return [piece for pair in zip(*pieces) for piece in pair]


def out_part(second_out, cots):
    width, rows_dev = second_out.shape
    majors, minors = lax.axis_size("major"), lax.axis_size("minor")
    mine = lax.axis_index("major")
    slabs = second_out.reshape(majors, width // majors, rows_dev)
    slab = [lax.dynamic_index_in_dim(slabs, mine ^ j, 0, keepdims=False) for j in range(majors)]
    slab = jnp.stack([swap(part, "major", j) if j else part for j, part in enumerate(slab)])
    total = jnp.einsum("mct,mtw->cw", slab, jnp.stack(cots), preferred_element_type=jnp.float32)
    total = total.reshape(minors // 2, 2, -1, total.shape[1])
    mine = lax.axis_index("minor") % 2
    part = lambda core: lax.dynamic_index_in_dim(total, core, 1, keepdims=False)
    return part(mine) + swap(part(1 - mine), "minor", 1)


def out_sum(total):
    mine = lax.axis_index("minor") // 2
    part = lambda chip: lax.dynamic_index_in_dim(total, chip, 0, keepdims=False)
    sums = part(mine)
    for j in range(1, total.shape[0]):
        sums += swap(part(mine ^ j).astype(jnp.bfloat16), "minor", 2 * j).astype(jnp.float32)
    return sums


def regroup(x):
    return lax.all_to_all(x, AXES, split_axis=0, concat_axis=0, tiled=True)


def shards(block_in, out_cot, w_in, w_out, conv_one, conv_two, filter_one, filter_two):
    rows_dev, width = block_in.shape
    devices, majors = lax.axis_size(AXES), lax.axis_size("major")
    group = width // devices
    scale = (rows_dev * devices) ** (-0.5)
    fft_scale = scale / (rows_dev * devices)
    field = lambda *dims: jax.ShapeDtypeStruct((devices, *dims, group, rows_dev), jnp.bfloat16)
    array = lambda *dims: jax.ShapeDtypeStruct(dims, jnp.bfloat16)

    near_in = near_chips(block_in)
    square = jnp.eye(rows_dev, dtype=jnp.bfloat16)
    sent, second_out, late = on_chip(
        begin_kernel,
        [field(7), array(width, rows_dev), array(rows_dev, width)],
        (square, conv_one, filter_two, filter_one, out_cot, conv_two, block_in, w_out, w_in),
        [
            pltpu.VMEM((6, rows_dev, width), jnp.bfloat16),
            pltpu.VMEM((width, width), jnp.bfloat16),
            pltpu.VMEM((3, width, width), jnp.bfloat16),
            pltpu.SemaphoreType.DMA((10,)),
        ],
        range(1, 9),
        60,
    )
    cots = [swap(out_cot, "major", j) if j else out_cot for j in range(majors)]
    sent = after(sent, *cots, *[block for block in near_in if block is not None])
    here = regroup(sent)
    total = out_part(after(second_out, sent), cots)
    late = lax.dot_general(late, w_in[:, 2 * width :], LAST, preferred_element_type=jnp.float32)
    lines = major_near(far_chips(near_in, sent))
    here = after(here, late, total, *[piece for line in lines for piece in line if piece is not None])

    spec = pltpu.VMEM((devices * group, 2 * rows_dev), jnp.float32)
    back, slab = on_chip(
        functools.partial(middle_kernel, fft_scale),
        [field(4), array(rows_dev, devices * rows_dev)],
        (lax.axis_index(AXES).astype(jnp.int32)[None], here, *tables(devices, rows_dev)),
        [pltpu.VMEM((devices * group, rows_dev), jnp.float32), spec, spec, spec],
    )
    home = regroup(back)
    all_in = gather_chips(lines, back)
    all_in += [swap(piece, "minor", 1) for piece in all_in]
    w_out_grad = out_sum(after(total, back)) * scale

    rows = all_in[0].shape[0]
    slots = min(len(all_in), 16 * 2**20 // (2 * rows * width))
    part = on_chip(
        functools.partial(slab_kernel, scale),
        field(),
        (slab, *all_in),
        [pltpu.VMEM((slots, rows, width), jnp.bfloat16), pltpu.SemaphoreType.DMA((len(all_in),))],
        range(1, 1 + len(all_in)),
        60,
    )
    taken = regroup(after(part, home, w_out_grad))
    in_grad, filter_one_grad, filter_two_grad = on_chip(
        home_kernel,
        [array(rows_dev, width)] * 3,
        (square, home, late, w_in),
        [
            pltpu.VMEM(home.shape, jnp.bfloat16),
            pltpu.VMEM((rows_dev, width), jnp.float32),
            pltpu.VMEM((2, width, width), jnp.bfloat16),
            pltpu.SemaphoreType.DMA((4,)),
        ],
        range(1, 4),
        60,
    )
    w_in_grad = on_chip(
        place_kernel, jax.ShapeDtypeStruct((group, 3 * width), jnp.float32), (taken, moves_of(group, rows_dev, 3))
    )
    return in_grad, w_in_grad, w_out_grad, filter_one_grad, filter_two_grad


def solution(mesh):
    tokens = P(AXES, None)
    return jax.shard_map(
        shards,
        mesh=mesh,
        in_specs=(tokens, tokens, P(), P(), tokens, tokens, tokens, tokens),
        out_specs=(tokens,) * 5,
        check_vma=False,
    )
```

time: 194 us -> 155 us (0.80)
  waiting for transfers between devices: 96.8 us -> 71.1 us
  Pallas kernels: 10 us -> 31 us
  local copies, waits for them, and re-layouts: 23.8 us -> 3.51 us
  starting transfers between devices: 25.1 us -> 41.4 us
  matrix products: 19.4 us -> 4.74 us
  between operations: 14.3 us -> 1.06 us
  other arithmetic: 3.38 us -> 1.36 us
    all_to_all x5 -> x3, waiting for transfers between devices: 55.4 us -> 5.03 us  [regroup(): return lax.all_to_all(x, AXES, split_axis=0, concat_axis=0, tiled=True)]
    ppermute x2 -> x27, starting transfers between devices: 3.24 us -> 29.3 us  [swap(): lax.ppermute(block, axis, [(i, i ^ bit) for i in range(lax.axis_size(axis...]
    ppermute x2 -> x27, waiting for transfers between devices: 40.7 us -> 66 us  [swap(): lax.ppermute(block, axis, [(i, i ^ bit) for i in range(lax.axis_size(axis...]
    pallas_call x1 -> x5, Pallas kernels: 10 us -> 31 us  [on_chip(): pl.pallas_call(kernel, out_shape=out_shape, in_specs=[pl.BlockSpec(memory...]
    dot_general x5 -> x2, matrix products: 19.4 us -> 4.74 us  [the longest x1 3.27 us: shards(): lax.dot_general(late, w_in[:, 2 * width:], LAST, preferred_element_type=j...]
    all_to_all x5 -> x3, starting transfers between devices: 21.8 us -> 12.1 us  [regroup(): return lax.all_to_all(x, AXES, split_axis=0, concat_axis=0, tiled=True)]
    convert_element_type x3 -> x1, local copies, waits for them, and re-layouts: 8.28 us -> 0.03 us  [out_sum(): part(mine ^ j).astype(jnp.bfloat16)]
    unnamed x32 -> x50, local copies, waits for them, and re-layouts: 8.73 us -> 3.37 us
  transfers between devices with their start and end apart: 8 -> 30, of which waited for: 6 -> 14; matrix products, arithmetic and copies ran while one was open for 16% -> 4% of each run, Pallas kernels for 5% -> 12%
where the time goes in v2:
time: 155 us; the launch traced here: 154 us
  waiting for transfers between devices  71.1 us (46%)
  starting transfers between devices  41.4 us (27%)
  Pallas kernels  31 us (20%)
  matrix products  4.74 us (3%)
  local copies, waits for them, and re-layouts  3.51 us (2%)
    ppermute x27, waiting for transfers between devices, swap(): lax.ppermute(block, axis, [(i, i ^ bit) for i in range(lax.axis_size(axis...  66 us
    pallas_call x5, Pallas kernels, on_chip(): pl.pallas_call(kernel, out_shape=out_shape, in_specs=[pl.BlockSpec(memory...  31 us
    ppermute x27, starting transfers between devices, swap(): lax.ppermute(block, axis, [(i, i ^ bit) for i in range(lax.axis_size(axis...  29.3 us
    all_to_all x3, starting transfers between devices, regroup(): return lax.all_to_all(x, AXES, split_axis=0, concat_axis=0, tiled=True)  12.1 us
    all_to_all x3, waiting for transfers between devices, regroup(): return lax.all_to_all(x, AXES, split_axis=0, concat_axis=0, tiled=True)  5.03 us
    unnamed x50, local copies, waits for them, and re-layouts  3.37 us
    dot_general x1, matrix products, shards(): lax.dot_general(late, w_in[:, 2 * width:], LAST, preferred_element_type=j...  3.27 us
  transfers between devices with their start and end apart: 30, of which 14 were waited for; matrix products, arithmetic and copies ran while one was open for 4% of the time, Pallas kernels for 12%

profile of v2, /device:TPU:0, one launch (start us, length us, event | category | flops | bytes accessed | tf_op | source)
XLA Modules:
  0.0 154.2 jit_solution(2549198182930680400)
XLA Ops:
  0.6 3.0 %collective-permute-start = (bf16[128,1024]{1,0:T(8,128)(2,1)}, bf16[128,1024]{1,0:T(8,128)(2,1)S(1)}, u32[]{:S(2)}, u32[]{:S(2)}) collective-permute-start(bf16[128,1024]{1,0:T(8,128)(2,1)} %out_cot.1), channel_id=1, source_target_pairs={{0,8},{8,0},{16,24},{24,16},{1,9},{9,1},{17,25},{25,17},{2,10},{10... | collective-permute-start | bytes 786440 | tf_op jit(solution)/shard_map/ppermute | solution.py:310
  3.6 1.5 collective-permute-start.1
  5.2 2.0 %collective-permute-start.3 = (bf16[128,1024]{1,0:T(8,128)(2,1)}, bf16[128,1024]{1,0:T(8,128)(2,1)S(1)}, u32[]{:S(2)}, u32[]{:S(2)}) collective-permute-start(bf16[128,1024]{1,0:T(8,128)(2,1)} %block_in.1), channel_id=1, source_target_pairs={{0,2},{1,3},{2,0},{3,1},{4,6},{5,7},{6,4},{7,5},{8,10},{9,11},{10,... | collective-permute-start | bytes 786440 | tf_op jit(solution)/shard_map/ppermute | solution.py:310
  7.2 2.6 %collective-permute-start.4 = (bf16[128,1024]{1,0:T(8,128)(2,1)}, bf16[128,1024]{1,0:T(8,128)(2,1)S(1)}, u32[]{:S(2)}, u32[]{:S(2)}) collective-permute-start(bf16[128,1024]{1,0:T(8,128)(2,1)} %block_in.1), channel_id=1, source_target_pairs={{0,4},{1,5},{2,6},{3,7},{4,0},{5,1},{6,2},{7,3},{8,12},{9,13},{10,... | collective-permute-start | bytes 786440 | tf_op jit(solution)/shard_map/ppermute | solution.py:310
  10.4 7.3 %shard_map.164 = (bf16[32,7,32,128]{3,2,1,0:T(8,128)(2,1)}, bf16[1024,128]{1,0:T(8,128)(2,1)}, bf16[128,1024]{1,0:T(8,128)(2,1)}) custom-call(bf16[128,128]{1,0:T(8,128)(2,1)} %fusion.23.square, bf16[128,1024]{1,0:T(8,128)(2,1)} %conv_one.1, bf16[128,1024]{1,0:T(8,128)(2,1)} %filter_two.1, bf16[128,1024]{1,0:T(8,128)(2,1)} %filter_one.1, ...), custom_call_target="tpu_custom_call" | custom-call | tf_op jit(solution)/shard_map/pallas_call | solution.py:244
  18.4 2.6 %collective-permute-done.4 = bf16[128,1024]{1,0:T(8,128)(2,1)S(1)} collective-permute-done((bf16[128,1024]{1,0:T(8,128)(2,1)}, bf16[128,1024]{1,0:T(8,128)(2,1)S(1)}, u32[]{:S(2)}, u32[]{:S(2)}) %collective-permute-start.4) | collective-permute-done | bytes 262176 | tf_op jit(solution)/shard_map/ppermute | solution.py:310
  20.9 4.7 %all-to-all-start = ((bf16[32,7,32,128]{3,2,1,0:T(8,128)(2,1)}), bf16[32,7,32,128]{3,2,1,0:T(8,128)(2,1)S(1)}, u32[]{:S(2)}, u32[]{:S(2)}) async-start(bf16[32,7,32,128]{3,2,1,0:T(8,128)(2,1)} %get-tuple-element.28), calls=%async_computation | async-start | bytes 3670016 | tf_op jit(solution)/shard_map/all_to_all | solution.py:381
  25.7 1.8 %collective-permute-start.5 = (bf16[256,128]{1,0:T(8,128)(2,1)S(1)}, bf16[256,128]{1,0:T(8,128)(2,1)S(1)}, u32[]{:S(2)}, u32[]{:S(2)}) collective-permute-start(bf16[256,128]{1,0:T(8,128)(2,1)S(1)} %get-tuple-element.55), channel_id=1, source_target_pairs={{0,8},{8,0},{16,24},{24,16},{1,9},{9,1},{17,25},{25,17},{2,10},{10... | collective-permute-start | bytes 196616 | tf_op jit(solution)/shard_map/ppermute | solution.py:310
  27.6 1.5 collective-permute-start.6
  29.4 1.8 %collective-permute-start.10 = (bf16[256,1024]{1,0:T(8,128)(2,1)S(1)}, bf16[256,1024]{1,0:T(8,128)(2,1)S(1)}, u32[]{:S(2)}, u32[]{:S(2)}) collective-permute-start(bf16[256,1024]{1,0:T(8,128)(2,1)S(1)} %constant_dynamic-update-slice_fusion.refs_0_), channel_id=1, source_target_pairs={{0,16},{8,24},{16,0},{24,8},{1,17},{9,25},{17,1},{25,9},{2,18},{10... | collective-permute-start | bytes 1572872 | tf_op jit(solution)/shard_map/ppermute | solution.py:310
  31.2 1.5 collective-permute-start.9
  32.7 7.1 %collective-permute-done.5 = bf16[256,128]{1,0:T(8,128)(2,1)S(1)} collective-permute-done((bf16[256,128]{1,0:T(8,128)(2,1)S(1)}, bf16[256,128]{1,0:T(8,128)(2,1)S(1)}, u32[]{:S(2)}, u32[]{:S(2)}) %collective-permute-start.5) | collective-permute-done | bytes 65568 | tf_op jit(solution)/shard_map/ppermute | solution.py:310
  41.1 2.7 %collective-permute-done.7 = bf16[256,128]{1,0:T(8,128)(2,1)S(1)} collective-permute-done((bf16[256,128]{1,0:T(8,128)(2,1)S(1)}, bf16[256,128]{1,0:T(8,128)(2,1)S(1)}, u32[]{:S(2)}, u32[]{:S(2)}) %collective-permute-start.7) | collective-permute-done | bytes 65568 | tf_op jit(solution)/shard_map/ppermute | solution.py:310
  43.8 1.5 fusion.2
  45.5 16.2 %collective-permute-done.11 = bf16[128,1024]{1,0:T(8,128)(2,1)S(1)} collective-permute-done((bf16[128,1024]{1,0:T(8,128)(2,1)S(1)}, bf16[128,1024]{1,0:T(8,128)(2,1)S(1)}, u32[]{:S(2)}, u32[]{:S(2)}) %collective-permute-start.11) | collective-permute-done | bytes 262176 | tf_op jit(solution)/shard_map/ppermute | solution.py:310
  61.7 1.7 %collective-permute-start.12 = (bf16[256,1024]{1,0:T(8,128)(2,1)S(1)}, bf16[256,1024]{1,0:T(8,128)(2,1)S(1)}, u32[]{:S(2)}, u32[]{:S(2)}) collective-permute-start(bf16[256,1024]{1,0:T(8,128)(2,1)S(1)} %constant_dynamic-update-slice_fusion.2.refs_1_), channel_id=1, source_target_pairs={{0,8},{8,0},{16,24},{24,16},{1,9},{9,1},{17,25},{25,17},{2,10},{10... | collective-permute-start | bytes 1572872 | tf_op jit(solution)/shard_map/ppermute | solution.py:310
  63.4 1.5 collective-permute-start.13
  64.9 3.3 %fusion.part = f32[128,1024]{1,0:T(8,128)} fusion(bf16[128,1024]{1,0:T(8,128)(2,1)S(1)} %copy-done.21, bf16[1024,3072]{1,0:T(8,128)(2,1)} %w_in.3), kind=kOutput, calls=%fused_computation | convolution fusion | flops 268435456 | bytes 2883584 | tf_op jit(solution)/shard_map/dot_general | solution.py:412
  68.3 8.9 %collective-permute-done.12.refs_3_ = bf16[256,1024]{1,0:T(8,128)(2,1)S(1)} collective-permute-done((bf16[256,1024]{1,0:T(8,128)(2,1)S(1)}, bf16[256,1024]{1,0:T(8,128)(2,1)S(1)}, u32[]{:S(2)}, u32[]{:S(2)}) %collective-permute-start.12) | collective-permute-done | bytes 524320 | tf_op jit(solution)/shard_map/ppermute | solution.py:310
  78.6 11.3 %shard_map.165 = (bf16[32,4,32,128]{3,2,1,0:T(8,128)(2,1)}, bf16[128,4096]{1,0:T(8,128)(2,1)S(1)}) custom-call(s32[1]{0:T(128)} %bitcast.me, bf16[32,7,32,128]{3,2,1,0:T(8,128)(2,1)S(1)} %all-to-all-done.here, bf16[256,256]{1,0:T(8,128)(2,1)S(1)} %copy-done.2, bf16[256,256]{1,0:T(8,128)(2,1)S(1)} %copy-done.3, f32[256,128]{1,0:T(8,128)S(1)} %copy-done.4, ...), custom_call_target="tpu_custom_call" | custom-call | tf_op jit(solution)/shard_map/pallas_call | solution.py:244
  90.8 4.2 %all-to-all-start.1 = ((bf16[32,4,32,128]{3,2,1,0:T(8,128)(2,1)}), bf16[32,4,32,128]{3,2,1,0:T(8,128)(2,1)S(1)}, u32[]{:S(2)}, u32[]{:S(2)}) async-start(bf16[32,4,32,128]{3,2,1,0:T(8,128)(2,1)} %get-tuple-element.36), calls=%async_computation.1 | async-start | bytes 2097152 | tf_op jit(solution)/shard_map/all_to_all | solution.py:381
  95.1 1.8 %collective-permute-start.24 = (bf16[32,1024]{1,0:T(8,128)(2,1)S(1)}, bf16[32,1024]{1,0:T(8,128)(2,1)S(1)}, u32[]{:S(2)}, u32[]{:S(2)}) collective-permute-start(bf16[32,1024]{1,0:T(8,128)(2,1)S(1)} %get-tuple-element.49), channel_id=1, source_target_pairs={{0,2},{1,3},{2,0},{3,1},{4,6},{5,7},{6,4},{7,5},{8,10},{9,11},{10,... | collective-permute-start | bytes 196616 | tf_op jit(solution)/shard_map/ppermute | solution.py:310
  97.0 2.4 %collective-permute-start.25 = (bf16[32,1024]{1,0:T(8,128)(2,1)S(1)}, bf16[32,1024]{1,0:T(8,128)(2,1)S(1)}, u32[]{:S(2)}, u32[]{:S(2)}) collective-permute-start(bf16[32,1024]{1,0:T(8,128)(2,1)S(1)} %get-tuple-element.51), channel_id=1, source_target_pairs={{0,4},{1,5},{2,6},{3,7},{4,0},{5,1},{6,2},{7,3},{8,12},{9,13},{10,... | collective-permute-start | bytes 196616 | tf_op jit(solution)/shard_map/ppermute | solution.py:310
  99.6 1.8 %collective-permute-start.15 = (bf16[256,1024]{1,0:T(8,128)(2,1)}, bf16[256,1024]{1,0:T(8,128)(2,1)}, u32[]{:S(2)}, u32[]{:S(2)}) collective-permute-start(bf16[256,1024]{1,0:T(8,128)(2,1)} %collective-permute-done.13.refs_5_), channel_id=1, source_target_pairs={{0,8},{8,0},{16,24},{24,16},{1,9},{9,1},{17,25},{25,17},{2,10},{10... | collective-permute-start | bytes 1572872 | tf_op jit(solution)/shard_map/ppermute | solution.py:310
  101.3 1.5 collective-permute-start.14
  102.8 11.5 %collective-permute-done.24 = bf16[32,1024]{1,0:T(8,128)(2,1)S(1)} collective-permute-done((bf16[32,1024]{1,0:T(8,128)(2,1)S(1)}, bf16[32,1024]{1,0:T(8,128)(2,1)S(1)}, u32[]{:S(2)}, u32[]{:S(2)}) %collective-permute-start.24) | collective-permute-done | bytes 65568 | tf_op jit(solution)/shard_map/ppermute | solution.py:310
  114.4 11.6 %collective-permute-done.25 = bf16[32,1024]{1,0:T(8,128)(2,1)S(1)} collective-permute-done((bf16[32,1024]{1,0:T(8,128)(2,1)S(1)}, bf16[32,1024]{1,0:T(8,128)(2,1)S(1)}, u32[]{:S(2)}, u32[]{:S(2)}) %collective-permute-start.25) | collective-permute-done | bytes 65568 | tf_op jit(solution)/shard_map/ppermute | solution.py:310
  128.7 1.6 %collective-permute-done.19.refs_11_ = bf16[256,1024]{1,0:T(8,128)(2,1)S(1)} collective-permute-done((bf16[256,1024]{1,0:T(8,128)(2,1)}, bf16[256,1024]{1,0:T(8,128)(2,1)S(1)}, u32[]{:S(2)}, u32[]{:S(2)}) %collective-permute-start.19) | collective-permute-done | bytes 524320 | tf_op jit(solution)/shard_map/ppermute | solution.py:310
  133.4 5.7 %shard_map.167 = bf16[32,32,128]{2,1,0:T(8,128)(2,1)} custom-call(bf16[128,4096]{1,0:T(8,128)(2,1)} %copy-done, bf16[256,1024]{1,0:T(8,128)(2,1)} %copy-done.8, bf16[256,1024]{1,0:T(8,128)(2,1)} %copy-done.7, bf16[256,1024]{1,0:T(8,128)(2,1)} %copy-done.13, bf16[256,1024]{1,0:T(8,128)(2,1)} %copy-done.14, bf16[256,1024]{1,0:T(8,128)(2,1)} %copy-done.11, ...), custom_call_target="tpu_custom_call" | custom-call | tf_op jit(solution)/shard_map/pallas_call | solution.py:244
  139.2 3.2 %all-to-all-start.2 = ((bf16[32,32,128]{2,1,0:T(8,128)(2,1)}), bf16[32,32,128]{2,1,0:T(8,128)(2,1)S(1)}, u32[]{:S(2)}, u32[]{:S(2)}) async-start(bf16[32,32,128]{2,1,0:T(8,128)(2,1)} %shard_map.167), calls=%async_computation.2 | async-start | bytes 524288 | tf_op jit(solution)/shard_map/all_to_all | solution.py:381
  142.4 5.3 %shard_map.166 = (bf16[128,1024]{1,0:T(8,128)(2,1)}, bf16[128,1024]{1,0:T(8,128)(2,1)}, bf16[128,1024]{1,0:T(8,128)(2,1)}) custom-call(bf16[128,128]{1,0:T(8,128)(2,1)} %fusion.23.square, bf16[32,4,32,128]{3,2,1,0:T(8,128)(2,1)} %copy-done.6, f32[128,1024]{1,0:T(8,128)} %fusion.part, bf16[1024,3072]{1,0:T(8,128)(2,1)} %w_in.3), custom_call_target="tpu_custom_call" | custom-call | tf_op jit(solution)/shard_map/pallas_call | solution.py:244
  147.7 5.0 %all-to-all-done.2.taken = bf16[32,32,128]{2,1,0:T(8,128)(2,1)S(1)} async-done(((bf16[32,32,128]{2,1,0:T(8,128)(2,1)}), bf16[32,32,128]{2,1,0:T(8,128)(2,1)S(1)}, u32[]{:S(2)}, u32[]{:S(2)}) %all-to-all-start.2) | async-done | bytes 262176 | tf_op jit(solution)/shard_map/all_to_all | solution.py:381
  (93 shorter events, 12.9 us)
Async XLA Ops:
  0.6 17.1 %collective-permute-start = (bf16[128,1024]{1,0:T(8,128)(2,1)}, bf16[128,1024]{1,0:T(8,128)(2,1)S(1)}, u32[]{:S(2)}, u32[]{:S(2)}) collective-permute-start(bf16[128,1024]{1,0:T(8,128)(2,1)} %out_cot.1), channel_id=1, source_target_pairs={{0,8},{8,0},{16,24},{24,16},{1,9},{9,1},{17,25},{25,17},{2,10},{10... | collective-permute-start | bytes 786440 | tf_op jit(solution)/shard_map/ppermute | solution.py:310
  3.6 14.1 %collective-permute-start.1 = (bf16[128,1024]{1,0:T(8,128)(2,1)}, bf16[128,1024]{1,0:T(8,128)(2,1)S(1)}, u32[]{:S(2)}, u32[]{:S(2)}) collective-permute-start(bf16[128,1024]{1,0:T(8,128)(2,1)} %out_cot.1), channel_id=1, source_target_pairs={{0,16},{8,24},{16,0},{24,8},{1,17},{9,25},{17,1},{25,9},{2,18},{10... | collective-permute-start | bytes 786440 | tf_op jit(solution)/shard_map/ppermute | solution.py:310
  5.2 12.6 %collective-permute-start.2 = (bf16[128,1024]{1,0:T(8,128)(2,1)}, bf16[128,1024]{1,0:T(8,128)(2,1)S(1)}, u32[]{:S(2)}, u32[]{:S(2)}) collective-permute-start(bf16[128,1024]{1,0:T(8,128)(2,1)} %out_cot.1), channel_id=1, source_target_pairs={{0,24},{8,16},{16,8},{24,0},{1,25},{9,17},{17,9},{25,1},{2,26},{10... | collective-permute-start | bytes 786440 | tf_op jit(solution)/shard_map/ppermute | solution.py:310
  5.2 13.2 %collective-permute-start.3 = (bf16[128,1024]{1,0:T(8,128)(2,1)}, bf16[128,1024]{1,0:T(8,128)(2,1)S(1)}, u32[]{:S(2)}, u32[]{:S(2)}) collective-permute-start(bf16[128,1024]{1,0:T(8,128)(2,1)} %block_in.1), channel_id=1, source_target_pairs={{0,2},{1,3},{2,0},{3,1},{4,6},{5,7},{6,4},{7,5},{8,10},{9,11},{10,... | collective-permute-start | bytes 786440 | tf_op jit(solution)/shard_map/ppermute | solution.py:310
  7.2 13.7 %collective-permute-start.4 = (bf16[128,1024]{1,0:T(8,128)(2,1)}, bf16[128,1024]{1,0:T(8,128)(2,1)S(1)}, u32[]{:S(2)}, u32[]{:S(2)}) collective-permute-start(bf16[128,1024]{1,0:T(8,128)(2,1)} %block_in.1), channel_id=1, source_target_pairs={{0,4},{1,5},{2,6},{3,7},{4,0},{5,1},{6,2},{7,3},{8,12},{9,13},{10,... | collective-permute-start | bytes 786440 | tf_op jit(solution)/shard_map/ppermute | solution.py:310
  20.9 57.6 %all-to-all-start = ((bf16[32,7,32,128]{3,2,1,0:T(8,128)(2,1)}), bf16[32,7,32,128]{3,2,1,0:T(8,128)(2,1)S(1)}, u32[]{:S(2)}, u32[]{:S(2)}) async-start(bf16[32,7,32,128]{3,2,1,0:T(8,128)(2,1)} %get-tuple-element.28), calls=%async_computation | async-start | bytes 3670016 | tf_op jit(solution)/shard_map/all_to_all | solution.py:381
  25.7 14.0 %collective-permute-start.5 = (bf16[256,128]{1,0:T(8,128)(2,1)S(1)}, bf16[256,128]{1,0:T(8,128)(2,1)S(1)}, u32[]{:S(2)}, u32[]{:S(2)}) collective-permute-start(bf16[256,128]{1,0:T(8,128)(2,1)S(1)} %get-tuple-element.55), channel_id=1, source_target_pairs={{0,8},{8,0},{16,24},{24,16},{1,9},{9,1},{17,25},{25,17},{2,10},{10... | collective-permute-start | bytes 196616 | tf_op jit(solution)/shard_map/ppermute | solution.py:310
  27.6 13.5 %collective-permute-start.6 = (bf16[256,128]{1,0:T(8,128)(2,1)S(1)}, bf16[256,128]{1,0:T(8,128)(2,1)S(1)}, u32[]{:S(2)}, u32[]{:S(2)}) collective-permute-start(bf16[256,128]{1,0:T(8,128)(2,1)S(1)} %get-tuple-element.54), channel_id=1, source_target_pairs={{0,16},{8,24},{16,0},{24,8},{1,17},{9,25},{17,1},{25,9},{2,18},{10... | collective-permute-start | bytes 196616 | tf_op jit(solution)/shard_map/ppermute | solution.py:310
  29.0 14.8 %collective-permute-start.7 = (bf16[256,128]{1,0:T(8,128)(2,1)S(1)}, bf16[256,128]{1,0:T(8,128)(2,1)S(1)}, u32[]{:S(2)}, u32[]{:S(2)}) collective-permute-start(bf16[256,128]{1,0:T(8,128)(2,1)S(1)} %get-tuple-element.53), channel_id=1, source_target_pairs={{0,24},{8,16},{16,8},{24,0},{1,25},{9,17},{17,9},{25,1},{2,26},{10... | collective-permute-start | bytes 196616 | tf_op jit(solution)/shard_map/ppermute | solution.py:310
  29.4 38.9 %collective-permute-start.10 = (bf16[256,1024]{1,0:T(8,128)(2,1)S(1)}, bf16[256,1024]{1,0:T(8,128)(2,1)S(1)}, u32[]{:S(2)}, u32[]{:S(2)}) collective-permute-start(bf16[256,1024]{1,0:T(8,128)(2,1)S(1)} %constant_dynamic-update-slice_fusion.refs_0_), channel_id=1, source_target_pairs={{0,16},{8,24},{16,0},{24,8},{1,17},{9,25},{17,1},{25,9},{2,18},{10... | collective-permute-start | bytes 1572872 | tf_op jit(solution)/shard_map/ppermute | solution.py:310
  31.2 37.1 %collective-permute-start.9 = (bf16[256,1024]{1,0:T(8,128)(2,1)S(1)}, bf16[256,1024]{1,0:T(8,128)(2,1)S(1)}, u32[]{:S(2)}, u32[]{:S(2)}) collective-permute-start(bf16[256,1024]{1,0:T(8,128)(2,1)S(1)} %constant_dynamic-update-slice_fusion.refs_0_), channel_id=1, source_target_pairs={{0,8},{8,0},{16,24},{24,16},{1,9},{9,1},{17,25},{25,17},{2,10},{10... | collective-permute-start | bytes 1572872 | tf_op jit(solution)/shard_map/ppermute | solution.py:310
  39.8 21.9 %collective-permute-start.11 = (bf16[128,1024]{1,0:T(8,128)(2,1)S(1)}, bf16[128,1024]{1,0:T(8,128)(2,1)S(1)}, u32[]{:S(2)}, u32[]{:S(2)}) collective-permute-start(bf16[128,1024]{1,0:T(8,128)(2,1)S(1)} %collective-permute-done.4), channel_id=1, source_target_pairs={{0,2},{1,3},{2,0},{3,1},{4,6},{5,7},{6,4},{7,5},{8,10},{9,11},{10,... | collective-permute-start | bytes 786440 | tf_op jit(solution)/shard_map/ppermute | solution.py:310
  45.4 22.8 %collective-permute-start.8 = (f32[4,32,1024]{2,1,0:T(8,128)S(1)}, f32[4,32,1024]{2,1,0:T(8,128)S(1)}, u32[]{:S(2)}, u32[]{:S(2)}) collective-permute-start(f32[4,32,1024]{2,1,0:T(8,128)S(1)} %dynamic-slice_bitcast_fusion), channel_id=1, source_target_pairs={{0,1},{1,0},{2,3},{3,2},{4,5},{5,4},{6,7},{7,6},{8,9},{9,8},{10,11... | collective-permute-start | bytes 1572872 | tf_op jit(solution)/shard_map/ppermute | solution.py:310
  61.7 64.9 %copy-start.7 = (bf16[256,1024]{1,0:T(8,128)(2,1)}, bf16[256,1024]{1,0:T(8,128)(2,1)S(1)}, u32[]{:S(2)}) copy-start(bf16[256,1024]{1,0:T(8,128)(2,1)S(1)} %constant_dynamic-update-slice_fusion.2.refs_1_) | copy-start | bytes 1572868
  61.7 15.5 %collective-permute-start.12 = (bf16[256,1024]{1,0:T(8,128)(2,1)S(1)}, bf16[256,1024]{1,0:T(8,128)(2,1)S(1)}, u32[]{:S(2)}, u32[]{:S(2)}) collective-permute-start(bf16[256,1024]{1,0:T(8,128)(2,1)S(1)} %constant_dynamic-update-slice_fusion.2.refs_1_), channel_id=1, source_target_pairs={{0,8},{8,0},{16,24},{24,16},{1,9},{9,1},{17,25},{25,17},{2,10},{10... | collective-permute-start | bytes 1572872 | tf_op jit(solution)/shard_map/ppermute | solution.py:310
  63.4 15.1 %collective-permute-start.13 = (bf16[256,1024]{1,0:T(8,128)(2,1)S(1)}, bf16[256,1024]{1,0:T(8,128)(2,1)}, u32[]{:S(2)}, u32[]{:S(2)}) collective-permute-start(bf16[256,1024]{1,0:T(8,128)(2,1)S(1)} %constant_dynamic-update-slice_fusion.2.refs_1_), channel_id=1, source_target_pairs={{0,16},{8,24},{16,0},{24,8},{1,17},{9,25},{17,1},{25,9},{2,18},{10... | collective-permute-start | bytes 1572872 | tf_op jit(solution)/shard_map/ppermute | solution.py:310
  90.8 36.2 %copy-start.9 = (bf16[256,1024]{1,0:T(8,128)(2,1)S(1)}, bf16[256,1024]{1,0:T(8,128)(2,1)}, u32[]{:S(2)}) copy-start(bf16[256,1024]{1,0:T(8,128)(2,1)} %copy-done.8) | copy-start | bytes 1572868
  90.8 48.3 %all-to-all-start.1 = ((bf16[32,4,32,128]{3,2,1,0:T(8,128)(2,1)}), bf16[32,4,32,128]{3,2,1,0:T(8,128)(2,1)S(1)}, u32[]{:S(2)}, u32[]{:S(2)}) async-start(bf16[32,4,32,128]{3,2,1,0:T(8,128)(2,1)} %get-tuple-element.36), calls=%async_computation.1 | async-start | bytes 2097152 | tf_op jit(solution)/shard_map/all_to_all | solution.py:381
  95.1 19.2 %collective-permute-start.24 = (bf16[32,1024]{1,0:T(8,128)(2,1)S(1)}, bf16[32,1024]{1,0:T(8,128)(2,1)S(1)}, u32[]{:S(2)}, u32[]{:S(2)}) collective-permute-start(bf16[32,1024]{1,0:T(8,128)(2,1)S(1)} %get-tuple-element.49), channel_id=1, source_target_pairs={{0,2},{1,3},{2,0},{3,1},{4,6},{5,7},{6,4},{7,5},{8,10},{9,11},{10,... | collective-permute-start | bytes 196616 | tf_op jit(solution)/shard_map/ppermute | solution.py:310
  97.0 29.0 %collective-permute-start.25 = (bf16[32,1024]{1,0:T(8,128)(2,1)S(1)}, bf16[32,1024]{1,0:T(8,128)(2,1)S(1)}, u32[]{:S(2)}, u32[]{:S(2)}) collective-permute-start(bf16[32,1024]{1,0:T(8,128)(2,1)S(1)} %get-tuple-element.51), channel_id=1, source_target_pairs={{0,4},{1,5},{2,6},{3,7},{4,0},{5,1},{6,2},{7,3},{8,12},{9,13},{10,... | collective-permute-start | bytes 196616 | tf_op jit(solution)/shard_map/ppermute | solution.py:310
  99.4 26.6 %collective-permute-start.26 = (bf16[32,1024]{1,0:T(8,128)(2,1)S(1)}, bf16[32,1024]{1,0:T(8,128)(2,1)S(1)}, u32[]{:S(2)}, u32[]{:S(2)}) collective-permute-start(bf16[32,1024]{1,0:T(8,128)(2,1)S(1)} %get-tuple-element.50), channel_id=1, source_target_pairs={{0,6},{1,7},{2,4},{3,5},{4,2},{5,3},{6,0},{7,1},{8,14},{9,15},{10,... | collective-permute-start | bytes 196616 | tf_op jit(solution)/shard_map/ppermute | solution.py:310
  99.6 26.9 %collective-permute-start.15 = (bf16[256,1024]{1,0:T(8,128)(2,1)}, bf16[256,1024]{1,0:T(8,128)(2,1)}, u32[]{:S(2)}, u32[]{:S(2)}) collective-permute-start(bf16[256,1024]{1,0:T(8,128)(2,1)} %collective-permute-done.13.refs_5_), channel_id=1, source_target_pairs={{0,8},{8,0},{16,24},{24,16},{1,9},{9,1},{17,25},{25,17},{2,10},{10... | collective-permute-start | bytes 1572872 | tf_op jit(solution)/shard_map/ppermute | solution.py:310
  101.3 25.2 %collective-permute-start.14 = (bf16[256,1024]{1,0:T(8,128)(2,1)}, bf16[256,1024]{1,0:T(8,128)(2,1)}, u32[]{:S(2)}, u32[]{:S(2)}) collective-permute-start(bf16[256,1024]{1,0:T(8,128)(2,1)} %copy-done.13), channel_id=1, source_target_pairs={{0,16},{8,24},{16,0},{24,8},{1,17},{9,25},{17,1},{25,9},{2,18},{10... | collective-permute-start | bytes 1572872 | tf_op jit(solution)/shard_map/ppermute | solution.py:310
  114.4 12.7 %collective-permute-start.21 = (bf16[256,1024]{1,0:T(8,128)(2,1)}, bf16[256,1024]{1,0:T(8,128)(2,1)S(1)}, u32[]{:S(2)}, u32[]{:S(2)}) collective-permute-start(bf16[256,1024]{1,0:T(8,128)(2,1)} %collective-permute-done.13.refs_5_), channel_id=1, source_target_pairs={{0,1},{1,0},{2,3},{3,2},{4,5},{5,4},{6,7},{7,6},{8,9},{9,8},{10,11... | collective-permute-start | bytes 1572872 | tf_op jit(solution)/shard_map/ppermute | solution.py:310
  126.0 1.9 %collective-permute-start.20 = (bf16[256,1024]{1,0:T(8,128)(2,1)S(1)}, bf16[256,1024]{1,0:T(8,128)(2,1)S(1)}, u32[]{:S(2)}, u32[]{:S(2)}) collective-permute-start(bf16[256,1024]{1,0:T(8,128)(2,1)S(1)} %copy-done.12), channel_id=1, source_target_pairs={{0,1},{1,0},{2,3},{3,2},{4,5},{5,4},{6,7},{7,6},{8,9},{9,8},{10,11... | collective-permute-start | bytes 1572872 | tf_op jit(solution)/shard_map/ppermute | solution.py:310
  126.0 4.3 %collective-permute-start.19 = (bf16[256,1024]{1,0:T(8,128)(2,1)}, bf16[256,1024]{1,0:T(8,128)(2,1)S(1)}, u32[]{:S(2)}, u32[]{:S(2)}) collective-permute-start(bf16[256,1024]{1,0:T(8,128)(2,1)} %copy-done.14), channel_id=1, source_target_pairs={{0,1},{1,0},{2,3},{3,2},{4,5},{5,4},{6,7},{7,6},{8,9},{9,8},{10,11... | collective-permute-start | bytes 1572872 | tf_op jit(solution)/shard_map/ppermute | solution.py:310
  126.5 5.5 %collective-permute-start.18 = (bf16[256,1024]{1,0:T(8,128)(2,1)}, bf16[256,1024]{1,0:T(8,128)(2,1)}, u32[]{:S(2)}, u32[]{:S(2)}) collective-permute-start(bf16[256,1024]{1,0:T(8,128)(2,1)} %copy-done.13), channel_id=1, source_target_pairs={{0,1},{1,0},{2,3},{3,2},{4,5},{5,4},{6,7},{7,6},{8,9},{9,8},{10,11... | collective-permute-start | bytes 1572872 | tf_op jit(solution)/shard_map/ppermute | solution.py:310
  126.6 5.4 %collective-permute-start.17 = (bf16[256,1024]{1,0:T(8,128)(2,1)S(1)}, bf16[256,1024]{1,0:T(8,128)(2,1)}, u32[]{:S(2)}, u32[]{:S(2)}) collective-permute-start(bf16[256,1024]{1,0:T(8,128)(2,1)S(1)} %constant_dynamic-update-slice_fusion.2.refs_1_), channel_id=1, source_target_pairs={{0,1},{1,0},{2,3},{3,2},{4,5},{5,4},{6,7},{7,6},{8,9},{9,8},{10,11... | collective-permute-start | bytes 1572872 | tf_op jit(solution)/shard_map/ppermute | solution.py:310
  127.0 4.9 %collective-permute-start.16 = (bf16[256,1024]{1,0:T(8,128)(2,1)S(1)}, bf16[256,1024]{1,0:T(8,128)(2,1)}, u32[]{:S(2)}, u32[]{:S(2)}) collective-permute-start(bf16[256,1024]{1,0:T(8,128)(2,1)S(1)} %copy-done.9), channel_id=1, source_target_pairs={{0,1},{1,0},{2,3},{3,2},{4,5},{5,4},{6,7},{7,6},{8,9},{9,8},{10,11... | collective-permute-start | bytes 1572872 | tf_op jit(solution)/shard_map/ppermute | solution.py:310
  127.9 4.1 %collective-permute-start.23 = (bf16[256,1024]{1,0:T(8,128)(2,1)}, bf16[256,1024]{1,0:T(8,128)(2,1)S(1)}, u32[]{:S(2)}, u32[]{:S(2)}) collective-permute-start(bf16[256,1024]{1,0:T(8,128)(2,1)} %collective-permute-done.15.refs_7_), channel_id=1, source_target_pairs={{0,1},{1,0},{2,3},{3,2},{4,5},{5,4},{6,7},{7,6},{8,9},{9,8},{10,11... | collective-permute-start | bytes 1572872 | tf_op jit(solution)/shard_map/ppermute | solution.py:310
  131.1 2.3 %collective-permute-start.22 = (bf16[256,1024]{1,0:T(8,128)(2,1)}, bf16[256,1024]{1,0:T(8,128)(2,1)}, u32[]{:S(2)}, u32[]{:S(2)}) collective-permute-start(bf16[256,1024]{1,0:T(8,128)(2,1)} %collective-permute-done.14.refs_6_), channel_id=1, source_target_pairs={{0,1},{1,0},{2,3},{3,2},{4,5},{5,4},{6,7},{7,6},{8,9},{9,8},{10,11... | collective-permute-start | bytes 1572872 | tf_op jit(solution)/shard_map/ppermute | solution.py:310
  139.2 13.6 %all-to-all-start.2 = ((bf16[32,32,128]{2,1,0:T(8,128)(2,1)}), bf16[32,32,128]{2,1,0:T(8,128)(2,1)S(1)}, u32[]{:S(2)}, u32[]{:S(2)}) async-start(bf16[32,32,128]{2,1,0:T(8,128)(2,1)} %shard_map.167), calls=%async_computation.2 | async-start | bytes 524288 | tf_op jit(solution)/shard_map/all_to_all | solution.py:381
  (22 other events, 208.2 us)

commit v3 on v2

--- a/solution.py
+++ b/solution.py
@@ -314,20 +314,20 @@
     return lax.optimization_barrier((x, *others))[0]
 
 
-def near_chips(block):
-    bits = bits_of(lax.axis_size("minor"))[1:]
-    blocks = [block] + [None] * (2 ** len(bits) - 1)
-    for bit in bits:
-        blocks[bit // 2] = swap(block, "minor", bit)
+def chips_of(block):
+    blocks = [block] + [None] * (lax.axis_size("minor") // 2 - 1)
+    for j in range(len(blocks) - 1, 0, -1):
+        if j & (j - 1) == 0:
+            blocks[j] = swap(block, "minor", 2 * j)
     return blocks
 
 
 def far_chips(blocks, later):
-    blocks = [block if block is None else after(block, later) for block in blocks]
+    blocks = list(blocks)
     for j in range(1, len(blocks)):
         low = j & -j
         if j != low:
-            blocks[j] = swap(blocks[j ^ low], "minor", 2 * low)
+            blocks[j] = swap(after(blocks[j ^ low], later), "minor", 2 * low)
     return blocks
 
 
@@ -335,9 +335,11 @@
     half = max(len(blocks) // 2, 1)
     lines = []
     for part in (blocks[:half], blocks[half:]):
-        held = [jnp.concatenate(part)] + [None] * (lax.axis_size("major") - 1)
-        for bit in bits_of(lax.axis_size("major")):
-            held[bit] = swap(held[0], "major", bit)
+        whole = jnp.concatenate(part)
+        held = [whole] + [None] * (lax.axis_size("major") - 1)
+        for j in range(1, len(held)):
+            if j & (j - 1) == 0:
+                held[j] = swap(whole, "major", j)
         lines.append(held)
     return lines
 
@@ -368,13 +370,10 @@
     return part(mine) + swap(part(1 - mine), "minor", 1)
 
 
-def out_sum(total):
+def out_parts(total):
     mine = lax.axis_index("minor") // 2
     part = lambda chip: lax.dynamic_index_in_dim(total, chip, 0, keepdims=False)
-    sums = part(mine)
-    for j in range(1, total.shape[0]):
-        sums += swap(part(mine ^ j).astype(jnp.bfloat16), "minor", 2 * j).astype(jnp.float32)
-    return sums
+    return [part(mine)] + [swap(part(mine ^ j).astype(jnp.bfloat16), "minor", 2 * j) for j in range(1, total.shape[0])]
 
 
 def regroup(x):
@@ -390,7 +389,7 @@
     field = lambda *dims: jax.ShapeDtypeStruct((devices, *dims, group, rows_dev), jnp.bfloat16)
     array = lambda *dims: jax.ShapeDtypeStruct(dims, jnp.bfloat16)
 
-    near_in = near_chips(block_in)
+    near_in = chips_of(block_in)
     square = jnp.eye(rows_dev, dtype=jnp.bfloat16)
     sent, second_out, late = on_chip(
         begin_kernel,
@@ -406,11 +405,12 @@
         60,
     )
     cots = [swap(out_cot, "major", j) if j else out_cot for j in range(majors)]
-    sent = after(sent, *cots, *[block for block in near_in if block is not None])
+    near_in = far_chips(near_in, late)
+    sent = after(sent, *cots, *near_in)
     here = regroup(sent)
     total = out_part(after(second_out, sent), cots)
     late = lax.dot_general(late, w_in[:, 2 * width :], LAST, preferred_element_type=jnp.float32)
-    lines = major_near(far_chips(near_in, sent))
+    lines = major_near([after(block, sent) for block in near_in])
     here = after(here, late, total, *[piece for line in lines for piece in line if piece is not None])
 
     spec = pltpu.VMEM((devices * group, 2 * rows_dev), jnp.float32)
@@ -420,10 +420,12 @@
         (lax.axis_index(AXES).astype(jnp.int32)[None], here, *tables(devices, rows_dev)),
         [pltpu.VMEM((devices * group, rows_dev), jnp.float32), spec, spec, spec],
     )
+    all_in = gather_chips(lines, here)
+    parts = out_parts(after(total, *[piece for piece in lines[0] if piece is not None]))
+    back, *parts = lax.optimization_barrier((back, *parts, *all_in))[: 1 + len(parts)]
+    w_out_grad = sum(part.astype(jnp.float32) for part in parts) * scale
     home = regroup(back)
-    all_in = gather_chips(lines, back)
-    all_in += [swap(piece, "minor", 1) for piece in all_in]
-    w_out_grad = out_sum(after(total, back)) * scale
+    all_in += [swap(after(piece, back), "minor", 1) for piece in all_in]
 
     rows = all_in[0].shape[0]
     slots = min(len(all_in), 16 * 2**20 // (2 * rows * width))
@@ -435,7 +437,7 @@
         range(1, 1 + len(all_in)),
         60,
     )
-    taken = regroup(after(part, home, w_out_grad))
+    taken = regroup(after(part, home))
     in_grad, filter_one_grad, filter_two_grad = on_chip(
         home_kernel,
         [array(rows_dev, width)] * 3,

time: 155 us -> 146 us (0.942)
  waiting for transfers between devices: 71.1 us -> 63.9 us
  starting transfers between devices: 41.4 us -> 38.7 us
    ppermute x27, waiting for transfers between devices: 66 us -> 47.1 us  [swap(): lax.ppermute(block, axis, [(i, i ^ bit) for i in range(lax.axis_size(axis...]
    all_to_all x3, waiting for transfers between devices: 5.03 us -> 16.7 us  [regroup(): return lax.all_to_all(x, AXES, split_axis=0, concat_axis=0, tiled=True)]
    ppermute x27, starting transfers between devices: 29.3 us -> 26 us  [swap(): lax.ppermute(block, axis, [(i, i ^ bit) for i in range(lax.axis_size(axis...]
    unnamed x50 -> x62, local copies, waits for them, and re-layouts: 3.37 us -> 3.29 us
  transfers between devices with their start and end apart: 30 -> 30, of which waited for: 14 -> 16; matrix products, arithmetic and copies ran while one was open for 4% -> 5% of each run, Pallas kernels for 12% -> 20%
where the time goes in v3:
time: 146 us; the launch traced here: 145 us
  waiting for transfers between devices  63.9 us (44%)
  starting transfers between devices  38.7 us (27%)
  Pallas kernels  31 us (21%)
  matrix products  4.8 us (3%)
  local copies, waits for them, and re-layouts  3.44 us (2%)
  other arithmetic  2.27 us (2%)
    ppermute x27, waiting for transfers between devices, swap(): lax.ppermute(block, axis, [(i, i ^ bit) for i in range(lax.axis_size(axis...  47.1 us
    pallas_call x5, Pallas kernels, on_chip(): pl.pallas_call(kernel, out_shape=out_shape, in_specs=[pl.BlockSpec(memory...  31 us
    ppermute x27, starting transfers between devices, swap(): lax.ppermute(block, axis, [(i, i ^ bit) for i in range(lax.axis_size(axis...  26 us
    all_to_all x3, waiting for transfers between devices, regroup(): return lax.all_to_all(x, AXES, split_axis=0, concat_axis=0, tiled=True)  16.7 us
    all_to_all x3, starting transfers between devices, regroup(): return lax.all_to_all(x, AXES, split_axis=0, concat_axis=0, tiled=True)  12.8 us
    unnamed x62, local copies, waits for them, and re-layouts  3.29 us
    dot_general x1, matrix products, shards(): lax.dot_general(late, w_in[:, 2 * width:], LAST, preferred_element_type=j...  3.21 us
  transfers between devices with their start and end apart: 30, of which 16 were waited for; matrix products, arithmetic and copies ran while one was open for 5% of the time, Pallas kernels for 20%

profile of v3, /device:TPU:0, one launch (start us, length us, event | category | flops | bytes accessed | tf_op | source)
XLA Modules:
  0.0 145.1 jit_solution(13745858777953030266)
XLA Ops:
  0.6 4.1 %collective-permute-start.4 = (bf16[128,1024]{1,0:T(8,128)(2,1)}, bf16[128,1024]{1,0:T(8,128)(2,1)S(1)}, u32[]{:S(2)}, u32[]{:S(2)}) collective-permute-start(bf16[128,1024]{1,0:T(8,128)(2,1)} %block_in.1), channel_id=1, source_target_pairs={{0,4},{1,5},{2,6},{3,7},{4,0},{5,1},{6,2},{7,3},{8,12},{9,13},{10,... | collective-permute-start | bytes 786440 | tf_op jit(solution)/shard_map/ppermute | solution.py:310
  4.7 1.5 %collective-permute-start = (bf16[128,1024]{1,0:T(8,128)(2,1)}, bf16[128,1024]{1,0:T(8,128)(2,1)S(1)}, u32[]{:S(2)}, u32[]{:S(2)}) collective-permute-start(bf16[128,1024]{1,0:T(8,128)(2,1)} %out_cot.1), channel_id=1, source_target_pairs={{0,8},{8,0},{16,24},{24,16},{1,9},{9,1},{17,25},{25,17},{2,10},{10... | collective-permute-start | bytes 786440 | tf_op jit(solution)/shard_map/ppermute | solution.py:310
  6.2 1.5 %collective-permute-start.1 = (bf16[128,1024]{1,0:T(8,128)(2,1)}, bf16[128,1024]{1,0:T(8,128)(2,1)S(1)}, u32[]{:S(2)}, u32[]{:S(2)}) collective-permute-start(bf16[128,1024]{1,0:T(8,128)(2,1)} %out_cot.1), channel_id=1, source_target_pairs={{0,16},{8,24},{16,0},{24,8},{1,17},{9,25},{17,1},{25,9},{2,18},{10... | collective-permute-start | bytes 786440 | tf_op jit(solution)/shard_map/ppermute | solution.py:310
  8.2 1.6 %collective-permute-start.3 = (bf16[128,1024]{1,0:T(8,128)(2,1)}, bf16[128,1024]{1,0:T(8,128)(2,1)S(1)}, u32[]{:S(2)}, u32[]{:S(2)}) collective-permute-start(bf16[128,1024]{1,0:T(8,128)(2,1)} %block_in.1), channel_id=1, source_target_pairs={{0,2},{1,3},{2,0},{3,1},{4,6},{5,7},{6,4},{7,5},{8,10},{9,11},{10,... | collective-permute-start | bytes 786440 | tf_op jit(solution)/shard_map/ppermute | solution.py:310
  10.4 7.3 %shard_map.164 = (bf16[32,7,32,128]{3,2,1,0:T(8,128)(2,1)}, bf16[1024,128]{1,0:T(8,128)(2,1)}, bf16[128,1024]{1,0:T(8,128)(2,1)}) custom-call(bf16[128,128]{1,0:T(8,128)(2,1)} %fusion.20.square, bf16[128,1024]{1,0:T(8,128)(2,1)} %conv_one.1, bf16[128,1024]{1,0:T(8,128)(2,1)} %filter_two.1, bf16[128,1024]{1,0:T(8,128)(2,1)} %filter_one.1, ...), custom_call_target="tpu_custom_call" | custom-call | tf_op jit(solution)/shard_map/pallas_call | solution.py:244
  18.2 1.3 collective-permute-done.1
  20.7 4.7 %collective-permute-done.5 = bf16[128,1024]{1,0:T(8,128)(2,1)S(1)} collective-permute-done((bf16[128,1024]{1,0:T(8,128)(2,1)S(1)}, bf16[128,1024]{1,0:T(8,128)(2,1)S(1)}, u32[]{:S(2)}, u32[]{:S(2)}) %collective-permute-start.5) | collective-permute-done | bytes 262176 | tf_op jit(solution)/shard_map/ppermute | solution.py:310
  25.4 5.5 %all-to-all-start = ((bf16[32,7,32,128]{3,2,1,0:T(8,128)(2,1)}), bf16[32,7,32,128]{3,2,1,0:T(8,128)(2,1)S(1)}, u32[]{:S(2)}, u32[]{:S(2)}) async-start(bf16[32,7,32,128]{3,2,1,0:T(8,128)(2,1)} %get-tuple-element.45), calls=%async_computation | async-start | bytes 3670016 | tf_op jit(solution)/shard_map/all_to_all | solution.py:380
  31.0 1.8 %collective-permute-start.6 = (bf16[256,128]{1,0:T(8,128)(2,1)S(1)}, bf16[256,128]{1,0:T(8,128)(2,1)S(1)}, u32[]{:S(2)}, u32[]{:S(2)}) collective-permute-start(bf16[256,128]{1,0:T(8,128)(2,1)S(1)} %get-tuple-element.85), channel_id=1, source_target_pairs={{0,8},{8,0},{16,24},{24,16},{1,9},{9,1},{17,25},{25,17},{2,10},{10... | collective-permute-start | bytes 196616 | tf_op jit(solution)/shard_map/ppermute | solution.py:310
  32.9 1.5 %collective-permute-start.7 = (bf16[256,128]{1,0:T(8,128)(2,1)S(1)}, bf16[256,128]{1,0:T(8,128)(2,1)S(1)}, u32[]{:S(2)}, u32[]{:S(2)}) collective-permute-start(bf16[256,128]{1,0:T(8,128)(2,1)S(1)} %get-tuple-element.84), channel_id=1, source_target_pairs={{0,16},{8,24},{16,0},{24,8},{1,17},{9,25},{17,1},{25,9},{2,18},{10... | collective-permute-start | bytes 196616 | tf_op jit(solution)/shard_map/ppermute | solution.py:310
  34.7 1.8 %collective-permute-start.12 = (bf16[256,1024]{1,0:T(8,128)(2,1)S(1)}, bf16[256,1024]{1,0:T(8,128)(2,1)S(1)}, u32[]{:S(2)}, u32[]{:S(2)}) collective-permute-start(bf16[256,1024]{1,0:T(8,128)(2,1)S(1)} %constant_dynamic-update-slice_fusion.2.refs_1_), channel_id=1, source_target_pairs={{0,8},{8,0},{16,24},{24,16},{1,9},{9,1},{17,25},{25,17},{2,10},{10... | collective-permute-start | bytes 1572872 | tf_op jit(solution)/shard_map/ppermute | solution.py:310
  36.5 1.5 %collective-permute-start.13 = (bf16[256,1024]{1,0:T(8,128)(2,1)S(1)}, bf16[256,1024]{1,0:T(8,128)(2,1)S(1)}, u32[]{:S(2)}, u32[]{:S(2)}) collective-permute-start(bf16[256,1024]{1,0:T(8,128)(2,1)S(1)} %constant_dynamic-update-slice_fusion.2.refs_1_), channel_id=1, source_target_pairs={{0,16},{8,24},{16,0},{24,8},{1,17},{9,25},{17,1},{25,9},{2,18},{10... | collective-permute-start | bytes 1572872 | tf_op jit(solution)/shard_map/ppermute | solution.py:310
  38.0 7.1 %collective-permute-done.6 = bf16[256,128]{1,0:T(8,128)(2,1)S(1)} collective-permute-done((bf16[256,128]{1,0:T(8,128)(2,1)S(1)}, bf16[256,128]{1,0:T(8,128)(2,1)S(1)}, u32[]{:S(2)}, u32[]{:S(2)}) %collective-permute-start.6) | collective-permute-done | bytes 65568 | tf_op jit(solution)/shard_map/ppermute | solution.py:310
  45.0 1.3 collective-permute-done.7
  46.4 2.7 %collective-permute-done.8 = bf16[256,128]{1,0:T(8,128)(2,1)S(1)} collective-permute-done((bf16[256,128]{1,0:T(8,128)(2,1)S(1)}, bf16[256,128]{1,0:T(8,128)(2,1)S(1)}, u32[]{:S(2)}, u32[]{:S(2)}) %collective-permute-start.8) | collective-permute-done | bytes 65568 | tf_op jit(solution)/shard_map/ppermute | solution.py:310
  49.1 1.6 %fusion.2 = f32[256,1024,1]{1,0,2:T(8,128)S(1)} fusion(bf16[1,128,1024]{2,1,0:T(8,128)(2,1)} %bitcast.37, bf16[1,128,1024]{2,1,0:T(8,128)(2,1)} %bitcast.36, bf16[1,128,1024]{2,1,0:T(8,128)(2,1)} %bitcast.35, bf16[1,128,1024]{2,1,0:T(8,128)(2,1)S(1)} %bitcast.33, bf16[1,256,128]{2,1,0:T(8,128)(2,1)S(1)} %bitcast.40, bf16[1,256,128]{2,1,0:T(8,128)(2,1)S(1)} %bitcast.39, ...), kind=kOutput, calls=%fused_computation.2 | convolution fusion | flops 270401536 | bytes 2359296 | tf_op jit(solution)/shard_map/mct,mtw->cw/dot_general | solution.py:366
  51.9 3.2 %fusion.part = f32[128,1024]{1,0:T(8,128)} fusion(bf16[128,1024]{1,0:T(8,128)(2,1)S(1)} %copy-done.26, bf16[1024,3072]{1,0:T(8,128)(2,1)} %w_in.3), kind=kOutput, calls=%fused_computation | convolution fusion | flops 268435456 | bytes 2883584 | tf_op jit(solution)/shard_map/dot_general | solution.py:412
  55.2 9.6 %collective-permute-done.12.refs_3_ = bf16[256,1024]{1,0:T(8,128)(2,1)S(1)} collective-permute-done((bf16[256,1024]{1,0:T(8,128)(2,1)S(1)}, bf16[256,1024]{1,0:T(8,128)(2,1)S(1)}, u32[]{:S(2)}, u32[]{:S(2)}) %collective-permute-start.12) | collective-permute-done | bytes 524320 | tf_op jit(solution)/shard_map/ppermute | solution.py:310
  65.1 13.9 %collective-permute-done.10.refs_2_ = bf16[256,1024]{1,0:T(8,128)(2,1)S(1)} collective-permute-done((bf16[256,1024]{1,0:T(8,128)(2,1)S(1)}, bf16[256,1024]{1,0:T(8,128)(2,1)S(1)}, u32[]{:S(2)}, u32[]{:S(2)}) %collective-permute-start.10) | collective-permute-done | bytes 524320 | tf_op jit(solution)/shard_map/ppermute | solution.py:310
  80.3 1.3 collective-permute-start.17
  81.6 1.5 %collective-permute-start.14 = (bf16[32,1024]{1,0:T(8,128)(2,1)S(1)}, bf16[32,1024]{1,0:T(8,128)(2,1)}, u32[]{:S(2)}, u32[]{:S(2)}) collective-permute-start(bf16[32,1024]{1,0:T(8,128)(2,1)S(1)} %get-tuple-element.81), channel_id=1, source_target_pairs={{0,2},{1,3},{2,0},{3,1},{4,6},{5,7},{6,4},{7,5},{8,10},{9,11},{10,... | collective-permute-start | bytes 196616 | tf_op jit(solution)/shard_map/ppermute | solution.py:310
  83.2 2.6 %collective-permute-start.15 = (bf16[32,1024]{1,0:T(8,128)(2,1)S(1)}, bf16[32,1024]{1,0:T(8,128)(2,1)}, u32[]{:S(2)}, u32[]{:S(2)}) collective-permute-start(bf16[32,1024]{1,0:T(8,128)(2,1)S(1)} %get-tuple-element.80), channel_id=1, source_target_pairs={{0,4},{1,5},{2,6},{3,7},{4,0},{5,1},{6,2},{7,3},{8,12},{9,13},{10,... | collective-permute-start | bytes 196616 | tf_op jit(solution)/shard_map/ppermute | solution.py:310
  86.2 11.2 %shard_map.165 = (bf16[32,4,32,128]{3,2,1,0:T(8,128)(2,1)}, bf16[128,4096]{1,0:T(8,128)(2,1)S(1)}) custom-call(s32[1]{0:T(128)} %bitcast.me, bf16[32,7,32,128]{3,2,1,0:T(8,128)(2,1)S(1)} %all-to-all-done.here, bf16[256,256]{1,0:T(8,128)(2,1)S(1)} %copy-done.2, bf16[256,256]{1,0:T(8,128)(2,1)S(1)} %copy-done.3, f32[256,128]{1,0:T(8,128)S(1)} %copy-done.4, ...), custom_call_target="tpu_custom_call" | custom-call | tf_op jit(solution)/shard_map/pallas_call | solution.py:244
  98.4 4.7 %all-to-all-start.1 = ((bf16[32,4,32,128]{3,2,1,0:T(8,128)(2,1)}), bf16[32,4,32,128]{3,2,1,0:T(8,128)(2,1)S(1)}, u32[]{:S(2)}, u32[]{:S(2)}) async-start(bf16[32,4,32,128]{3,2,1,0:T(8,128)(2,1)} %get-tuple-element.61), calls=%async_computation.1 | async-start | bytes 2097152 | tf_op jit(solution)/shard_map/all_to_all | solution.py:380
  108.3 1.5 %collective-permute-done.21.refs_10_ = bf16[256,1024]{1,0:T(8,128)(2,1)S(1)} collective-permute-done((bf16[256,1024]{1,0:T(8,128)(2,1)}, bf16[256,1024]{1,0:T(8,128)(2,1)S(1)}, u32[]{:S(2)}, u32[]{:S(2)}) %collective-permute-start.21) | collective-permute-done | bytes 524320 | tf_op jit(solution)/shard_map/ppermute | solution.py:310
  111.7 5.7 %shard_map.167 = bf16[32,32,128]{2,1,0:T(8,128)(2,1)} custom-call(bf16[128,4096]{1,0:T(8,128)(2,1)} %copy-done, bf16[256,1024]{1,0:T(8,128)(2,1)} %copy-done.8, bf16[256,1024]{1,0:T(8,128)(2,1)} %copy-done.7, bf16[256,1024]{1,0:T(8,128)(2,1)} %copy-done.15, bf16[256,1024]{1,0:T(8,128)(2,1)} %copy-done.11, bf16[256,1024]{1,0:T(8,128)(2,1)} %collective-permute-done.11.refs_4_, ...), custom_call_target="tpu_custom_call" | custom-call | tf_op jit(solution)/shard_map/pallas_call | solution.py:244
  117.4 13.3 %all-to-all-done.1.home = bf16[32,4,32,128]{3,2,1,0:T(8,128)(2,1)S(1)} async-done(((bf16[32,4,32,128]{3,2,1,0:T(8,128)(2,1)}), bf16[32,4,32,128]{3,2,1,0:T(8,128)(2,1)S(1)}, u32[]{:S(2)}, u32[]{:S(2)}) %all-to-all-start.1) | async-done | bytes 1048608 | tf_op jit(solution)/shard_map/all_to_all | solution.py:380
  130.7 2.6 %all-to-all-start.2 = ((bf16[32,32,128]{2,1,0:T(8,128)(2,1)}), bf16[32,32,128]{2,1,0:T(8,128)(2,1)S(1)}, u32[]{:S(2)}, u32[]{:S(2)}) async-start(bf16[32,32,128]{2,1,0:T(8,128)(2,1)} %shard_map.167), calls=%async_computation.2 | async-start | bytes 524288 | tf_op jit(solution)/shard_map/all_to_all | solution.py:380
  133.3 1.6 %add_multiply_fusion = f32[32,1024]{1,0:T(8,128)} fusion(bf16[32,1024]{1,0:T(8,128)(2,1)} %collective-permute-done.16, bf16[32,1024]{1,0:T(8,128)(2,1)} %collective-permute-done.15, f32[32,1024]{1,0:T(8,128)S(1)} %dynamic-slice_bitcast_fusion.1, bf16[32,1024]{1,0:T(8,128)(2,1)} %collective-permute-done.14), kind=kLoop, calls=%fused_computation.19 | loop fusion | flops 229376 | bytes 458752 | tf_op jit(solution)/shard_map/mul | solution.py:426
  134.9 5.3 %shard_map.166 = (bf16[128,1024]{1,0:T(8,128)(2,1)}, bf16[128,1024]{1,0:T(8,128)(2,1)}, bf16[128,1024]{1,0:T(8,128)(2,1)}) custom-call(bf16[128,128]{1,0:T(8,128)(2,1)} %fusion.20.square, bf16[32,4,32,128]{3,2,1,0:T(8,128)(2,1)} %copy-done.6, f32[128,1024]{1,0:T(8,128)} %fusion.part, bf16[1024,3072]{1,0:T(8,128)(2,1)} %w_in.3), custom_call_target="tpu_custom_call" | custom-call | tf_op jit(solution)/shard_map/pallas_call | solution.py:244
  140.2 3.4 %all-to-all-done.2.taken = bf16[32,32,128]{2,1,0:T(8,128)(2,1)S(1)} async-done(((bf16[32,32,128]{2,1,0:T(8,128)(2,1)}), bf16[32,32,128]{2,1,0:T(8,128)(2,1)S(1)}, u32[]{:S(2)}, u32[]{:S(2)}) %all-to-all-start.2) | async-done | bytes 262176 | tf_op jit(solution)/shard_map/all_to_all | solution.py:380
  143.7 1.4 shard_map.168
  (106 shorter events, 14.4 us)
Async XLA Ops:
  0.6 17.1 %collective-permute-start.4 = (bf16[128,1024]{1,0:T(8,128)(2,1)}, bf16[128,1024]{1,0:T(8,128)(2,1)S(1)}, u32[]{:S(2)}, u32[]{:S(2)}) collective-permute-start(bf16[128,1024]{1,0:T(8,128)(2,1)} %block_in.1), channel_id=1, source_target_pairs={{0,4},{1,5},{2,6},{3,7},{4,0},{5,1},{6,2},{7,3},{8,12},{9,13},{10,... | collective-permute-start | bytes 786440 | tf_op jit(solution)/shard_map/ppermute | solution.py:310
  4.7 13.5 %collective-permute-start = (bf16[128,1024]{1,0:T(8,128)(2,1)}, bf16[128,1024]{1,0:T(8,128)(2,1)S(1)}, u32[]{:S(2)}, u32[]{:S(2)}) collective-permute-start(bf16[128,1024]{1,0:T(8,128)(2,1)} %out_cot.1), channel_id=1, source_target_pairs={{0,8},{8,0},{16,24},{24,16},{1,9},{9,1},{17,25},{25,17},{2,10},{10... | collective-permute-start | bytes 786440 | tf_op jit(solution)/shard_map/ppermute | solution.py:310
  6.2 13.3 %collective-permute-start.1 = (bf16[128,1024]{1,0:T(8,128)(2,1)}, bf16[128,1024]{1,0:T(8,128)(2,1)S(1)}, u32[]{:S(2)}, u32[]{:S(2)}) collective-permute-start(bf16[128,1024]{1,0:T(8,128)(2,1)} %out_cot.1), channel_id=1, source_target_pairs={{0,16},{8,24},{16,0},{24,8},{1,17},{9,25},{17,1},{25,9},{2,18},{10... | collective-permute-start | bytes 786440 | tf_op jit(solution)/shard_map/ppermute | solution.py:310
  7.7 11.8 %collective-permute-start.2 = (bf16[128,1024]{1,0:T(8,128)(2,1)}, bf16[128,1024]{1,0:T(8,128)(2,1)S(1)}, u32[]{:S(2)}, u32[]{:S(2)}) collective-permute-start(bf16[128,1024]{1,0:T(8,128)(2,1)} %out_cot.1), channel_id=1, source_target_pairs={{0,24},{8,16},{16,8},{24,0},{1,25},{9,17},{17,9},{25,1},{2,26},{10... | collective-permute-start | bytes 786440 | tf_op jit(solution)/shard_map/ppermute | solution.py:310
  8.2 12.5 %collective-permute-start.3 = (bf16[128,1024]{1,0:T(8,128)(2,1)}, bf16[128,1024]{1,0:T(8,128)(2,1)S(1)}, u32[]{:S(2)}, u32[]{:S(2)}) collective-permute-start(bf16[128,1024]{1,0:T(8,128)(2,1)} %block_in.1), channel_id=1, source_target_pairs={{0,2},{1,3},{2,0},{3,1},{4,6},{5,7},{6,4},{7,5},{8,10},{9,11},{10,... | collective-permute-start | bytes 786440 | tf_op jit(solution)/shard_map/ppermute | solution.py:310
  17.7 7.7 %collective-permute-start.5 = (bf16[128,1024]{1,0:T(8,128)(2,1)S(1)}, bf16[128,1024]{1,0:T(8,128)(2,1)S(1)}, u32[]{:S(2)}, u32[]{:S(2)}) collective-permute-start(bf16[128,1024]{1,0:T(8,128)(2,1)S(1)} %collective-permute-done.4), channel_id=1, source_target_pairs={{0,2},{1,3},{2,0},{3,1},{4,6},{5,7},{6,4},{7,5},{8,10},{9,11},{10,... | collective-permute-start | bytes 786440 | tf_op jit(solution)/shard_map/ppermute | solution.py:310
  25.4 54.3 %all-to-all-start = ((bf16[32,7,32,128]{3,2,1,0:T(8,128)(2,1)}), bf16[32,7,32,128]{3,2,1,0:T(8,128)(2,1)S(1)}, u32[]{:S(2)}, u32[]{:S(2)}) async-start(bf16[32,7,32,128]{3,2,1,0:T(8,128)(2,1)} %get-tuple-element.45), calls=%async_computation | async-start | bytes 3670016 | tf_op jit(solution)/shard_map/all_to_all | solution.py:380
  31.0 14.0 %collective-permute-start.6 = (bf16[256,128]{1,0:T(8,128)(2,1)S(1)}, bf16[256,128]{1,0:T(8,128)(2,1)S(1)}, u32[]{:S(2)}, u32[]{:S(2)}) collective-permute-start(bf16[256,128]{1,0:T(8,128)(2,1)S(1)} %get-tuple-element.85), channel_id=1, source_target_pairs={{0,8},{8,0},{16,24},{24,16},{1,9},{9,1},{17,25},{25,17},{2,10},{10... | collective-permute-start | bytes 196616 | tf_op jit(solution)/shard_map/ppermute | solution.py:310
  32.9 13.5 %collective-permute-start.7 = (bf16[256,128]{1,0:T(8,128)(2,1)S(1)}, bf16[256,128]{1,0:T(8,128)(2,1)S(1)}, u32[]{:S(2)}, u32[]{:S(2)}) collective-permute-start(bf16[256,128]{1,0:T(8,128)(2,1)S(1)} %get-tuple-element.84), channel_id=1, source_target_pairs={{0,16},{8,24},{16,0},{24,8},{1,17},{9,25},{17,1},{25,9},{2,18},{10... | collective-permute-start | bytes 196616 | tf_op jit(solution)/shard_map/ppermute | solution.py:310
  34.3 14.8 %collective-permute-start.8 = (bf16[256,128]{1,0:T(8,128)(2,1)S(1)}, bf16[256,128]{1,0:T(8,128)(2,1)S(1)}, u32[]{:S(2)}, u32[]{:S(2)}) collective-permute-start(bf16[256,128]{1,0:T(8,128)(2,1)S(1)} %get-tuple-element.83), channel_id=1, source_target_pairs={{0,24},{8,16},{16,8},{24,0},{1,25},{9,17},{17,9},{25,1},{2,26},{10... | collective-permute-start | bytes 196616 | tf_op jit(solution)/shard_map/ppermute | solution.py:310
  34.6 72.2 %copy-start.7 = (bf16[256,1024]{1,0:T(8,128)(2,1)}, bf16[256,1024]{1,0:T(8,128)(2,1)S(1)}, u32[]{:S(2)}) copy-start(bf16[256,1024]{1,0:T(8,128)(2,1)S(1)} %constant_dynamic-update-slice_fusion.2.refs_1_) | copy-start | bytes 1572868
  34.7 30.1 %collective-permute-start.12 = (bf16[256,1024]{1,0:T(8,128)(2,1)S(1)}, bf16[256,1024]{1,0:T(8,128)(2,1)S(1)}, u32[]{:S(2)}, u32[]{:S(2)}) collective-permute-start(bf16[256,1024]{1,0:T(8,128)(2,1)S(1)} %constant_dynamic-update-slice_fusion.2.refs_1_), channel_id=1, source_target_pairs={{0,8},{8,0},{16,24},{24,16},{1,9},{9,1},{17,25},{25,17},{2,10},{10... | collective-permute-start | bytes 1572872 | tf_op jit(solution)/shard_map/ppermute | solution.py:310
  36.5 28.6 %collective-permute-start.13 = (bf16[256,1024]{1,0:T(8,128)(2,1)S(1)}, bf16[256,1024]{1,0:T(8,128)(2,1)S(1)}, u32[]{:S(2)}, u32[]{:S(2)}) collective-permute-start(bf16[256,1024]{1,0:T(8,128)(2,1)S(1)} %constant_dynamic-update-slice_fusion.2.refs_1_), channel_id=1, source_target_pairs={{0,16},{8,24},{16,0},{24,8},{1,17},{9,25},{17,1},{25,9},{2,18},{10... | collective-permute-start | bytes 1572872 | tf_op jit(solution)/shard_map/ppermute | solution.py:310
  50.8 4.3 %collective-permute-start.9 = (f32[4,32,1024]{2,1,0:T(8,128)S(1)}, f32[4,32,1024]{2,1,0:T(8,128)S(1)}, u32[]{:S(2)}, u32[]{:S(2)}) collective-permute-start(f32[4,32,1024]{2,1,0:T(8,128)S(1)} %dynamic-slice_bitcast_fusion), channel_id=1, source_target_pairs={{0,1},{1,0},{2,3},{3,2},{4,5},{5,4},{6,7},{7,6},{8,9},{9,8},{10,11... | collective-permute-start | bytes 1572872 | tf_op jit(solution)/shard_map/ppermute | solution.py:310
  50.9 35.2 %copy-start.2 = (bf16[256,256]{1,0:T(8,128)(2,1)S(1)}, bf16[256,256]{1,0:T(8,128)(2,1)}, u32[]{:S(2)}) copy-start(bf16[256,256]{1,0:T(8,128)(2,1)} %constant.77.clone.forward) | copy-start | bytes 393220
  51.0 28.0 %collective-permute-start.10 = (bf16[256,1024]{1,0:T(8,128)(2,1)S(1)}, bf16[256,1024]{1,0:T(8,128)(2,1)S(1)}, u32[]{:S(2)}, u32[]{:S(2)}) collective-permute-start(bf16[256,1024]{1,0:T(8,128)(2,1)S(1)} %constant_dynamic-update-slice_fusion.refs_0_), channel_id=1, source_target_pairs={{0,8},{8,0},{16,24},{24,16},{1,9},{9,1},{17,25},{25,17},{2,10},{10... | collective-permute-start | bytes 1572872 | tf_op jit(solution)/shard_map/ppermute | solution.py:310
  51.5 28.3 %collective-permute-start.11 = (bf16[256,1024]{1,0:T(8,128)(2,1)S(1)}, bf16[256,1024]{1,0:T(8,128)(2,1)}, u32[]{:S(2)}, u32[]{:S(2)}) collective-permute-start(bf16[256,1024]{1,0:T(8,128)(2,1)S(1)} %constant_dynamic-update-slice_fusion.refs_0_), channel_id=1, source_target_pairs={{0,16},{8,24},{16,0},{24,8},{1,17},{9,25},{17,1},{25,9},{2,18},{10... | collective-permute-start | bytes 1572872 | tf_op jit(solution)/shard_map/ppermute | solution.py:310
  79.8 18.6 %collective-permute-start.18 = (bf16[256,1024]{1,0:T(8,128)(2,1)}, bf16[256,1024]{1,0:T(8,128)(2,1)}, u32[]{:S(2)}, u32[]{:S(2)}) collective-permute-start(bf16[256,1024]{1,0:T(8,128)(2,1)} %copy-done.13), channel_id=1, source_target_pairs={{0,8},{8,0},{16,24},{24,16},{1,9},{9,1},{17,25},{25,17},{2,10},{10... | collective-permute-start | bytes 1572872 | tf_op jit(solution)/shard_map/ppermute | solution.py:310
  80.3 18.1 %collective-permute-start.17 = (bf16[256,1024]{1,0:T(8,128)(2,1)}, bf16[256,1024]{1,0:T(8,128)(2,1)}, u32[]{:S(2)}, u32[]{:S(2)}) collective-permute-start(bf16[256,1024]{1,0:T(8,128)(2,1)} %copy-done.15), channel_id=1, source_target_pairs={{0,16},{8,24},{16,0},{24,8},{1,17},{9,25},{17,1},{25,9},{2,18},{10... | collective-permute-start | bytes 1572872 | tf_op jit(solution)/shard_map/ppermute | solution.py:310
  81.6 16.8 %collective-permute-start.14 = (bf16[32,1024]{1,0:T(8,128)(2,1)S(1)}, bf16[32,1024]{1,0:T(8,128)(2,1)}, u32[]{:S(2)}, u32[]{:S(2)}) collective-permute-start(bf16[32,1024]{1,0:T(8,128)(2,1)S(1)} %get-tuple-element.81), channel_id=1, source_target_pairs={{0,2},{1,3},{2,0},{3,1},{4,6},{5,7},{6,4},{7,5},{8,10},{9,11},{10,... | collective-permute-start | bytes 196616 | tf_op jit(solution)/shard_map/ppermute | solution.py:310
  83.2 15.2 %collective-permute-start.15 = (bf16[32,1024]{1,0:T(8,128)(2,1)S(1)}, bf16[32,1024]{1,0:T(8,128)(2,1)}, u32[]{:S(2)}, u32[]{:S(2)}) collective-permute-start(bf16[32,1024]{1,0:T(8,128)(2,1)S(1)} %get-tuple-element.80), channel_id=1, source_target_pairs={{0,4},{1,5},{2,6},{3,7},{4,0},{5,1},{6,2},{7,3},{8,12},{9,13},{10,... | collective-permute-start | bytes 196616 | tf_op jit(solution)/shard_map/ppermute | solution.py:310
  85.8 12.6 %collective-permute-start.16 = (bf16[32,1024]{1,0:T(8,128)(2,1)S(1)}, bf16[32,1024]{1,0:T(8,128)(2,1)}, u32[]{:S(2)}, u32[]{:S(2)}) collective-permute-start(bf16[32,1024]{1,0:T(8,128)(2,1)S(1)} %get-tuple-element.79), channel_id=1, source_target_pairs={{0,6},{1,7},{2,4},{3,5},{4,2},{5,3},{6,0},{7,1},{8,14},{9,15},{10,... | collective-permute-start | bytes 196616 | tf_op jit(solution)/shard_map/ppermute | solution.py:310
  98.4 32.3 %all-to-all-start.1 = ((bf16[32,4,32,128]{3,2,1,0:T(8,128)(2,1)}), bf16[32,4,32,128]{3,2,1,0:T(8,128)(2,1)S(1)}, u32[]{:S(2)}, u32[]{:S(2)}) async-start(bf16[32,4,32,128]{3,2,1,0:T(8,128)(2,1)} %get-tuple-element.61), calls=%async_computation.1 | async-start | bytes 2097152 | tf_op jit(solution)/shard_map/all_to_all | solution.py:380
  103.1 2.2 %collective-permute-start.26 = (bf16[256,1024]{1,0:T(8,128)(2,1)}, bf16[256,1024]{1,0:T(8,128)(2,1)S(1)}, u32[]{:S(2)}, u32[]{:S(2)}) collective-permute-start(bf16[256,1024]{1,0:T(8,128)(2,1)} %collective-permute-done.18.refs_7_), channel_id=1, source_target_pairs={{0,1},{1,0},{2,3},{3,2},{4,5},{5,4},{6,7},{7,6},{8,9},{9,8},{10,11... | collective-permute-start | bytes 1572872 | tf_op jit(solution)/shard_map/ppermute | solution.py:310
  103.4 3.4 %collective-permute-start.25 = (bf16[256,1024]{1,0:T(8,128)(2,1)}, bf16[256,1024]{1,0:T(8,128)(2,1)S(1)}, u32[]{:S(2)}, u32[]{:S(2)}) collective-permute-start(bf16[256,1024]{1,0:T(8,128)(2,1)} %collective-permute-done.17.refs_6_), channel_id=1, source_target_pairs={{0,1},{1,0},{2,3},{3,2},{4,5},{5,4},{6,7},{7,6},{8,9},{9,8},{10,11... | collective-permute-start | bytes 1572872 | tf_op jit(solution)/shard_map/ppermute | solution.py:310
  103.7 3.4 %collective-permute-start.24 = (bf16[256,1024]{1,0:T(8,128)(2,1)S(1)}, bf16[256,1024]{1,0:T(8,128)(2,1)S(1)}, u32[]{:S(2)}, u32[]{:S(2)}) collective-permute-start(bf16[256,1024]{1,0:T(8,128)(2,1)S(1)} %copy-done.14), channel_id=1, source_target_pairs={{0,1},{1,0},{2,3},{3,2},{4,5},{5,4},{6,7},{7,6},{8,9},{9,8},{10,11... | collective-permute-start | bytes 1572872 | tf_op jit(solution)/shard_map/ppermute | solution.py:310
  103.9 4.4 %collective-permute-start.23 = (bf16[256,1024]{1,0:T(8,128)(2,1)}, bf16[256,1024]{1,0:T(8,128)(2,1)S(1)}, u32[]{:S(2)}, u32[]{:S(2)}) collective-permute-start(bf16[256,1024]{1,0:T(8,128)(2,1)} %collective-permute-done.11.refs_4_), channel_id=1, source_target_pairs={{0,1},{1,0},{2,3},{3,2},{4,5},{5,4},{6,7},{7,6},{8,9},{9,8},{10,11... | collective-permute-start | bytes 1572872 | tf_op jit(solution)/shard_map/ppermute | solution.py:310
  104.2 4.1 %collective-permute-start.22 = (bf16[256,1024]{1,0:T(8,128)(2,1)S(1)}, bf16[256,1024]{1,0:T(8,128)(2,1)S(1)}, u32[]{:S(2)}, u32[]{:S(2)}) collective-permute-start(bf16[256,1024]{1,0:T(8,128)(2,1)S(1)} %copy-done.12), channel_id=1, source_target_pairs={{0,1},{1,0},{2,3},{3,2},{4,5},{5,4},{6,7},{7,6},{8,9},{9,8},{10,11... | collective-permute-start | bytes 1572872 | tf_op jit(solution)/shard_map/ppermute | solution.py:310
  105.3 4.5 %collective-permute-start.21 = (bf16[256,1024]{1,0:T(8,128)(2,1)}, bf16[256,1024]{1,0:T(8,128)(2,1)S(1)}, u32[]{:S(2)}, u32[]{:S(2)}) collective-permute-start(bf16[256,1024]{1,0:T(8,128)(2,1)} %copy-done.15), channel_id=1, source_target_pairs={{0,1},{1,0},{2,3},{3,2},{4,5},{5,4},{6,7},{7,6},{8,9},{9,8},{10,11... | collective-permute-start | bytes 1572872 | tf_op jit(solution)/shard_map/ppermute | solution.py:310
  106.8 3.0 %collective-permute-start.20 = (bf16[256,1024]{1,0:T(8,128)(2,1)S(1)}, bf16[256,1024]{1,0:T(8,128)(2,1)S(1)}, u32[]{:S(2)}, u32[]{:S(2)}) collective-permute-start(bf16[256,1024]{1,0:T(8,128)(2,1)S(1)} %constant_dynamic-update-slice_fusion.2.refs_1_), channel_id=1, source_target_pairs={{0,1},{1,0},{2,3},{3,2},{4,5},{5,4},{6,7},{7,6},{8,9},{9,8},{10,11... | collective-permute-start | bytes 1572872 | tf_op jit(solution)/shard_map/ppermute | solution.py:310
  107.1 3.3 %collective-permute-start.19 = (bf16[256,1024]{1,0:T(8,128)(2,1)S(1)}, bf16[256,1024]{1,0:T(8,128)(2,1)S(1)}, u32[]{:S(2)}, u32[]{:S(2)}) collective-permute-start(bf16[256,1024]{1,0:T(8,128)(2,1)S(1)} %copy-done.9), channel_id=1, source_target_pairs={{0,1},{1,0},{2,3},{3,2},{4,5},{5,4},{6,7},{7,6},{8,9},{9,8},{10,11... | collective-permute-start | bytes 1572872 | tf_op jit(solution)/shard_map/ppermute | solution.py:310
  130.7 13.0 %all-to-all-start.2 = ((bf16[32,32,128]{2,1,0:T(8,128)(2,1)}), bf16[32,32,128]{2,1,0:T(8,128)(2,1)S(1)}, u32[]{:S(2)}, u32[]{:S(2)}) async-start(bf16[32,32,128]{2,1,0:T(8,128)(2,1)} %shard_map.167), calls=%async_computation.2 | async-start | bytes 524288 | tf_op jit(solution)/shard_map/all_to_all | solution.py:380
  (28 other events, 268.4 us)

commit v4 on v3

--- a/solution.py
+++ b/solution.py
@@ -35,42 +35,62 @@
     )
 
 
-def fft_real(xs):
-    size = len(xs)
+def turned_by(pair, step, size):
+    re, im = pair
+    step %= size
+    if step == 0:
+        return pair
+    if 4 * step == size:
+        return im, -re
+    if 2 * step == size:
+        return -re, -im
+    if 4 * step == 3 * size:
+        return -im, re
+    cos, sin = math.cos(2.0 * math.pi * step / size), math.sin(2.0 * math.pi * step / size)
+    if 8 * step == size:
+        return (re + im) * cos, (im - re) * cos
+    if 8 * step == 3 * size:
+        return (im - re) * sin, -(re + im) * sin
+    if 8 * step == 5 * size:
+        return (re + im) * cos, (im - re) * cos
+    if 8 * step == 7 * size:
+        return (re - im) * cos, (im + re) * cos
+    return re * cos + im * sin, im * cos - re * sin
+
+
+def fft(pairs):
+    size = len(pairs)
     if size == 1:
-        return [(xs[0], None)]
-    if size == 2:
-        turned = xs[1] * math.cos(math.pi / 4)
-        return [(xs[0] + turned, -turned), (xs[0] - turned, turned)]
-    even, odd = fft_real(xs[0::2]), fft_real(xs[1::2])
+        return pairs
+    even, odd = fft(pairs[0::2]), fft(pairs[1::2])
     low, high = [], []
     for k in range(size // 2):
-        angle = -2.0 * math.pi * (k + 0.25) / size
-        cos, sin = math.cos(angle), math.sin(angle)
-        (er, ei), (orr, oi) = even[k], odd[k]
-        tr = orr * cos - oi * sin
-        ti = orr * sin + oi * cos
+        (er, ei), (tr, ti) = even[k], turned_by(odd[k], k, size)
         low.append((er + tr, ei + ti))
         high.append((er - tr, ei - ti))
     return low + high
 
 
+def fft_real(xs):
+    angles = [2.0 * math.pi * n / (4 * len(xs)) for n in range(len(xs))]
+    return fft([(x * math.cos(angle), x * -math.sin(angle)) for x, angle in zip(xs, angles)])
+
+
 def fft_back(pairs):
-    size = len(pairs)
-    if size == 2:
-        (ar, ai), (br, bi) = pairs
-        return [ar + br, ((ar - br) - (ai - bi)) * math.cos(math.pi / 4)]
-    half = size // 2
-    even, odd = [], []
-    for k in range(half):
-        angle = 2.0 * math.pi * (k + 0.25) / size
-        cos, sin = math.cos(angle), math.sin(angle)
-        (ar, ai), (br, bi) = pairs[k], pairs[k + half]
-        even.append((ar + br, ai + bi))
-        dr, di = ar - br, ai - bi
-        odd.append((dr * cos - di * sin, dr * sin + di * cos))
-    even, odd = fft_back(even), fft_back(odd)
-    return [term for pair in zip(even, odd) for term in pair]
+    def sums(pairs):
+        size = len(pairs)
+        if size == 1:
+            return pairs
+        half = size // 2
+        even, odd = [], []
+        for k in range(half):
+            (ar, ai), (br, bi) = pairs[k], pairs[k + half]
+            even.append((ar + br, ai + bi))
+            odd.append(turned_by((ar - br, ai - bi), -k, size))
+        return [term for pair in zip(sums(even), sums(odd)) for term in pair]
+
+    angles = [2.0 * math.pi * n / (4 * len(pairs)) for n in range(len(pairs))]
+    return [re * math.cos(angle) - im * math.sin(angle) for (re, im), angle in zip(sums(pairs), angles)]
 
 
 def transforms(devices, group, held, turn_cos, turn_sin):
@@ -179,9 +199,10 @@
     send(5, project(0))
 
 
-def middle_kernel(scale, me, here, forward, backward, turn_cos, turn_sin, back, slab, held, spec_a, spec_b, spec_c):
+def middle_kernel(scale, me, here, forward, backward, turn_cos, turn_sin, back_far, slab, held, spec_a, spec_b, spec_c, back, done):
     devices, _, group, cols = here.shape
     rows = devices * group
+    copies = [pltpu.make_async_copy(back.at[:, i], back_far.at[:, i], done.at[i]) for i in range(4)]
     into, outof = transforms(devices, group, held, turn_cos, turn_sin)
     flat = lambda i: here[:, i].astype(jnp.float32).reshape(rows, cols)
     blocks = lambda x: x.astype(jnp.bfloat16).reshape(devices, group, cols)
@@ -201,10 +222,12 @@
     correlate(spec_a, spec_b, spec_c, forward, backward)
     outof(spec_c, scale)
     back[:, 3] = blocks(held[...])
+    copies[3].start()
     outof(spec_b, scale)
     grad_first = held[...].astype(jnp.bfloat16).astype(jnp.float32)
     gate_grad = grad_first * flat(0)
     back[:, 1] = blocks(gate_grad)
+    copies[1].start()
     lay(1, gate_grad)
     held[...] = (grad_first * flat(4)).astype(jnp.bfloat16).astype(jnp.float32)
     into(spec_a)
@@ -217,9 +240,13 @@
     correlate(spec_a, spec_b, spec_c, forward, backward)
     outof(spec_c, scale)
     back[:, 2] = blocks(held[...])
+    copies[2].start()
     outof(spec_b, scale)
     back[:, 0] = blocks(held[...])
+    copies[0].start()
     lay(0, held[...])
+    for copy in copies:
+        copy.wait()
 
 
 def slab_kernel(scale, slab, *refs):
@@ -238,17 +265,19 @@
     part[...] = (total * scale).T.astype(jnp.bfloat16).reshape(devices, group, cols)
 
 
-def on_chip(kernel, out_shape, args, scratch=(), far=(), vmem_mib=48):
-    vmem = pl.BlockSpec(memory_space=pltpu.VMEM)
+def on_chip(kernel, out_shape, args, scratch=(), far=(), vmem_mib=48, far_out=()):
+    alone = not isinstance(out_shape, list)
+    out_shape = [out_shape] if alone else out_shape
     spaces = [pltpu.SMEM if x.dtype == jnp.int32 else pltpu.HBM if i in far else pltpu.VMEM for i, x in enumerate(args)]
-    return pl.pallas_call(
+    outs = pl.pallas_call(
         kernel,
         out_shape=out_shape,
         in_specs=[pl.BlockSpec(memory_space=space) for space in spaces],
-        out_specs=jax.tree.map(lambda _: vmem, out_shape),
+        out_specs=[pl.BlockSpec(memory_space=pltpu.HBM if i in far_out else pltpu.VMEM) for i in range(len(out_shape))],
         scratch_shapes=list(scratch),
         compiler_params=pltpu.CompilerParams(vmem_limit_bytes=vmem_mib * 2**20),
     )(*args)
+    return outs[0] if alone else outs
 
 
 def long_convs(rows, rows_dev):
@@ -323,12 +352,14 @@
 
 
 def far_chips(blocks, later):
-    blocks = list(blocks)
+    blocks, first = list(blocks), []
     for j in range(1, len(blocks)):
         low = j & -j
         if j != low:
-            blocks[j] = swap(after(blocks[j ^ low], later), "minor", 2 * low)
-    return blocks
+            block = after(blocks[j ^ low], later)
+            first.append(swap(block[:16], "minor", 2 * low))
+            blocks[j] = jnp.concatenate([first[-1], swap(block[16:], "minor", 2 * low)])
+    return blocks, first
 
 
 def major_near(blocks):
@@ -405,8 +436,9 @@
         60,
     )
     cots = [swap(out_cot, "major", j) if j else out_cot for j in range(majors)]
-    near_in = far_chips(near_in, late)
-    sent = after(sent, *cots, *near_in)
+    sent = after(sent, *cots, *[block for block in near_in if block is not None])
+    near_in, first = far_chips(near_in, late)
+    sent = after(sent, *first)
     here = regroup(sent)
     total = out_part(after(second_out, sent), cots)
     late = lax.dot_general(late, w_in[:, 2 * width :], LAST, preferred_element_type=jnp.float32)
@@ -418,7 +450,15 @@
         functools.partial(middle_kernel, fft_scale),
         [field(4), array(rows_dev, devices * rows_dev)],
         (lax.axis_index(AXES).astype(jnp.int32)[None], here, *tables(devices, rows_dev)),
-        [pltpu.VMEM((devices * group, rows_dev), jnp.float32), spec, spec, spec],
+        [
+            pltpu.VMEM((devices * group, rows_dev), jnp.float32),
+            spec,
+            spec,
+            spec,
+            pltpu.VMEM((devices, 4, group, rows_dev), jnp.bfloat16),
+            pltpu.SemaphoreType.DMA((4,)),
+        ],
+        far_out=(0,),
     )
     all_in = gather_chips(lines, here)
     parts = out_parts(after(total, *[piece for piece in lines[0] if piece is not None]))

time: 146 us -> 143 us (0.979)
  waiting for transfers between devices: 63.9 us -> 61.2 us
  starting transfers between devices: 38.7 us -> 41 us
    ppermute x27 -> x28, starting transfers between devices: 26 us -> 30.3 us  [swap(): lax.ppermute(block, axis, [(i, i ^ bit) for i in range(lax.axis_size(axis...]
    ppermute x27 -> x28, waiting for transfers between devices: 47.1 us -> 44 us  [swap(): lax.ppermute(block, axis, [(i, i ^ bit) for i in range(lax.axis_size(axis...]
    all_to_all x3, starting transfers between devices: 12.8 us -> 10.7 us  [regroup(): return lax.all_to_all(x, AXES, split_axis=0, concat_axis=0, tiled=True)]
    unnamed x62 -> x64, local copies, waits for them, and re-layouts: 3.29 us -> 2.98 us
  transfers between devices with their start and end apart: 30 -> 31, of which waited for: 16 -> 16; matrix products, arithmetic and copies ran while one was open for 5% -> 4% of each run, Pallas kernels for 20% -> 20%
where the time goes in v4:
time: 143 us; the launch traced here: 142 us
  waiting for transfers between devices  61.2 us (43%)
  starting transfers between devices  41 us (29%)
  Pallas kernels  29.8 us (21%)
  matrix products  3.66 us (3%)
  local copies, waits for them, and re-layouts  3.14 us (2%)
  other arithmetic  2.29 us (2%)
    ppermute x28, waiting for transfers between devices, swap(): lax.ppermute(block, axis, [(i, i ^ bit) for i in range(lax.axis_size(axis...  44 us
    ppermute x28, starting transfers between devices, swap(): lax.ppermute(block, axis, [(i, i ^ bit) for i in range(lax.axis_size(axis...  30.3 us
    pallas_call x5, Pallas kernels, on_chip(): pl.pallas_call(kernel, out_shape=out_shape, in_specs=[pl.BlockSpec(memory...  29.8 us
    all_to_all x3, waiting for transfers between devices, regroup(): return lax.all_to_all(x, AXES, split_axis=0, concat_axis=0, tiled=True)  17.1 us
    all_to_all x3, starting transfers between devices, regroup(): return lax.all_to_all(x, AXES, split_axis=0, concat_axis=0, tiled=True)  10.7 us
    dot_general x1, matrix products, shards(): lax.dot_general(late, w_in[:, 2 * width:], LAST, preferred_element_type=j...  3.22 us
    unnamed x64, local copies, waits for them, and re-layouts  2.98 us
  transfers between devices with their start and end apart: 31, of which 16 were waited for; matrix products, arithmetic and copies ran while one was open for 4% of the time, Pallas kernels for 20%

profile of v4, /device:TPU:0, one launch (start us, length us, event | category | flops | bytes accessed | tf_op | source)
XLA Modules:
  0.0 142.2 jit_solution(7567478462573704848)
XLA Ops:
  0.6 4.1 %collective-permute-start.4 = (bf16[128,1024]{1,0:T(8,128)(2,1)}, bf16[128,1024]{1,0:T(8,128)(2,1)S(1)}, u32[]{:S(2)}, u32[]{:S(2)}) collective-permute-start(bf16[128,1024]{1,0:T(8,128)(2,1)} %block_in.1), channel_id=1, source_target_pairs={{0,4},{1,5},{2,6},{3,7},{4,0},{5,1},{6,2},{7,3},{8,12},{9,13},{10,... | collective-permute-start | bytes 786440 | tf_op jit(solution)/shard_map/ppermute | solution.py:339
  4.7 1.5 %collective-permute-start = (bf16[128,1024]{1,0:T(8,128)(2,1)}, bf16[128,1024]{1,0:T(8,128)(2,1)S(1)}, u32[]{:S(2)}, u32[]{:S(2)}) collective-permute-start(bf16[128,1024]{1,0:T(8,128)(2,1)} %out_cot.1), channel_id=1, source_target_pairs={{0,8},{8,0},{16,24},{24,16},{1,9},{9,1},{17,25},{25,17},{2,10},{10... | collective-permute-start | bytes 786440 | tf_op jit(solution)/shard_map/ppermute | solution.py:339
  6.2 1.5 %collective-permute-start.1 = (bf16[128,1024]{1,0:T(8,128)(2,1)}, bf16[128,1024]{1,0:T(8,128)(2,1)S(1)}, u32[]{:S(2)}, u32[]{:S(2)}) collective-permute-start(bf16[128,1024]{1,0:T(8,128)(2,1)} %out_cot.1), channel_id=1, source_target_pairs={{0,16},{8,24},{16,0},{24,8},{1,17},{9,25},{17,1},{25,9},{2,18},{10... | collective-permute-start | bytes 786440 | tf_op jit(solution)/shard_map/ppermute | solution.py:339
  8.2 1.6 %collective-permute-start.3 = (bf16[128,1024]{1,0:T(8,128)(2,1)}, bf16[128,1024]{1,0:T(8,128)(2,1)S(1)}, u32[]{:S(2)}, u32[]{:S(2)}) collective-permute-start(bf16[128,1024]{1,0:T(8,128)(2,1)} %block_in.1), channel_id=1, source_target_pairs={{0,2},{1,3},{2,0},{3,1},{4,6},{5,7},{6,4},{7,5},{8,10},{9,11},{10,... | collective-permute-start | bytes 786440 | tf_op jit(solution)/shard_map/ppermute | solution.py:339
  10.4 7.3 %shard_map.164 = (bf16[32,7,32,128]{3,2,1,0:T(8,128)(2,1)}, bf16[1024,128]{1,0:T(8,128)(2,1)}, bf16[128,1024]{1,0:T(8,128)(2,1)}) custom-call(bf16[128,128]{1,0:T(8,128)(2,1)} %fusion.20.square, bf16[128,1024]{1,0:T(8,128)(2,1)} %conv_one.1, bf16[128,1024]{1,0:T(8,128)(2,1)} %filter_two.1, bf16[128,1024]{1,0:T(8,128)(2,1)} %filter_one.1, ...), custom_call_target="tpu_custom_call" | custom-call | tf_op jit(solution)/shard_map/pallas_call | solution.py:272
  20.3 1.4 collective-permute-done.5
  21.7 5.0 %all-to-all-start = ((bf16[32,7,32,128]{3,2,1,0:T(8,128)(2,1)}), bf16[32,7,32,128]{3,2,1,0:T(8,128)(2,1)S(1)}, u32[]{:S(2)}, u32[]{:S(2)}) async-start(bf16[32,7,32,128]{3,2,1,0:T(8,128)(2,1)} %get-tuple-element.47), calls=%async_computation | async-start | bytes 3670016 | tf_op jit(solution)/shard_map/all_to_all | solution.py:411
  26.8 1.8 %collective-permute-start.12 = (bf16[112,1024]{1,0:T(8,128)(2,1)S(1)}, bf16[112,1024]{1,0:T(8,128)(2,1)S(1)}, u32[]{:S(2)}, u32[]{:S(2)}) collective-permute-start(bf16[112,1024]{1,0:T(8,128)(2,1)S(1)} %slice.11), channel_id=1, source_target_pairs={{0,2},{1,3},{2,0},{3,1},{4,6},{5,7},{6,4},{7,5},{8,10},{9,11},{10,... | collective-permute-start | bytes 688136 | tf_op jit(solution)/shard_map/ppermute | solution.py:339
  28.6 1.5 %collective-permute-start.6 = (bf16[256,128]{1,0:T(8,128)(2,1)S(1)}, bf16[256,128]{1,0:T(8,128)(2,1)S(1)}, u32[]{:S(2)}, u32[]{:S(2)}) collective-permute-start(bf16[256,128]{1,0:T(8,128)(2,1)S(1)} %get-tuple-element.87), channel_id=1, source_target_pairs={{0,8},{8,0},{16,24},{24,16},{1,9},{9,1},{17,25},{25,17},{2,10},{10... | collective-permute-start | bytes 196616 | tf_op jit(solution)/shard_map/ppermute | solution.py:339
  30.2 1.5 %collective-permute-start.7 = (bf16[256,128]{1,0:T(8,128)(2,1)S(1)}, bf16[256,128]{1,0:T(8,128)(2,1)S(1)}, u32[]{:S(2)}, u32[]{:S(2)}) collective-permute-start(bf16[256,128]{1,0:T(8,128)(2,1)S(1)} %get-tuple-element.86), channel_id=1, source_target_pairs={{0,16},{8,24},{16,0},{24,8},{1,17},{9,25},{17,1},{25,9},{2,18},{10... | collective-permute-start | bytes 196616 | tf_op jit(solution)/shard_map/ppermute | solution.py:339
  32.3 1.5 %collective-permute-start.10 = (bf16[256,1024]{1,0:T(8,128)(2,1)S(1)}, bf16[256,1024]{1,0:T(8,128)(2,1)S(1)}, u32[]{:S(2)}, u32[]{:S(2)}) collective-permute-start(bf16[256,1024]{1,0:T(8,128)(2,1)S(1)} %constant_dynamic-update-slice_fusion.refs_0_), channel_id=1, source_target_pairs={{0,8},{8,0},{16,24},{24,16},{1,9},{9,1},{17,25},{25,17},{2,10},{10... | collective-permute-start | bytes 1572872 | tf_op jit(solution)/shard_map/ppermute | solution.py:339
  33.8 7.0 %collective-permute-done.6 = bf16[256,128]{1,0:T(8,128)(2,1)S(1)} collective-permute-done((bf16[256,128]{1,0:T(8,128)(2,1)S(1)}, bf16[256,128]{1,0:T(8,128)(2,1)S(1)}, u32[]{:S(2)}, u32[]{:S(2)}) %collective-permute-start.6) | collective-permute-done | bytes 65568 | tf_op jit(solution)/shard_map/ppermute | solution.py:339
  40.8 1.5 %collective-permute-start.11 = (bf16[256,1024]{1,0:T(8,128)(2,1)S(1)}, bf16[256,1024]{1,0:T(8,128)(2,1)S(1)}, u32[]{:S(2)}, u32[]{:S(2)}) collective-permute-start(bf16[256,1024]{1,0:T(8,128)(2,1)S(1)} %constant_dynamic-update-slice_fusion.refs_0_), channel_id=1, source_target_pairs={{0,16},{8,24},{16,0},{24,8},{1,17},{9,25},{17,1},{25,9},{2,18},{10... | collective-permute-start | bytes 1572872 | tf_op jit(solution)/shard_map/ppermute | solution.py:339
  42.2 2.6 %collective-permute-done.8 = bf16[256,128]{1,0:T(8,128)(2,1)S(1)} collective-permute-done((bf16[256,128]{1,0:T(8,128)(2,1)S(1)}, bf16[256,128]{1,0:T(8,128)(2,1)S(1)}, u32[]{:S(2)}, u32[]{:S(2)}) %collective-permute-start.8) | collective-permute-done | bytes 65568 | tf_op jit(solution)/shard_map/ppermute | solution.py:339
  45.5 16.5 %collective-permute-done.12 = bf16[112,1024]{1,0:T(8,128)(2,1)S(1)} collective-permute-done((bf16[112,1024]{1,0:T(8,128)(2,1)S(1)}, bf16[112,1024]{1,0:T(8,128)(2,1)S(1)}, u32[]{:S(2)}, u32[]{:S(2)}) %collective-permute-start.12) | collective-permute-done | bytes 229408 | tf_op jit(solution)/shard_map/ppermute | solution.py:339
  62.1 1.7 %collective-permute-start.13 = (bf16[256,1024]{1,0:T(8,128)(2,1)S(1)}, bf16[256,1024]{1,0:T(8,128)(2,1)S(1)}, u32[]{:S(2)}, u32[]{:S(2)}) collective-permute-start(bf16[256,1024]{1,0:T(8,128)(2,1)S(1)} %constant_dynamic-update-slice_fusion.2.refs_1_), channel_id=1, source_target_pairs={{0,8},{8,0},{16,24},{24,16},{1,9},{9,1},{17,25},{25,17},{2,10},{10... | collective-permute-start | bytes 1572872 | tf_op jit(solution)/shard_map/ppermute | solution.py:339
  63.8 1.5 %collective-permute-start.14 = (bf16[256,1024]{1,0:T(8,128)(2,1)S(1)}, bf16[256,1024]{1,0:T(8,128)(2,1)}, u32[]{:S(2)}, u32[]{:S(2)}) collective-permute-start(bf16[256,1024]{1,0:T(8,128)(2,1)S(1)} %constant_dynamic-update-slice_fusion.2.refs_1_), channel_id=1, source_target_pairs={{0,16},{8,24},{16,0},{24,8},{1,17},{9,25},{17,1},{25,9},{2,18},{10... | collective-permute-start | bytes 1572872 | tf_op jit(solution)/shard_map/ppermute | solution.py:339
  65.3 3.2 %fusion.part = f32[128,1024]{1,0:T(8,128)} fusion(bf16[128,1024]{1,0:T(8,128)(2,1)S(1)} %copy-done.26, bf16[1024,3072]{1,0:T(8,128)(2,1)} %w_in.3), kind=kOutput, calls=%fused_computation | convolution fusion | flops 268435456 | bytes 2883584 | tf_op jit(solution)/shard_map/dot_general | solution.py:444
  68.6 9.0 %collective-permute-done.13.refs_3_ = bf16[256,1024]{1,0:T(8,128)(2,1)S(1)} collective-permute-done((bf16[256,1024]{1,0:T(8,128)(2,1)S(1)}, bf16[256,1024]{1,0:T(8,128)(2,1)S(1)}, u32[]{:S(2)}, u32[]{:S(2)}) %collective-permute-start.13) | collective-permute-done | bytes 524320 | tf_op jit(solution)/shard_map/ppermute | solution.py:339
  79.9 1.5 %collective-permute-start.18 = (bf16[256,1024]{1,0:T(8,128)(2,1)}, bf16[256,1024]{1,0:T(8,128)(2,1)}, u32[]{:S(2)}, u32[]{:S(2)}) collective-permute-start(bf16[256,1024]{1,0:T(8,128)(2,1)} %copy-done.11), channel_id=1, source_target_pairs={{0,16},{8,24},{16,0},{24,8},{1,17},{9,25},{17,1},{25,9},{2,18},{10... | collective-permute-start | bytes 1572872 | tf_op jit(solution)/shard_map/ppermute | solution.py:339
  81.4 1.3 collective-permute-start.15
  82.7 1.4 %collective-permute-start.16 = (bf16[32,1024]{1,0:T(8,128)(2,1)S(1)}, bf16[32,1024]{1,0:T(8,128)(2,1)}, u32[]{:S(2)}, u32[]{:S(2)}) collective-permute-start(bf16[32,1024]{1,0:T(8,128)(2,1)S(1)} %get-tuple-element.82), channel_id=1, source_target_pairs={{0,4},{1,5},{2,6},{3,7},{4,0},{5,1},{6,2},{7,3},{8,12},{9,13},{10,... | collective-permute-start | bytes 196616 | tf_op jit(solution)/shard_map/ppermute | solution.py:339
  84.2 1.7 %collective-permute-start.17 = (bf16[32,1024]{1,0:T(8,128)(2,1)S(1)}, bf16[32,1024]{1,0:T(8,128)(2,1)}, u32[]{:S(2)}, u32[]{:S(2)}) collective-permute-start(bf16[32,1024]{1,0:T(8,128)(2,1)S(1)} %get-tuple-element.81), channel_id=1, source_target_pairs={{0,6},{1,7},{2,4},{3,5},{4,2},{5,3},{6,0},{7,1},{8,14},{9,15},{10,... | collective-permute-start | bytes 196616 | tf_op jit(solution)/shard_map/ppermute | solution.py:339
  85.9 10.1 %shard_map.165 = (bf16[32,4,32,128]{3,2,1,0:T(8,128)(2,1)}, bf16[128,4096]{1,0:T(8,128)(2,1)S(1)}) custom-call(s32[1]{0:T(128)} %bitcast.me, bf16[32,7,32,128]{3,2,1,0:T(8,128)(2,1)S(1)} %all-to-all-done.here, bf16[256,256]{1,0:T(8,128)(2,1)S(1)} %copy-done.2, bf16[256,256]{1,0:T(8,128)(2,1)S(1)} %copy-done.3, f32[256,128]{1,0:T(8,128)S(1)} %copy-done.4, ...), custom_call_target="tpu_custom_call" | custom-call | tf_op jit(solution)/shard_map/pallas_call | solution.py:272
  97.0 3.1 %all-to-all-start.1 = ((bf16[32,4,32,128]{3,2,1,0:T(8,128)(2,1)}), bf16[32,4,32,128]{3,2,1,0:T(8,128)(2,1)S(1)}, u32[]{:S(2)}, u32[]{:S(2)}) async-start(bf16[32,4,32,128]{3,2,1,0:T(8,128)(2,1)} %get-tuple-element.63), calls=%async_computation.1 | async-start | bytes 2097152 | tf_op jit(solution)/shard_map/all_to_all | solution.py:411
  108.3 5.7 %shard_map.167 = bf16[32,32,128]{2,1,0:T(8,128)(2,1)} custom-call(bf16[128,4096]{1,0:T(8,128)(2,1)} %copy-done, bf16[256,1024]{1,0:T(8,128)(2,1)} %copy-done.8, bf16[256,1024]{1,0:T(8,128)(2,1)} %copy-done.7, bf16[256,1024]{1,0:T(8,128)(2,1)} %copy-done.11, bf16[256,1024]{1,0:T(8,128)(2,1)} %copy-done.15, bf16[256,1024]{1,0:T(8,128)(2,1)} %copy-done.13, ...), custom_call_target="tpu_custom_call" | custom-call | tf_op jit(solution)/shard_map/pallas_call | solution.py:272
  114.1 13.7 %all-to-all-done.1.home = bf16[32,4,32,128]{3,2,1,0:T(8,128)(2,1)S(1)} async-done(((bf16[32,4,32,128]{3,2,1,0:T(8,128)(2,1)}), bf16[32,4,32,128]{3,2,1,0:T(8,128)(2,1)S(1)}, u32[]{:S(2)}, u32[]{:S(2)}) %all-to-all-start.1) | async-done | bytes 1048608 | tf_op jit(solution)/shard_map/all_to_all | solution.py:411
  127.8 2.6 %all-to-all-start.2 = ((bf16[32,32,128]{2,1,0:T(8,128)(2,1)}), bf16[32,32,128]{2,1,0:T(8,128)(2,1)S(1)}, u32[]{:S(2)}, u32[]{:S(2)}) async-start(bf16[32,32,128]{2,1,0:T(8,128)(2,1)} %shard_map.167), calls=%async_computation.2 | async-start | bytes 524288 | tf_op jit(solution)/shard_map/all_to_all | solution.py:411
  130.4 1.6 %add_multiply_fusion = f32[32,1024]{1,0:T(8,128)} fusion(bf16[32,1024]{1,0:T(8,128)(2,1)} %collective-permute-done.17, bf16[32,1024]{1,0:T(8,128)(2,1)} %collective-permute-done.16, f32[32,1024]{1,0:T(8,128)S(1)} %dynamic-slice_bitcast_fusion.1, bf16[32,1024]{1,0:T(8,128)(2,1)} %collective-permute-done.15), kind=kLoop, calls=%fused_computation.20 | loop fusion | flops 229376 | bytes 458752 | tf_op jit(solution)/shard_map/mul | solution.py:466
  132.0 5.3 %shard_map.166 = (bf16[128,1024]{1,0:T(8,128)(2,1)}, bf16[128,1024]{1,0:T(8,128)(2,1)}, bf16[128,1024]{1,0:T(8,128)(2,1)}) custom-call(bf16[128,128]{1,0:T(8,128)(2,1)} %fusion.20.square, bf16[32,4,32,128]{3,2,1,0:T(8,128)(2,1)} %copy-done.6, f32[128,1024]{1,0:T(8,128)} %fusion.part, bf16[1024,3072]{1,0:T(8,128)(2,1)} %w_in.3), custom_call_target="tpu_custom_call" | custom-call | tf_op jit(solution)/shard_map/pallas_call | solution.py:272
  137.3 3.4 %all-to-all-done.2.taken = bf16[32,32,128]{2,1,0:T(8,128)(2,1)S(1)} async-done(((bf16[32,32,128]{2,1,0:T(8,128)(2,1)}), bf16[32,32,128]{2,1,0:T(8,128)(2,1)S(1)}, u32[]{:S(2)}, u32[]{:S(2)}) %all-to-all-start.2) | async-done | bytes 262176 | tf_op jit(solution)/shard_map/all_to_all | solution.py:411
  140.7 1.4 shard_map.168
  (113 shorter events, 16.6 us)
Async XLA Ops:
  0.6 17.1 %collective-permute-start.4 = (bf16[128,1024]{1,0:T(8,128)(2,1)}, bf16[128,1024]{1,0:T(8,128)(2,1)S(1)}, u32[]{:S(2)}, u32[]{:S(2)}) collective-permute-start(bf16[128,1024]{1,0:T(8,128)(2,1)} %block_in.1), channel_id=1, source_target_pairs={{0,4},{1,5},{2,6},{3,7},{4,0},{5,1},{6,2},{7,3},{8,12},{9,13},{10,... | collective-permute-start | bytes 786440 | tf_op jit(solution)/shard_map/ppermute | solution.py:339
  4.7 13.5 %collective-permute-start = (bf16[128,1024]{1,0:T(8,128)(2,1)}, bf16[128,1024]{1,0:T(8,128)(2,1)S(1)}, u32[]{:S(2)}, u32[]{:S(2)}) collective-permute-start(bf16[128,1024]{1,0:T(8,128)(2,1)} %out_cot.1), channel_id=1, source_target_pairs={{0,8},{8,0},{16,24},{24,16},{1,9},{9,1},{17,25},{25,17},{2,10},{10... | collective-permute-start | bytes 786440 | tf_op jit(solution)/shard_map/ppermute | solution.py:339
  6.2 13.3 %collective-permute-start.1 = (bf16[128,1024]{1,0:T(8,128)(2,1)}, bf16[128,1024]{1,0:T(8,128)(2,1)S(1)}, u32[]{:S(2)}, u32[]{:S(2)}) collective-permute-start(bf16[128,1024]{1,0:T(8,128)(2,1)} %out_cot.1), channel_id=1, source_target_pairs={{0,16},{8,24},{16,0},{24,8},{1,17},{9,25},{17,1},{25,9},{2,18},{10... | collective-permute-start | bytes 786440 | tf_op jit(solution)/shard_map/ppermute | solution.py:339
  7.7 11.8 %collective-permute-start.2 = (bf16[128,1024]{1,0:T(8,128)(2,1)}, bf16[128,1024]{1,0:T(8,128)(2,1)S(1)}, u32[]{:S(2)}, u32[]{:S(2)}) collective-permute-start(bf16[128,1024]{1,0:T(8,128)(2,1)} %out_cot.1), channel_id=1, source_target_pairs={{0,24},{8,16},{16,8},{24,0},{1,25},{9,17},{17,9},{25,1},{2,26},{10... | collective-permute-start | bytes 786440 | tf_op jit(solution)/shard_map/ppermute | solution.py:339
  8.2 11.9 %collective-permute-start.3 = (bf16[128,1024]{1,0:T(8,128)(2,1)}, bf16[128,1024]{1,0:T(8,128)(2,1)S(1)}, u32[]{:S(2)}, u32[]{:S(2)}) collective-permute-start(bf16[128,1024]{1,0:T(8,128)(2,1)} %block_in.1), channel_id=1, source_target_pairs={{0,2},{1,3},{2,0},{3,1},{4,6},{5,7},{6,4},{7,5},{8,10},{9,11},{10,... | collective-permute-start | bytes 786440 | tf_op jit(solution)/shard_map/ppermute | solution.py:339
  17.7 4.0 %collective-permute-start.5 = (bf16[16,1024]{1,0:T(8,128)(2,1)S(1)}, bf16[16,1024]{1,0:T(8,128)(2,1)S(1)}, u32[]{:S(2)}, u32[]{:S(2)}) collective-permute-start(bf16[16,1024]{1,0:T(8,128)(2,1)S(1)} %slice.9), channel_id=1, source_target_pairs={{0,2},{1,3},{2,0},{3,1},{4,6},{5,7},{6,4},{7,5},{8,10},{9,11},{10,... | collective-permute-start | bytes 98312 | tf_op jit(solution)/shard_map/ppermute | solution.py:339
  21.7 57.3 %all-to-all-start = ((bf16[32,7,32,128]{3,2,1,0:T(8,128)(2,1)}), bf16[32,7,32,128]{3,2,1,0:T(8,128)(2,1)S(1)}, u32[]{:S(2)}, u32[]{:S(2)}) async-start(bf16[32,7,32,128]{3,2,1,0:T(8,128)(2,1)} %get-tuple-element.47), calls=%async_computation | async-start | bytes 3670016 | tf_op jit(solution)/shard_map/all_to_all | solution.py:411
  26.8 35.2 %collective-permute-start.12 = (bf16[112,1024]{1,0:T(8,128)(2,1)S(1)}, bf16[112,1024]{1,0:T(8,128)(2,1)S(1)}, u32[]{:S(2)}, u32[]{:S(2)}) collective-permute-start(bf16[112,1024]{1,0:T(8,128)(2,1)S(1)} %slice.11), channel_id=1, source_target_pairs={{0,2},{1,3},{2,0},{3,1},{4,6},{5,7},{6,4},{7,5},{8,10},{9,11},{10,... | collective-permute-start | bytes 688136 | tf_op jit(solution)/shard_map/ppermute | solution.py:339
  28.6 12.1 %collective-permute-start.6 = (bf16[256,128]{1,0:T(8,128)(2,1)S(1)}, bf16[256,128]{1,0:T(8,128)(2,1)S(1)}, u32[]{:S(2)}, u32[]{:S(2)}) collective-permute-start(bf16[256,128]{1,0:T(8,128)(2,1)S(1)} %get-tuple-element.87), channel_id=1, source_target_pairs={{0,8},{8,0},{16,24},{24,16},{1,9},{9,1},{17,25},{25,17},{2,10},{10... | collective-permute-start | bytes 196616 | tf_op jit(solution)/shard_map/ppermute | solution.py:339
  30.2 12.1 %collective-permute-start.7 = (bf16[256,128]{1,0:T(8,128)(2,1)S(1)}, bf16[256,128]{1,0:T(8,128)(2,1)S(1)}, u32[]{:S(2)}, u32[]{:S(2)}) collective-permute-start(bf16[256,128]{1,0:T(8,128)(2,1)S(1)} %get-tuple-element.86), channel_id=1, source_target_pairs={{0,16},{8,24},{16,0},{24,8},{1,17},{9,25},{17,1},{25,9},{2,18},{10... | collective-permute-start | bytes 196616 | tf_op jit(solution)/shard_map/ppermute | solution.py:339
  31.6 13.2 %collective-permute-start.8 = (bf16[256,128]{1,0:T(8,128)(2,1)S(1)}, bf16[256,128]{1,0:T(8,128)(2,1)S(1)}, u32[]{:S(2)}, u32[]{:S(2)}) collective-permute-start(bf16[256,128]{1,0:T(8,128)(2,1)S(1)} %get-tuple-element.85), channel_id=1, source_target_pairs={{0,24},{8,16},{16,8},{24,0},{1,25},{9,17},{17,9},{25,1},{2,26},{10... | collective-permute-start | bytes 196616 | tf_op jit(solution)/shard_map/ppermute | solution.py:339
  32.3 36.3 %collective-permute-start.10 = (bf16[256,1024]{1,0:T(8,128)(2,1)S(1)}, bf16[256,1024]{1,0:T(8,128)(2,1)S(1)}, u32[]{:S(2)}, u32[]{:S(2)}) collective-permute-start(bf16[256,1024]{1,0:T(8,128)(2,1)S(1)} %constant_dynamic-update-slice_fusion.refs_0_), channel_id=1, source_target_pairs={{0,8},{8,0},{16,24},{24,16},{1,9},{9,1},{17,25},{25,17},{2,10},{10... | collective-permute-start | bytes 1572872 | tf_op jit(solution)/shard_map/ppermute | solution.py:339
  40.8 27.8 %collective-permute-start.11 = (bf16[256,1024]{1,0:T(8,128)(2,1)S(1)}, bf16[256,1024]{1,0:T(8,128)(2,1)S(1)}, u32[]{:S(2)}, u32[]{:S(2)}) collective-permute-start(bf16[256,1024]{1,0:T(8,128)(2,1)S(1)} %constant_dynamic-update-slice_fusion.refs_0_), channel_id=1, source_target_pairs={{0,16},{8,24},{16,0},{24,8},{1,17},{9,25},{17,1},{25,9},{2,18},{10... | collective-permute-start | bytes 1572872 | tf_op jit(solution)/shard_map/ppermute | solution.py:339
  45.4 23.1 %collective-permute-start.9 = (f32[4,32,1024]{2,1,0:T(8,128)S(1)}, f32[4,32,1024]{2,1,0:T(8,128)S(1)}, u32[]{:S(2)}, u32[]{:S(2)}) collective-permute-start(f32[4,32,1024]{2,1,0:T(8,128)S(1)} %dynamic-slice_bitcast_fusion), channel_id=1, source_target_pairs={{0,1},{1,0},{2,3},{3,2},{4,5},{5,4},{6,7},{7,6},{8,9},{9,8},{10,11... | collective-permute-start | bytes 1572872 | tf_op jit(solution)/shard_map/ppermute | solution.py:339
  62.0 41.1 %copy-start.7 = (bf16[256,1024]{1,0:T(8,128)(2,1)}, bf16[256,1024]{1,0:T(8,128)(2,1)S(1)}, u32[]{:S(2)}) copy-start(bf16[256,1024]{1,0:T(8,128)(2,1)S(1)} %constant_dynamic-update-slice_fusion.2.refs_1_) | copy-start | bytes 1572868
  62.1 15.5 %collective-permute-start.13 = (bf16[256,1024]{1,0:T(8,128)(2,1)S(1)}, bf16[256,1024]{1,0:T(8,128)(2,1)S(1)}, u32[]{:S(2)}, u32[]{:S(2)}) collective-permute-start(bf16[256,1024]{1,0:T(8,128)(2,1)S(1)} %constant_dynamic-update-slice_fusion.2.refs_1_), channel_id=1, source_target_pairs={{0,8},{8,0},{16,24},{24,16},{1,9},{9,1},{17,25},{25,17},{2,10},{10... | collective-permute-start | bytes 1572872 | tf_op jit(solution)/shard_map/ppermute | solution.py:339
  63.8 15.1 %collective-permute-start.14 = (bf16[256,1024]{1,0:T(8,128)(2,1)S(1)}, bf16[256,1024]{1,0:T(8,128)(2,1)}, u32[]{:S(2)}, u32[]{:S(2)}) collective-permute-start(bf16[256,1024]{1,0:T(8,128)(2,1)S(1)} %constant_dynamic-update-slice_fusion.2.refs_1_), channel_id=1, source_target_pairs={{0,16},{8,24},{16,0},{24,8},{1,17},{9,25},{17,1},{25,9},{2,18},{10... | collective-permute-start | bytes 1572872 | tf_op jit(solution)/shard_map/ppermute | solution.py:339
  79.0 18.1 %collective-permute-start.19 = (bf16[256,1024]{1,0:T(8,128)(2,1)}, bf16[256,1024]{1,0:T(8,128)(2,1)}, u32[]{:S(2)}, u32[]{:S(2)}) collective-permute-start(bf16[256,1024]{1,0:T(8,128)(2,1)} %collective-permute-done.14.refs_5_), channel_id=1, source_target_pairs={{0,8},{8,0},{16,24},{24,16},{1,9},{9,1},{17,25},{25,17},{2,10},{10... | collective-permute-start | bytes 1572872 | tf_op jit(solution)/shard_map/ppermute | solution.py:339
  79.9 17.1 %collective-permute-start.18 = (bf16[256,1024]{1,0:T(8,128)(2,1)}, bf16[256,1024]{1,0:T(8,128)(2,1)}, u32[]{:S(2)}, u32[]{:S(2)}) collective-permute-start(bf16[256,1024]{1,0:T(8,128)(2,1)} %copy-done.11), channel_id=1, source_target_pairs={{0,16},{8,24},{16,0},{24,8},{1,17},{9,25},{17,1},{25,9},{2,18},{10... | collective-permute-start | bytes 1572872 | tf_op jit(solution)/shard_map/ppermute | solution.py:339
  81.4 15.6 %collective-permute-start.15 = (bf16[32,1024]{1,0:T(8,128)(2,1)S(1)}, bf16[32,1024]{1,0:T(8,128)(2,1)}, u32[]{:S(2)}, u32[]{:S(2)}) collective-permute-start(bf16[32,1024]{1,0:T(8,128)(2,1)S(1)} %get-tuple-element.83), channel_id=1, source_target_pairs={{0,2},{1,3},{2,0},{3,1},{4,6},{5,7},{6,4},{7,5},{8,10},{9,11},{10,... | collective-permute-start | bytes 196616 | tf_op jit(solution)/shard_map/ppermute | solution.py:339
  82.7 14.3 %collective-permute-start.16 = (bf16[32,1024]{1,0:T(8,128)(2,1)S(1)}, bf16[32,1024]{1,0:T(8,128)(2,1)}, u32[]{:S(2)}, u32[]{:S(2)}) collective-permute-start(bf16[32,1024]{1,0:T(8,128)(2,1)S(1)} %get-tuple-element.82), channel_id=1, source_target_pairs={{0,4},{1,5},{2,6},{3,7},{4,0},{5,1},{6,2},{7,3},{8,12},{9,13},{10,... | collective-permute-start | bytes 196616 | tf_op jit(solution)/shard_map/ppermute | solution.py:339
  84.2 12.8 %collective-permute-start.17 = (bf16[32,1024]{1,0:T(8,128)(2,1)S(1)}, bf16[32,1024]{1,0:T(8,128)(2,1)}, u32[]{:S(2)}, u32[]{:S(2)}) collective-permute-start(bf16[32,1024]{1,0:T(8,128)(2,1)S(1)} %get-tuple-element.81), channel_id=1, source_target_pairs={{0,6},{1,7},{2,4},{3,5},{4,2},{5,3},{6,0},{7,1},{8,14},{9,15},{10,... | collective-permute-start | bytes 196616 | tf_op jit(solution)/shard_map/ppermute | solution.py:339
  97.0 30.7 %all-to-all-start.1 = ((bf16[32,4,32,128]{3,2,1,0:T(8,128)(2,1)}), bf16[32,4,32,128]{3,2,1,0:T(8,128)(2,1)S(1)}, u32[]{:S(2)}, u32[]{:S(2)}) async-start(bf16[32,4,32,128]{3,2,1,0:T(8,128)(2,1)} %get-tuple-element.63), calls=%async_computation.1 | async-start | bytes 2097152 | tf_op jit(solution)/shard_map/all_to_all | solution.py:411
  100.2 2.2 %collective-permute-start.27 = (bf16[256,1024]{1,0:T(8,128)(2,1)}, bf16[256,1024]{1,0:T(8,128)(2,1)S(1)}, u32[]{:S(2)}, u32[]{:S(2)}) collective-permute-start(bf16[256,1024]{1,0:T(8,128)(2,1)} %collective-permute-done.19.refs_7_), channel_id=1, source_target_pairs={{0,1},{1,0},{2,3},{3,2},{4,5},{5,4},{6,7},{7,6},{8,9},{9,8},{10,11... | collective-permute-start | bytes 1572872 | tf_op jit(solution)/shard_map/ppermute | solution.py:339
  100.5 2.6 %collective-permute-start.26 = (bf16[256,1024]{1,0:T(8,128)(2,1)}, bf16[256,1024]{1,0:T(8,128)(2,1)S(1)}, u32[]{:S(2)}, u32[]{:S(2)}) collective-permute-start(bf16[256,1024]{1,0:T(8,128)(2,1)} %collective-permute-done.18.refs_6_), channel_id=1, source_target_pairs={{0,1},{1,0},{2,3},{3,2},{4,5},{5,4},{6,7},{7,6},{8,9},{9,8},{10,11... | collective-permute-start | bytes 1572872 | tf_op jit(solution)/shard_map/ppermute | solution.py:339
  100.7 3.9 %collective-permute-start.25 = (bf16[256,1024]{1,0:T(8,128)(2,1)}, bf16[256,1024]{1,0:T(8,128)(2,1)S(1)}, u32[]{:S(2)}, u32[]{:S(2)}) collective-permute-start(bf16[256,1024]{1,0:T(8,128)(2,1)} %collective-permute-done.14.refs_5_), channel_id=1, source_target_pairs={{0,1},{1,0},{2,3},{3,2},{4,5},{5,4},{6,7},{7,6},{8,9},{9,8},{10,11... | collective-permute-start | bytes 1572872 | tf_op jit(solution)/shard_map/ppermute | solution.py:339
  101.0 3.9 %collective-permute-start.24 = (bf16[256,1024]{1,0:T(8,128)(2,1)S(1)}, bf16[256,1024]{1,0:T(8,128)(2,1)S(1)}, u32[]{:S(2)}, u32[]{:S(2)}) collective-permute-start(bf16[256,1024]{1,0:T(8,128)(2,1)S(1)} %copy-done.14), channel_id=1, source_target_pairs={{0,1},{1,0},{2,3},{3,2},{4,5},{5,4},{6,7},{7,6},{8,9},{9,8},{10,11... | collective-permute-start | bytes 1572872 | tf_op jit(solution)/shard_map/ppermute | solution.py:339
  101.3 4.8 %collective-permute-start.23 = (bf16[256,1024]{1,0:T(8,128)(2,1)}, bf16[256,1024]{1,0:T(8,128)(2,1)S(1)}, u32[]{:S(2)}, u32[]{:S(2)}) collective-permute-start(bf16[256,1024]{1,0:T(8,128)(2,1)} %copy-done.15), channel_id=1, source_target_pairs={{0,1},{1,0},{2,3},{3,2},{4,5},{5,4},{6,7},{7,6},{8,9},{9,8},{10,11... | collective-permute-start | bytes 1572872 | tf_op jit(solution)/shard_map/ppermute | solution.py:339
  102.4 3.7 %collective-permute-start.22 = (bf16[256,1024]{1,0:T(8,128)(2,1)S(1)}, bf16[256,1024]{1,0:T(8,128)(2,1)S(1)}, u32[]{:S(2)}, u32[]{:S(2)}) collective-permute-start(bf16[256,1024]{1,0:T(8,128)(2,1)S(1)} %copy-done.12), channel_id=1, source_target_pairs={{0,1},{1,0},{2,3},{3,2},{4,5},{5,4},{6,7},{7,6},{8,9},{9,8},{10,11... | collective-permute-start | bytes 1572872 | tf_op jit(solution)/shard_map/ppermute | solution.py:339
  103.1 3.5 %collective-permute-start.21 = (bf16[256,1024]{1,0:T(8,128)(2,1)S(1)}, bf16[256,1024]{1,0:T(8,128)(2,1)S(1)}, u32[]{:S(2)}, u32[]{:S(2)}) collective-permute-start(bf16[256,1024]{1,0:T(8,128)(2,1)S(1)} %constant_dynamic-update-slice_fusion.2.refs_1_), channel_id=1, source_target_pairs={{0,1},{1,0},{2,3},{3,2},{4,5},{5,4},{6,7},{7,6},{8,9},{9,8},{10,11... | collective-permute-start | bytes 1572872 | tf_op jit(solution)/shard_map/ppermute | solution.py:339
  104.6 2.8 %collective-permute-start.20 = (bf16[256,1024]{1,0:T(8,128)(2,1)S(1)}, bf16[256,1024]{1,0:T(8,128)(2,1)S(1)}, u32[]{:S(2)}, u32[]{:S(2)}) collective-permute-start(bf16[256,1024]{1,0:T(8,128)(2,1)S(1)} %copy-done.9), channel_id=1, source_target_pairs={{0,1},{1,0},{2,3},{3,2},{4,5},{5,4},{6,7},{7,6},{8,9},{9,8},{10,11... | collective-permute-start | bytes 1572872 | tf_op jit(solution)/shard_map/ppermute | solution.py:339
  127.8 13.0 %all-to-all-start.2 = ((bf16[32,32,128]{2,1,0:T(8,128)(2,1)}), bf16[32,32,128]{2,1,0:T(8,128)(2,1)S(1)}, u32[]{:S(2)}, u32[]{:S(2)}) async-start(bf16[32,32,128]{2,1,0:T(8,128)(2,1)} %shard_map.167), calls=%async_computation.2 | async-start | bytes 524288 | tf_op jit(solution)/shard_map/all_to_all | solution.py:411
  (30 other events, 285.2 us)

commit v5 on v4

--- a/solution.py
+++ b/solution.py
@@ -127,7 +127,7 @@
 
 def correlate(spec_a, spec_b, spec_c, forward, backward):
     rows, cols = spec_a.shape[0], spec_a.shape[1] // 2
-    block = min(rows, 256)
+    block = min(rows, 512)
 
     def step(i, carry):
         at = pl.ds(pl.multiple_of(i * block, block), block)
@@ -143,7 +143,7 @@
             spec[at, :] = jnp.dot(mixed, backward[...], preferred_element_type=jnp.float32)
         return carry
 
-    lax.fori_loop(0, rows // block, step, 0)
+    lax.fori_loop(0, rows // block, step, 0, unroll=True)
 
 
 def fetch(sources, slots, done):

time: 143 us -> 141 us (0.986)
  Pallas kernels: 29.8 us -> 28 us
    pallas_call x5, Pallas kernels: 29.8 us -> 28 us  [on_chip(): pl.pallas_call(kernel, out_shape=out_shape, in_specs=[pl.BlockSpec(memory...]
  transfers between devices with their start and end apart: 31 -> 31, of which waited for: 16 -> 16; matrix products, arithmetic and copies ran while one was open for 4% -> 4% of each run, Pallas kernels for 20% -> 19%
where the time goes in v5:
time: 141 us; the launch traced here: 140 us
  waiting for transfers between devices  61.2 us (43%)
  starting transfers between devices  41 us (29%)
  Pallas kernels  28 us (20%)
  matrix products  3.66 us (3%)
  local copies, waits for them, and re-layouts  3.14 us (2%)
  other arithmetic  2.29 us (2%)
    ppermute x28, waiting for transfers between devices, swap(): lax.ppermute(block, axis, [(i, i ^ bit) for i in range(lax.axis_size(axis...  44 us
    ppermute x28, starting transfers between devices, swap(): lax.ppermute(block, axis, [(i, i ^ bit) for i in range(lax.axis_size(axis...  30.3 us
    pallas_call x5, Pallas kernels, on_chip(): pl.pallas_call(kernel, out_shape=out_shape, in_specs=[pl.BlockSpec(memory...  28 us
    all_to_all x3, waiting for transfers between devices, regroup(): return lax.all_to_all(x, AXES, split_axis=0, concat_axis=0, tiled=True)  17.1 us
    all_to_all x3, starting transfers between devices, regroup(): return lax.all_to_all(x, AXES, split_axis=0, concat_axis=0, tiled=True)  10.7 us
    dot_general x1, matrix products, shards(): lax.dot_general(late, w_in[:, 2 * width:], LAST, preferred_element_type=j...  3.22 us
    unnamed x64, local copies, waits for them, and re-layouts  2.98 us
  transfers between devices with their start and end apart: 31, of which 16 were waited for; matrix products, arithmetic and copies ran while one was open for 4% of the time, Pallas kernels for 19%

profile of v5, /device:TPU:0, one launch (start us, length us, event | category | flops | bytes accessed | tf_op | source)
XLA Modules:
  0.0 140.4 jit_solution(11433798814015771597)
XLA Ops:
  0.6 4.1 %collective-permute-start.4 = (bf16[128,1024]{1,0:T(8,128)(2,1)}, bf16[128,1024]{1,0:T(8,128)(2,1)S(1)}, u32[]{:S(2)}, u32[]{:S(2)}) collective-permute-start(bf16[128,1024]{1,0:T(8,128)(2,1)} %block_in.1), channel_id=1, source_target_pairs={{0,4},{1,5},{2,6},{3,7},{4,0},{5,1},{6,2},{7,3},{8,12},{9,13},{10,... | collective-permute-start | bytes 786440 | tf_op jit(solution)/shard_map/ppermute | solution.py:339
  4.7 1.5 %collective-permute-start = (bf16[128,1024]{1,0:T(8,128)(2,1)}, bf16[128,1024]{1,0:T(8,128)(2,1)S(1)}, u32[]{:S(2)}, u32[]{:S(2)}) collective-permute-start(bf16[128,1024]{1,0:T(8,128)(2,1)} %out_cot.1), channel_id=1, source_target_pairs={{0,8},{8,0},{16,24},{24,16},{1,9},{9,1},{17,25},{25,17},{2,10},{10... | collective-permute-start | bytes 786440 | tf_op jit(solution)/shard_map/ppermute | solution.py:339
  6.2 1.5 %collective-permute-start.1 = (bf16[128,1024]{1,0:T(8,128)(2,1)}, bf16[128,1024]{1,0:T(8,128)(2,1)S(1)}, u32[]{:S(2)}, u32[]{:S(2)}) collective-permute-start(bf16[128,1024]{1,0:T(8,128)(2,1)} %out_cot.1), channel_id=1, source_target_pairs={{0,16},{8,24},{16,0},{24,8},{1,17},{9,25},{17,1},{25,9},{2,18},{10... | collective-permute-start | bytes 786440 | tf_op jit(solution)/shard_map/ppermute | solution.py:339
  8.2 1.6 %collective-permute-start.3 = (bf16[128,1024]{1,0:T(8,128)(2,1)}, bf16[128,1024]{1,0:T(8,128)(2,1)S(1)}, u32[]{:S(2)}, u32[]{:S(2)}) collective-permute-start(bf16[128,1024]{1,0:T(8,128)(2,1)} %block_in.1), channel_id=1, source_target_pairs={{0,2},{1,3},{2,0},{3,1},{4,6},{5,7},{6,4},{7,5},{8,10},{9,11},{10,... | collective-permute-start | bytes 786440 | tf_op jit(solution)/shard_map/ppermute | solution.py:339
  10.4 7.3 %shard_map.164 = (bf16[32,7,32,128]{3,2,1,0:T(8,128)(2,1)}, bf16[1024,128]{1,0:T(8,128)(2,1)}, bf16[128,1024]{1,0:T(8,128)(2,1)}) custom-call(bf16[128,128]{1,0:T(8,128)(2,1)} %fusion.20.square, bf16[128,1024]{1,0:T(8,128)(2,1)} %conv_one.1, bf16[128,1024]{1,0:T(8,128)(2,1)} %filter_two.1, bf16[128,1024]{1,0:T(8,128)(2,1)} %filter_one.1, ...), custom_call_target="tpu_custom_call" | custom-call | tf_op jit(solution)/shard_map/pallas_call | solution.py:272
  20.3 1.4 collective-permute-done.5
  21.7 5.0 %all-to-all-start = ((bf16[32,7,32,128]{3,2,1,0:T(8,128)(2,1)}), bf16[32,7,32,128]{3,2,1,0:T(8,128)(2,1)S(1)}, u32[]{:S(2)}, u32[]{:S(2)}) async-start(bf16[32,7,32,128]{3,2,1,0:T(8,128)(2,1)} %get-tuple-element.47), calls=%async_computation | async-start | bytes 3670016 | tf_op jit(solution)/shard_map/all_to_all | solution.py:411
  26.8 1.8 %collective-permute-start.12 = (bf16[112,1024]{1,0:T(8,128)(2,1)S(1)}, bf16[112,1024]{1,0:T(8,128)(2,1)S(1)}, u32[]{:S(2)}, u32[]{:S(2)}) collective-permute-start(bf16[112,1024]{1,0:T(8,128)(2,1)S(1)} %slice.11), channel_id=1, source_target_pairs={{0,2},{1,3},{2,0},{3,1},{4,6},{5,7},{6,4},{7,5},{8,10},{9,11},{10,... | collective-permute-start | bytes 688136 | tf_op jit(solution)/shard_map/ppermute | solution.py:339
  28.6 1.5 %collective-permute-start.6 = (bf16[256,128]{1,0:T(8,128)(2,1)S(1)}, bf16[256,128]{1,0:T(8,128)(2,1)S(1)}, u32[]{:S(2)}, u32[]{:S(2)}) collective-permute-start(bf16[256,128]{1,0:T(8,128)(2,1)S(1)} %get-tuple-element.87), channel_id=1, source_target_pairs={{0,8},{8,0},{16,24},{24,16},{1,9},{9,1},{17,25},{25,17},{2,10},{10... | collective-permute-start | bytes 196616 | tf_op jit(solution)/shard_map/ppermute | solution.py:339
  30.2 1.5 %collective-permute-start.7 = (bf16[256,128]{1,0:T(8,128)(2,1)S(1)}, bf16[256,128]{1,0:T(8,128)(2,1)S(1)}, u32[]{:S(2)}, u32[]{:S(2)}) collective-permute-start(bf16[256,128]{1,0:T(8,128)(2,1)S(1)} %get-tuple-element.86), channel_id=1, source_target_pairs={{0,16},{8,24},{16,0},{24,8},{1,17},{9,25},{17,1},{25,9},{2,18},{10... | collective-permute-start | bytes 196616 | tf_op jit(solution)/shard_map/ppermute | solution.py:339
  32.3 1.5 %collective-permute-start.10 = (bf16[256,1024]{1,0:T(8,128)(2,1)S(1)}, bf16[256,1024]{1,0:T(8,128)(2,1)S(1)}, u32[]{:S(2)}, u32[]{:S(2)}) collective-permute-start(bf16[256,1024]{1,0:T(8,128)(2,1)S(1)} %constant_dynamic-update-slice_fusion.refs_0_), channel_id=1, source_target_pairs={{0,8},{8,0},{16,24},{24,16},{1,9},{9,1},{17,25},{25,17},{2,10},{10... | collective-permute-start | bytes 1572872 | tf_op jit(solution)/shard_map/ppermute | solution.py:339
  33.8 7.0 %collective-permute-done.6 = bf16[256,128]{1,0:T(8,128)(2,1)S(1)} collective-permute-done((bf16[256,128]{1,0:T(8,128)(2,1)S(1)}, bf16[256,128]{1,0:T(8,128)(2,1)S(1)}, u32[]{:S(2)}, u32[]{:S(2)}) %collective-permute-start.6) | collective-permute-done | bytes 65568 | tf_op jit(solution)/shard_map/ppermute | solution.py:339
  40.8 1.5 %collective-permute-start.11 = (bf16[256,1024]{1,0:T(8,128)(2,1)S(1)}, bf16[256,1024]{1,0:T(8,128)(2,1)S(1)}, u32[]{:S(2)}, u32[]{:S(2)}) collective-permute-start(bf16[256,1024]{1,0:T(8,128)(2,1)S(1)} %constant_dynamic-update-slice_fusion.refs_0_), channel_id=1, source_target_pairs={{0,16},{8,24},{16,0},{24,8},{1,17},{9,25},{17,1},{25,9},{2,18},{10... | collective-permute-start | bytes 1572872 | tf_op jit(solution)/shard_map/ppermute | solution.py:339
  42.2 2.6 %collective-permute-done.8 = bf16[256,128]{1,0:T(8,128)(2,1)S(1)} collective-permute-done((bf16[256,128]{1,0:T(8,128)(2,1)S(1)}, bf16[256,128]{1,0:T(8,128)(2,1)S(1)}, u32[]{:S(2)}, u32[]{:S(2)}) %collective-permute-start.8) | collective-permute-done | bytes 65568 | tf_op jit(solution)/shard_map/ppermute | solution.py:339
  45.5 16.5 %collective-permute-done.12 = bf16[112,1024]{1,0:T(8,128)(2,1)S(1)} collective-permute-done((bf16[112,1024]{1,0:T(8,128)(2,1)S(1)}, bf16[112,1024]{1,0:T(8,128)(2,1)S(1)}, u32[]{:S(2)}, u32[]{:S(2)}) %collective-permute-start.12) | collective-permute-done | bytes 229408 | tf_op jit(solution)/shard_map/ppermute | solution.py:339
  62.1 1.7 %collective-permute-start.13 = (bf16[256,1024]{1,0:T(8,128)(2,1)S(1)}, bf16[256,1024]{1,0:T(8,128)(2,1)S(1)}, u32[]{:S(2)}, u32[]{:S(2)}) collective-permute-start(bf16[256,1024]{1,0:T(8,128)(2,1)S(1)} %constant_dynamic-update-slice_fusion.2.refs_1_), channel_id=1, source_target_pairs={{0,8},{8,0},{16,24},{24,16},{1,9},{9,1},{17,25},{25,17},{2,10},{10... | collective-permute-start | bytes 1572872 | tf_op jit(solution)/shard_map/ppermute | solution.py:339
  63.8 1.5 %collective-permute-start.14 = (bf16[256,1024]{1,0:T(8,128)(2,1)S(1)}, bf16[256,1024]{1,0:T(8,128)(2,1)}, u32[]{:S(2)}, u32[]{:S(2)}) collective-permute-start(bf16[256,1024]{1,0:T(8,128)(2,1)S(1)} %constant_dynamic-update-slice_fusion.2.refs_1_), channel_id=1, source_target_pairs={{0,16},{8,24},{16,0},{24,8},{1,17},{9,25},{17,1},{25,9},{2,18},{10... | collective-permute-start | bytes 1572872 | tf_op jit(solution)/shard_map/ppermute | solution.py:339
  65.3 3.2 %fusion.part = f32[128,1024]{1,0:T(8,128)} fusion(bf16[128,1024]{1,0:T(8,128)(2,1)S(1)} %copy-done.26, bf16[1024,3072]{1,0:T(8,128)(2,1)} %w_in.3), kind=kOutput, calls=%fused_computation | convolution fusion | flops 268435456 | bytes 2883584 | tf_op jit(solution)/shard_map/dot_general | solution.py:444
  68.6 9.0 %collective-permute-done.13.refs_3_ = bf16[256,1024]{1,0:T(8,128)(2,1)S(1)} collective-permute-done((bf16[256,1024]{1,0:T(8,128)(2,1)S(1)}, bf16[256,1024]{1,0:T(8,128)(2,1)S(1)}, u32[]{:S(2)}, u32[]{:S(2)}) %collective-permute-start.13) | collective-permute-done | bytes 524320 | tf_op jit(solution)/shard_map/ppermute | solution.py:339
  79.9 1.5 %collective-permute-start.18 = (bf16[256,1024]{1,0:T(8,128)(2,1)}, bf16[256,1024]{1,0:T(8,128)(2,1)}, u32[]{:S(2)}, u32[]{:S(2)}) collective-permute-start(bf16[256,1024]{1,0:T(8,128)(2,1)} %copy-done.11), channel_id=1, source_target_pairs={{0,16},{8,24},{16,0},{24,8},{1,17},{9,25},{17,1},{25,9},{2,18},{10... | collective-permute-start | bytes 1572872 | tf_op jit(solution)/shard_map/ppermute | solution.py:339
  81.4 1.3 collective-permute-start.15
  82.7 1.4 %collective-permute-start.16 = (bf16[32,1024]{1,0:T(8,128)(2,1)S(1)}, bf16[32,1024]{1,0:T(8,128)(2,1)}, u32[]{:S(2)}, u32[]{:S(2)}) collective-permute-start(bf16[32,1024]{1,0:T(8,128)(2,1)S(1)} %get-tuple-element.82), channel_id=1, source_target_pairs={{0,4},{1,5},{2,6},{3,7},{4,0},{5,1},{6,2},{7,3},{8,12},{9,13},{10,... | collective-permute-start | bytes 196616 | tf_op jit(solution)/shard_map/ppermute | solution.py:339
  84.2 1.7 %collective-permute-start.17 = (bf16[32,1024]{1,0:T(8,128)(2,1)S(1)}, bf16[32,1024]{1,0:T(8,128)(2,1)}, u32[]{:S(2)}, u32[]{:S(2)}) collective-permute-start(bf16[32,1024]{1,0:T(8,128)(2,1)S(1)} %get-tuple-element.81), channel_id=1, source_target_pairs={{0,6},{1,7},{2,4},{3,5},{4,2},{5,3},{6,0},{7,1},{8,14},{9,15},{10,... | collective-permute-start | bytes 196616 | tf_op jit(solution)/shard_map/ppermute | solution.py:339
  85.9 8.3 %shard_map.165 = (bf16[32,4,32,128]{3,2,1,0:T(8,128)(2,1)}, bf16[128,4096]{1,0:T(8,128)(2,1)S(1)}) custom-call(s32[1]{0:T(128)} %bitcast.me, bf16[32,7,32,128]{3,2,1,0:T(8,128)(2,1)S(1)} %all-to-all-done.here, bf16[256,256]{1,0:T(8,128)(2,1)S(1)} %copy-done.2, bf16[256,256]{1,0:T(8,128)(2,1)S(1)} %copy-done.3, f32[256,128]{1,0:T(8,128)S(1)} %copy-done.4, ...), custom_call_target="tpu_custom_call" | custom-call | tf_op jit(solution)/shard_map/pallas_call | solution.py:272
  95.3 3.1 %all-to-all-start.1 = ((bf16[32,4,32,128]{3,2,1,0:T(8,128)(2,1)}), bf16[32,4,32,128]{3,2,1,0:T(8,128)(2,1)S(1)}, u32[]{:S(2)}, u32[]{:S(2)}) async-start(bf16[32,4,32,128]{3,2,1,0:T(8,128)(2,1)} %get-tuple-element.63), calls=%async_computation.1 | async-start | bytes 2097152 | tf_op jit(solution)/shard_map/all_to_all | solution.py:411
  106.6 5.7 %shard_map.167 = bf16[32,32,128]{2,1,0:T(8,128)(2,1)} custom-call(bf16[128,4096]{1,0:T(8,128)(2,1)} %copy-done, bf16[256,1024]{1,0:T(8,128)(2,1)} %copy-done.8, bf16[256,1024]{1,0:T(8,128)(2,1)} %copy-done.7, bf16[256,1024]{1,0:T(8,128)(2,1)} %copy-done.11, bf16[256,1024]{1,0:T(8,128)(2,1)} %copy-done.15, bf16[256,1024]{1,0:T(8,128)(2,1)} %copy-done.13, ...), custom_call_target="tpu_custom_call" | custom-call | tf_op jit(solution)/shard_map/pallas_call | solution.py:272
  112.3 13.7 %all-to-all-done.1.home = bf16[32,4,32,128]{3,2,1,0:T(8,128)(2,1)S(1)} async-done(((bf16[32,4,32,128]{3,2,1,0:T(8,128)(2,1)}), bf16[32,4,32,128]{3,2,1,0:T(8,128)(2,1)S(1)}, u32[]{:S(2)}, u32[]{:S(2)}) %all-to-all-start.1) | async-done | bytes 1048608 | tf_op jit(solution)/shard_map/all_to_all | solution.py:411
  126.0 2.6 %all-to-all-start.2 = ((bf16[32,32,128]{2,1,0:T(8,128)(2,1)}), bf16[32,32,128]{2,1,0:T(8,128)(2,1)S(1)}, u32[]{:S(2)}, u32[]{:S(2)}) async-start(bf16[32,32,128]{2,1,0:T(8,128)(2,1)} %shard_map.167), calls=%async_computation.2 | async-start | bytes 524288 | tf_op jit(solution)/shard_map/all_to_all | solution.py:411
  128.6 1.6 %add_multiply_fusion = f32[32,1024]{1,0:T(8,128)} fusion(bf16[32,1024]{1,0:T(8,128)(2,1)} %collective-permute-done.17, bf16[32,1024]{1,0:T(8,128)(2,1)} %collective-permute-done.16, f32[32,1024]{1,0:T(8,128)S(1)} %dynamic-slice_bitcast_fusion.1, bf16[32,1024]{1,0:T(8,128)(2,1)} %collective-permute-done.15), kind=kLoop, calls=%fused_computation.20 | loop fusion | flops 229376 | bytes 458752 | tf_op jit(solution)/shard_map/mul | solution.py:466
  130.2 5.3 %shard_map.166 = (bf16[128,1024]{1,0:T(8,128)(2,1)}, bf16[128,1024]{1,0:T(8,128)(2,1)}, bf16[128,1024]{1,0:T(8,128)(2,1)}) custom-call(bf16[128,128]{1,0:T(8,128)(2,1)} %fusion.20.square, bf16[32,4,32,128]{3,2,1,0:T(8,128)(2,1)} %copy-done.6, f32[128,1024]{1,0:T(8,128)} %fusion.part, bf16[1024,3072]{1,0:T(8,128)(2,1)} %w_in.3), custom_call_target="tpu_custom_call" | custom-call | tf_op jit(solution)/shard_map/pallas_call | solution.py:272
  135.5 3.4 %all-to-all-done.2.taken = bf16[32,32,128]{2,1,0:T(8,128)(2,1)S(1)} async-done(((bf16[32,32,128]{2,1,0:T(8,128)(2,1)}), bf16[32,32,128]{2,1,0:T(8,128)(2,1)S(1)}, u32[]{:S(2)}, u32[]{:S(2)}) %all-to-all-start.2) | async-done | bytes 262176 | tf_op jit(solution)/shard_map/all_to_all | solution.py:411
  139.0 1.4 %shard_map.168 = f32[32,3072]{1,0:T(8,128)} custom-call(bf16[32,32,128]{2,1,0:T(8,128)(2,1)S(1)} %all-to-all-done.2.taken, bf16[4,128,384]{2,1,0:T(8,128)(2,1)S(1)} %copy-done.1), custom_call_target="tpu_custom_call" | custom-call | tf_op jit(solution)/shard_map/pallas_call | solution.py:272
  (113 shorter events, 16.6 us)
Async XLA Ops:
  0.6 17.1 %collective-permute-start.4 = (bf16[128,1024]{1,0:T(8,128)(2,1)}, bf16[128,1024]{1,0:T(8,128)(2,1)S(1)}, u32[]{:S(2)}, u32[]{:S(2)}) collective-permute-start(bf16[128,1024]{1,0:T(8,128)(2,1)} %block_in.1), channel_id=1, source_target_pairs={{0,4},{1,5},{2,6},{3,7},{4,0},{5,1},{6,2},{7,3},{8,12},{9,13},{10,... | collective-permute-start | bytes 786440 | tf_op jit(solution)/shard_map/ppermute | solution.py:339
  4.7 13.5 %collective-permute-start = (bf16[128,1024]{1,0:T(8,128)(2,1)}, bf16[128,1024]{1,0:T(8,128)(2,1)S(1)}, u32[]{:S(2)}, u32[]{:S(2)}) collective-permute-start(bf16[128,1024]{1,0:T(8,128)(2,1)} %out_cot.1), channel_id=1, source_target_pairs={{0,8},{8,0},{16,24},{24,16},{1,9},{9,1},{17,25},{25,17},{2,10},{10... | collective-permute-start | bytes 786440 | tf_op jit(solution)/shard_map/ppermute | solution.py:339
  6.2 13.3 %collective-permute-start.1 = (bf16[128,1024]{1,0:T(8,128)(2,1)}, bf16[128,1024]{1,0:T(8,128)(2,1)S(1)}, u32[]{:S(2)}, u32[]{:S(2)}) collective-permute-start(bf16[128,1024]{1,0:T(8,128)(2,1)} %out_cot.1), channel_id=1, source_target_pairs={{0,16},{8,24},{16,0},{24,8},{1,17},{9,25},{17,1},{25,9},{2,18},{10... | collective-permute-start | bytes 786440 | tf_op jit(solution)/shard_map/ppermute | solution.py:339
  7.7 11.8 %collective-permute-start.2 = (bf16[128,1024]{1,0:T(8,128)(2,1)}, bf16[128,1024]{1,0:T(8,128)(2,1)S(1)}, u32[]{:S(2)}, u32[]{:S(2)}) collective-permute-start(bf16[128,1024]{1,0:T(8,128)(2,1)} %out_cot.1), channel_id=1, source_target_pairs={{0,24},{8,16},{16,8},{24,0},{1,25},{9,17},{17,9},{25,1},{2,26},{10... | collective-permute-start | bytes 786440 | tf_op jit(solution)/shard_map/ppermute | solution.py:339
  8.2 11.9 %collective-permute-start.3 = (bf16[128,1024]{1,0:T(8,128)(2,1)}, bf16[128,1024]{1,0:T(8,128)(2,1)S(1)}, u32[]{:S(2)}, u32[]{:S(2)}) collective-permute-start(bf16[128,1024]{1,0:T(8,128)(2,1)} %block_in.1), channel_id=1, source_target_pairs={{0,2},{1,3},{2,0},{3,1},{4,6},{5,7},{6,4},{7,5},{8,10},{9,11},{10,... | collective-permute-start | bytes 786440 | tf_op jit(solution)/shard_map/ppermute | solution.py:339
  17.7 4.0 %collective-permute-start.5 = (bf16[16,1024]{1,0:T(8,128)(2,1)S(1)}, bf16[16,1024]{1,0:T(8,128)(2,1)S(1)}, u32[]{:S(2)}, u32[]{:S(2)}) collective-permute-start(bf16[16,1024]{1,0:T(8,128)(2,1)S(1)} %slice.9), channel_id=1, source_target_pairs={{0,2},{1,3},{2,0},{3,1},{4,6},{5,7},{6,4},{7,5},{8,10},{9,11},{10,... | collective-permute-start | bytes 98312 | tf_op jit(solution)/shard_map/ppermute | solution.py:339
  21.7 57.3 %all-to-all-start = ((bf16[32,7,32,128]{3,2,1,0:T(8,128)(2,1)}), bf16[32,7,32,128]{3,2,1,0:T(8,128)(2,1)S(1)}, u32[]{:S(2)}, u32[]{:S(2)}) async-start(bf16[32,7,32,128]{3,2,1,0:T(8,128)(2,1)} %get-tuple-element.47), calls=%async_computation | async-start | bytes 3670016 | tf_op jit(solution)/shard_map/all_to_all | solution.py:411
  26.8 35.2 %collective-permute-start.12 = (bf16[112,1024]{1,0:T(8,128)(2,1)S(1)}, bf16[112,1024]{1,0:T(8,128)(2,1)S(1)}, u32[]{:S(2)}, u32[]{:S(2)}) collective-permute-start(bf16[112,1024]{1,0:T(8,128)(2,1)S(1)} %slice.11), channel_id=1, source_target_pairs={{0,2},{1,3},{2,0},{3,1},{4,6},{5,7},{6,4},{7,5},{8,10},{9,11},{10,... | collective-permute-start | bytes 688136 | tf_op jit(solution)/shard_map/ppermute | solution.py:339
  28.6 12.1 %collective-permute-start.6 = (bf16[256,128]{1,0:T(8,128)(2,1)S(1)}, bf16[256,128]{1,0:T(8,128)(2,1)S(1)}, u32[]{:S(2)}, u32[]{:S(2)}) collective-permute-start(bf16[256,128]{1,0:T(8,128)(2,1)S(1)} %get-tuple-element.87), channel_id=1, source_target_pairs={{0,8},{8,0},{16,24},{24,16},{1,9},{9,1},{17,25},{25,17},{2,10},{10... | collective-permute-start | bytes 196616 | tf_op jit(solution)/shard_map/ppermute | solution.py:339
  30.2 12.1 %collective-permute-start.7 = (bf16[256,128]{1,0:T(8,128)(2,1)S(1)}, bf16[256,128]{1,0:T(8,128)(2,1)S(1)}, u32[]{:S(2)}, u32[]{:S(2)}) collective-permute-start(bf16[256,128]{1,0:T(8,128)(2,1)S(1)} %get-tuple-element.86), channel_id=1, source_target_pairs={{0,16},{8,24},{16,0},{24,8},{1,17},{9,25},{17,1},{25,9},{2,18},{10... | collective-permute-start | bytes 196616 | tf_op jit(solution)/shard_map/ppermute | solution.py:339
  31.6 13.2 %collective-permute-start.8 = (bf16[256,128]{1,0:T(8,128)(2,1)S(1)}, bf16[256,128]{1,0:T(8,128)(2,1)S(1)}, u32[]{:S(2)}, u32[]{:S(2)}) collective-permute-start(bf16[256,128]{1,0:T(8,128)(2,1)S(1)} %get-tuple-element.85), channel_id=1, source_target_pairs={{0,24},{8,16},{16,8},{24,0},{1,25},{9,17},{17,9},{25,1},{2,26},{10... | collective-permute-start | bytes 196616 | tf_op jit(solution)/shard_map/ppermute | solution.py:339
  32.3 36.3 %collective-permute-start.10 = (bf16[256,1024]{1,0:T(8,128)(2,1)S(1)}, bf16[256,1024]{1,0:T(8,128)(2,1)S(1)}, u32[]{:S(2)}, u32[]{:S(2)}) collective-permute-start(bf16[256,1024]{1,0:T(8,128)(2,1)S(1)} %constant_dynamic-update-slice_fusion.refs_0_), channel_id=1, source_target_pairs={{0,8},{8,0},{16,24},{24,16},{1,9},{9,1},{17,25},{25,17},{2,10},{10... | collective-permute-start | bytes 1572872 | tf_op jit(solution)/shard_map/ppermute | solution.py:339
  40.8 27.8 %collective-permute-start.11 = (bf16[256,1024]{1,0:T(8,128)(2,1)S(1)}, bf16[256,1024]{1,0:T(8,128)(2,1)S(1)}, u32[]{:S(2)}, u32[]{:S(2)}) collective-permute-start(bf16[256,1024]{1,0:T(8,128)(2,1)S(1)} %constant_dynamic-update-slice_fusion.refs_0_), channel_id=1, source_target_pairs={{0,16},{8,24},{16,0},{24,8},{1,17},{9,25},{17,1},{25,9},{2,18},{10... | collective-permute-start | bytes 1572872 | tf_op jit(solution)/shard_map/ppermute | solution.py:339
  45.4 23.1 %collective-permute-start.9 = (f32[4,32,1024]{2,1,0:T(8,128)S(1)}, f32[4,32,1024]{2,1,0:T(8,128)S(1)}, u32[]{:S(2)}, u32[]{:S(2)}) collective-permute-start(f32[4,32,1024]{2,1,0:T(8,128)S(1)} %dynamic-slice_bitcast_fusion), channel_id=1, source_target_pairs={{0,1},{1,0},{2,3},{3,2},{4,5},{5,4},{6,7},{7,6},{8,9},{9,8},{10,11... | collective-permute-start | bytes 1572872 | tf_op jit(solution)/shard_map/ppermute | solution.py:339
  62.0 39.3 %copy-start.7 = (bf16[256,1024]{1,0:T(8,128)(2,1)}, bf16[256,1024]{1,0:T(8,128)(2,1)S(1)}, u32[]{:S(2)}) copy-start(bf16[256,1024]{1,0:T(8,128)(2,1)S(1)} %constant_dynamic-update-slice_fusion.2.refs_1_) | copy-start | bytes 1572868
  62.1 15.5 %collective-permute-start.13 = (bf16[256,1024]{1,0:T(8,128)(2,1)S(1)}, bf16[256,1024]{1,0:T(8,128)(2,1)S(1)}, u32[]{:S(2)}, u32[]{:S(2)}) collective-permute-start(bf16[256,1024]{1,0:T(8,128)(2,1)S(1)} %constant_dynamic-update-slice_fusion.2.refs_1_), channel_id=1, source_target_pairs={{0,8},{8,0},{16,24},{24,16},{1,9},{9,1},{17,25},{25,17},{2,10},{10... | collective-permute-start | bytes 1572872 | tf_op jit(solution)/shard_map/ppermute | solution.py:339
  63.8 15.1 %collective-permute-start.14 = (bf16[256,1024]{1,0:T(8,128)(2,1)S(1)}, bf16[256,1024]{1,0:T(8,128)(2,1)}, u32[]{:S(2)}, u32[]{:S(2)}) collective-permute-start(bf16[256,1024]{1,0:T(8,128)(2,1)S(1)} %constant_dynamic-update-slice_fusion.2.refs_1_), channel_id=1, source_target_pairs={{0,16},{8,24},{16,0},{24,8},{1,17},{9,25},{17,1},{25,9},{2,18},{10... | collective-permute-start | bytes 1572872 | tf_op jit(solution)/shard_map/ppermute | solution.py:339
  79.0 16.3 %collective-permute-start.19 = (bf16[256,1024]{1,0:T(8,128)(2,1)}, bf16[256,1024]{1,0:T(8,128)(2,1)}, u32[]{:S(2)}, u32[]{:S(2)}) collective-permute-start(bf16[256,1024]{1,0:T(8,128)(2,1)} %collective-permute-done.14.refs_5_), channel_id=1, source_target_pairs={{0,8},{8,0},{16,24},{24,16},{1,9},{9,1},{17,25},{25,17},{2,10},{10... | collective-permute-start | bytes 1572872 | tf_op jit(solution)/shard_map/ppermute | solution.py:339
  79.9 15.3 %collective-permute-start.18 = (bf16[256,1024]{1,0:T(8,128)(2,1)}, bf16[256,1024]{1,0:T(8,128)(2,1)}, u32[]{:S(2)}, u32[]{:S(2)}) collective-permute-start(bf16[256,1024]{1,0:T(8,128)(2,1)} %copy-done.11), channel_id=1, source_target_pairs={{0,16},{8,24},{16,0},{24,8},{1,17},{9,25},{17,1},{25,9},{2,18},{10... | collective-permute-start | bytes 1572872 | tf_op jit(solution)/shard_map/ppermute | solution.py:339
  81.4 13.8 %collective-permute-start.15 = (bf16[32,1024]{1,0:T(8,128)(2,1)S(1)}, bf16[32,1024]{1,0:T(8,128)(2,1)}, u32[]{:S(2)}, u32[]{:S(2)}) collective-permute-start(bf16[32,1024]{1,0:T(8,128)(2,1)S(1)} %get-tuple-element.83), channel_id=1, source_target_pairs={{0,2},{1,3},{2,0},{3,1},{4,6},{5,7},{6,4},{7,5},{8,10},{9,11},{10,... | collective-permute-start | bytes 196616 | tf_op jit(solution)/shard_map/ppermute | solution.py:339
  82.7 12.5 %collective-permute-start.16 = (bf16[32,1024]{1,0:T(8,128)(2,1)S(1)}, bf16[32,1024]{1,0:T(8,128)(2,1)}, u32[]{:S(2)}, u32[]{:S(2)}) collective-permute-start(bf16[32,1024]{1,0:T(8,128)(2,1)S(1)} %get-tuple-element.82), channel_id=1, source_target_pairs={{0,4},{1,5},{2,6},{3,7},{4,0},{5,1},{6,2},{7,3},{8,12},{9,13},{10,... | collective-permute-start | bytes 196616 | tf_op jit(solution)/shard_map/ppermute | solution.py:339
  84.2 11.1 %collective-permute-start.17 = (bf16[32,1024]{1,0:T(8,128)(2,1)S(1)}, bf16[32,1024]{1,0:T(8,128)(2,1)}, u32[]{:S(2)}, u32[]{:S(2)}) collective-permute-start(bf16[32,1024]{1,0:T(8,128)(2,1)S(1)} %get-tuple-element.81), channel_id=1, source_target_pairs={{0,6},{1,7},{2,4},{3,5},{4,2},{5,3},{6,0},{7,1},{8,14},{9,15},{10,... | collective-permute-start | bytes 196616 | tf_op jit(solution)/shard_map/ppermute | solution.py:339
  95.3 30.7 %all-to-all-start.1 = ((bf16[32,4,32,128]{3,2,1,0:T(8,128)(2,1)}), bf16[32,4,32,128]{3,2,1,0:T(8,128)(2,1)S(1)}, u32[]{:S(2)}, u32[]{:S(2)}) async-start(bf16[32,4,32,128]{3,2,1,0:T(8,128)(2,1)} %get-tuple-element.63), calls=%async_computation.1 | async-start | bytes 2097152 | tf_op jit(solution)/shard_map/all_to_all | solution.py:411
  98.4 2.2 %collective-permute-start.27 = (bf16[256,1024]{1,0:T(8,128)(2,1)}, bf16[256,1024]{1,0:T(8,128)(2,1)S(1)}, u32[]{:S(2)}, u32[]{:S(2)}) collective-permute-start(bf16[256,1024]{1,0:T(8,128)(2,1)} %collective-permute-done.19.refs_7_), channel_id=1, source_target_pairs={{0,1},{1,0},{2,3},{3,2},{4,5},{5,4},{6,7},{7,6},{8,9},{9,8},{10,11... | collective-permute-start | bytes 1572872 | tf_op jit(solution)/shard_map/ppermute | solution.py:339
  98.7 2.6 %collective-permute-start.26 = (bf16[256,1024]{1,0:T(8,128)(2,1)}, bf16[256,1024]{1,0:T(8,128)(2,1)S(1)}, u32[]{:S(2)}, u32[]{:S(2)}) collective-permute-start(bf16[256,1024]{1,0:T(8,128)(2,1)} %collective-permute-done.18.refs_6_), channel_id=1, source_target_pairs={{0,1},{1,0},{2,3},{3,2},{4,5},{5,4},{6,7},{7,6},{8,9},{9,8},{10,11... | collective-permute-start | bytes 1572872 | tf_op jit(solution)/shard_map/ppermute | solution.py:339
  99.0 3.9 %collective-permute-start.25 = (bf16[256,1024]{1,0:T(8,128)(2,1)}, bf16[256,1024]{1,0:T(8,128)(2,1)S(1)}, u32[]{:S(2)}, u32[]{:S(2)}) collective-permute-start(bf16[256,1024]{1,0:T(8,128)(2,1)} %collective-permute-done.14.refs_5_), channel_id=1, source_target_pairs={{0,1},{1,0},{2,3},{3,2},{4,5},{5,4},{6,7},{7,6},{8,9},{9,8},{10,11... | collective-permute-start | bytes 1572872 | tf_op jit(solution)/shard_map/ppermute | solution.py:339
  99.2 3.9 %collective-permute-start.24 = (bf16[256,1024]{1,0:T(8,128)(2,1)S(1)}, bf16[256,1024]{1,0:T(8,128)(2,1)S(1)}, u32[]{:S(2)}, u32[]{:S(2)}) collective-permute-start(bf16[256,1024]{1,0:T(8,128)(2,1)S(1)} %copy-done.14), channel_id=1, source_target_pairs={{0,1},{1,0},{2,3},{3,2},{4,5},{5,4},{6,7},{7,6},{8,9},{9,8},{10,11... | collective-permute-start | bytes 1572872 | tf_op jit(solution)/shard_map/ppermute | solution.py:339
  99.5 4.8 %collective-permute-start.23 = (bf16[256,1024]{1,0:T(8,128)(2,1)}, bf16[256,1024]{1,0:T(8,128)(2,1)S(1)}, u32[]{:S(2)}, u32[]{:S(2)}) collective-permute-start(bf16[256,1024]{1,0:T(8,128)(2,1)} %copy-done.15), channel_id=1, source_target_pairs={{0,1},{1,0},{2,3},{3,2},{4,5},{5,4},{6,7},{7,6},{8,9},{9,8},{10,11... | collective-permute-start | bytes 1572872 | tf_op jit(solution)/shard_map/ppermute | solution.py:339
  100.6 3.7 %collective-permute-start.22 = (bf16[256,1024]{1,0:T(8,128)(2,1)S(1)}, bf16[256,1024]{1,0:T(8,128)(2,1)S(1)}, u32[]{:S(2)}, u32[]{:S(2)}) collective-permute-start(bf16[256,1024]{1,0:T(8,128)(2,1)S(1)} %copy-done.12), channel_id=1, source_target_pairs={{0,1},{1,0},{2,3},{3,2},{4,5},{5,4},{6,7},{7,6},{8,9},{9,8},{10,11... | collective-permute-start | bytes 1572872 | tf_op jit(solution)/shard_map/ppermute | solution.py:339
  101.3 3.5 %collective-permute-start.21 = (bf16[256,1024]{1,0:T(8,128)(2,1)S(1)}, bf16[256,1024]{1,0:T(8,128)(2,1)S(1)}, u32[]{:S(2)}, u32[]{:S(2)}) collective-permute-start(bf16[256,1024]{1,0:T(8,128)(2,1)S(1)} %constant_dynamic-update-slice_fusion.2.refs_1_), channel_id=1, source_target_pairs={{0,1},{1,0},{2,3},{3,2},{4,5},{5,4},{6,7},{7,6},{8,9},{9,8},{10,11... | collective-permute-start | bytes 1572872 | tf_op jit(solution)/shard_map/ppermute | solution.py:339
  102.8 2.8 %collective-permute-start.20 = (bf16[256,1024]{1,0:T(8,128)(2,1)S(1)}, bf16[256,1024]{1,0:T(8,128)(2,1)S(1)}, u32[]{:S(2)}, u32[]{:S(2)}) collective-permute-start(bf16[256,1024]{1,0:T(8,128)(2,1)S(1)} %copy-done.9), channel_id=1, source_target_pairs={{0,1},{1,0},{2,3},{3,2},{4,5},{5,4},{6,7},{7,6},{8,9},{9,8},{10,11... | collective-permute-start | bytes 1572872 | tf_op jit(solution)/shard_map/ppermute | solution.py:339
  126.0 13.0 %all-to-all-start.2 = ((bf16[32,32,128]{2,1,0:T(8,128)(2,1)}), bf16[32,32,128]{2,1,0:T(8,128)(2,1)S(1)}, u32[]{:S(2)}, u32[]{:S(2)}) async-start(bf16[32,32,128]{2,1,0:T(8,128)(2,1)} %shard_map.167), calls=%async_computation.2 | async-start | bytes 524288 | tf_op jit(solution)/shard_map/all_to_all | solution.py:411
  (30 other events, 283.5 us)
